TPU v7x, 128 devices: a whole 4x4x4 slice. The times are simulated.
128 devices in a mesh: leaf: 16 (over x, y), sub: 8 (over z, core).
Axes of the slice: x: 4, y: 4, z: 4, core: 2. Of those that a mesh axis runs over, the one named last changes fastest.
Arguments:
- points: float32 [32, 524288], P(None, ('leaf', 'sub')), may hold values from -6 to 6
- right_side: float32 [16, 524288], P(None, ('leaf', 'sub')), may hold values from -6 to 6
- interp: float32 [1024, 512, 128], P(('leaf', 'sub')), may hold values from -0.5 to 0.5
- leaf_skel: int32 [1024, 128], P(('leaf', 'sub')), may hold values from 0 to 511, as said below
- up_one: float32 [512, 256, 128], P(('leaf', 'sub')), may hold values from -0.375 to 0.375
- skel_one: int32 [512, 128], P(('leaf', 'sub')), may hold values from 0 to 255, as said below
- up_two: float32 [256, 256, 128], P(('leaf', 'sub')), may hold values from -0.375 to 0.375
- skel_two: int32 [256, 128], P(('leaf', 'sub')), may hold values from 0 to 255, as said below
- up_three: float32 [128, 256, 128], P(('leaf', 'sub')), may hold values from -0.375 to 0.375
- skel_three: int32 [128, 128], P(('leaf', 'sub')), may hold values from 0 to 255, as said below
- up_top: float32 [96, 256, 128], replicated, may hold values from -0.375 to 0.375
- skel_top: int32 [96, 128], replicated, may hold values from 0 to 255, as said below
- near_list: int32 [1024, 12], P(('leaf', 'sub')), may hold values from 0 to 1023, as said below
- far_three: int32 [128, 2], P(('leaf', 'sub')), may hold values from 0 to 127, as said below
- far_top: int32 [96, 4], replicated, may hold values from 0 to 95, as said below
Outputs:
- solution: float32 [16, 524288], P(None, ('leaf', 'sub'))
- residual: float32 [16, 524288], P(None, ('leaf', 'sub'))
Inputs may be any that keep to these rules, and one draw needn't show every extreme that they name: `leaf_skel`: each row holds 128 different positions among the leaf's 512 points. `skel_one`: each row holds 128 different positions among the two children's 2 * 128 skeleton points. `skel_two`: each row holds 128 different positions among the two children's 2 * 128 skeleton points. `skel_three`: each row holds 128 different positions among the two children's 2 * 128 skeleton points. `skel_top`: each row holds 128 different positions among the two children's 2 * 128 skeleton points. `near_list`: row a lists different leaves b with b != a and |b - a| <= 8 in its first slots and a in the remaining ones; in every draw some leaf fills all 12 slots. `far_three`: row n lists n - 1 or n + 1 or both in its first slots and n in the remaining ones; in every draw some node fills both slots. `far_top`: row t lists different nodes of t's own level other than t in its first slots and t in the remaining ones; on each level some node fills all 4 slots in every draw.
All inputs are finite; a program needn't handle non-finite values.
Results may differ from a plain program's by a relative error of at most 0.0003.
Values sent between devices are 32-bit elements; how exact they have to be, the bound alone decides.
No kernel may reach another device: no remote copies, remote signals or barrier semaphores. Data moves between devices by JAX's collectives and lax.ppermute only.
A program may use at most 128 MiB of HBM per device.

v0:
```python
import jax
import jax.numpy as jnp
from jax import lax
from jax.sharding import PartitionSpec as P

LEAF = 512
DIMS = 32
RIGHT_HAND_COUNT = 16
RANK = 128
LEAF_DEV = 8
ITERS = 2


RIDGE_TERM = 12.0
KERNEL_SPREAD = 24.0
exact_answer = lax.Precision.HIGHEST


def padded(block, sides, width):
    for axis, dim in sides:
        count = lax.axis_size(axis)
        forward = [(i, i + 1) for i in range(count - 1)]
        backward = [(target, source) for source, target in forward]
        low = lax.ppermute(
            lax.slice_in_dim(block, block.shape[dim] - width, None, axis=dim), axis, forward
        )
        high = lax.ppermute(lax.slice_in_dim(block, 0, width, axis=dim), axis, backward)
        block = jnp.concatenate([low, block, high], axis=dim)
    return block


def from_partner(value, axis, stride):
    mask = 2**stride
    pairs = [(source, source ^ mask) for source in range(lax.axis_size(axis))]
    return lax.ppermute(value, axis, pairs)


def kernel_blocks(left_pts, right_pts, left_sq, right_sq):
    cross_dot = jnp.einsum("dlm,dln->lmn", left_pts, right_pts, precision=exact_answer)
    return jnp.exp(-(left_sq[:, :, None] + right_sq[:, None, :] - 2.0 * cross_dot) / KERNEL_SPREAD)


def lift(child_rows, weights):
    node_count = weights.shape[0]
    stacked = child_rows.reshape(node_count, 2 * RANK, RIGHT_HAND_COUNT)
    return jnp.einsum("nks,nkr->nsr", weights, stacked, precision=exact_answer)


def select(child_rows, chosen):
    node_count = chosen.shape[0]
    paired = (
        child_rows.reshape(node_count, 2, DIMS, RANK)
        .transpose(0, 2, 1, 3)
        .reshape(node_count, DIMS, 2 * RANK)
    )
    return jnp.take_along_axis(paired, chosen[:, None, :], axis=2)


def lower(weights, parent):
    node_count = weights.shape[0]
    spread = jnp.einsum("nks,nsr->nkr", weights, parent, precision=exact_answer)
    return spread.reshape(2 * node_count, RANK, RIGHT_HAND_COUNT)


def interact(own_skel, pool_skel, pool_charges, partners, self_ids):
    own_sq = jnp.sum(own_skel * own_skel, 1)
    running = jnp.zeros((own_skel.shape[0], RANK, RIGHT_HAND_COUNT), jnp.float32)
    for slot_index in range(partners.shape[1]):
        other_ids = partners[:, slot_index]
        weight = (other_ids != self_ids).astype(jnp.float32)
        other_skel = jnp.take(pool_skel, other_ids, axis=0)
        other_sq = jnp.sum(other_skel * other_skel, 1)
        cross_dot = jnp.einsum("kdi,kdj->kij", own_skel, other_skel, precision=exact_answer)
        block = (
            jnp.exp(-(own_sq[:, :, None] + other_sq[:, None, :] - 2.0 * cross_dot) / KERNEL_SPREAD)
            * weight[:, None, None]
        )
        running = running + jnp.einsum(
            "kij,kjr->kir", block, jnp.take(pool_charges, other_ids, axis=0), precision=exact_answer
        )
    return running


def local(
    points,
    right_side,
    interp,
    leaf_skel,
    up_one,
    skel_one,
    up_two,
    skel_two,
    up_three,
    skel_three,
    up_top,
    skel_top,
    near_list,
    far_three,
    far_top,
):
    device = lax.axis_index(("leaf", "sub"))
    block_width = LEAF_DEV * LEAF
    top_four = up_top.shape[0] * 2 // 3
    ext_points = padded(points, ((("leaf", "sub"), 1),), block_width).reshape(
        DIMS, 3 * LEAF_DEV, LEAF
    )
    ext_sq = jnp.sum(ext_points * ext_points, 0)
    own_points = ext_points[:, LEAF_DEV : 2 * LEAF_DEV]
    own_sq = ext_sq[LEAF_DEV : 2 * LEAF_DEV]
    first_leaf = device * LEAF_DEV
    leaf_ids = first_leaf + jnp.arange(LEAF_DEV, dtype=jnp.int32)
    filled = near_list != leaf_ids[:, None]
    places = near_list - first_leaf + LEAF_DEV
    turn_count = jnp.max(jnp.sum(filled.astype(jnp.int32), 1))
    self_blocks = kernel_blocks(own_points, own_points, own_sq, own_sq)
    leaves_first = points.reshape(DIMS, LEAF_DEV, LEAF).transpose(1, 0, 2)
    skel_base = jnp.take_along_axis(leaves_first, leaf_skel[:, None, :], axis=2)
    skel_mid = select(select(select(skel_base, skel_one), skel_two), skel_three)
    parity = device & 1
    quarter = device & 3
    node_four = device >> 1
    node_five = device >> 2
    own_ids = jnp.stack([node_four, top_four + node_five])
    rim_skel = padded(skel_mid, ((("leaf", "sub"), 0),), 1)
    current = skel_mid
    climbed = []
    for bit_index in range(2):
        partner = from_partner(current, ("leaf", "sub"), bit_index)
        upper_side = device >> bit_index & 1 == 1
        lower_half = jnp.where(upper_side, partner, current)
        upper_half = jnp.where(upper_side, current, partner)
        node_id = (device >> bit_index + 1) + bit_index * top_four
        current = select(
            jnp.concatenate([lower_half, upper_half], 0),
            lax.dynamic_slice_in_dim(skel_top, node_id, 1, 0),
        )
        climbed.append(current)
    piece_four = lax.dynamic_slice_in_dim(climbed[0], parity * (RANK // 2), RANK // 2, 2)
    piece_five = lax.dynamic_slice_in_dim(climbed[1], quarter * (RANK // 4), RANK // 4, 2)
    got_four, got_five = (
        lax.all_gather(piece_four, ("leaf", "sub"), axis=0, tiled=True),
        lax.all_gather(piece_five, ("leaf", "sub"), axis=0, tiled=True),
    )
    skel_four = (
        got_four.reshape(top_four, 2, DIMS, RANK // 2)
        .transpose(0, 2, 1, 3)
        .reshape(top_four, DIMS, RANK)
    )
    skel_five = (
        got_five.reshape(top_four // 2, 4, DIMS, RANK // 4)
        .transpose(0, 2, 1, 3)
        .reshape(top_four // 2, DIMS, RANK)
    )
    skel_upper = jnp.concatenate([skel_four, skel_five], 0)
    own_upper = jnp.take(skel_upper, own_ids, axis=0)
    own_lists = jnp.take(far_top, own_ids, axis=0)
    weight_five = lax.dynamic_slice_in_dim(up_top, top_four + node_five, 1, 0)
    weight_four = lax.dynamic_slice_in_dim(up_top, node_four, 1, 0)

    def residual_norm(field_now):
        return lax.psum(jnp.sum(field_now * field_now, 1), ("leaf", "sub"))

    solution = jnp.zeros_like(right_side)
    residual = right_side
    direction = right_side
    norm_now = residual_norm(residual)
    for turn_index in range(ITERS):
        ext_values = padded(direction, ((("leaf", "sub"), 1),), block_width).reshape(
            RIGHT_HAND_COUNT, 3 * LEAF_DEV, LEAF
        )
        initial = jnp.einsum(
            "rlj,lji->rli",
            ext_values[:, LEAF_DEV : 2 * LEAF_DEV],
            self_blocks,
            precision=exact_answer,
        )

        def add_slot(slot_index, running):
            where_now = jnp.take(places, slot_index, axis=1)
            mark_slot = jnp.take(filled, slot_index, axis=1).astype(jnp.float32)
            blocks = kernel_blocks(
                jnp.take(ext_points, where_now, axis=1),
                own_points,
                jnp.take(ext_sq, where_now, axis=0),
                own_sq,
            )
            blocks = blocks * mark_slot[:, None, None]
            return running + jnp.einsum(
                "rlj,lji->rli",
                jnp.take(ext_values, where_now, axis=1),
                blocks,
                precision=exact_answer,
            )

        target_values = direction.reshape(RIGHT_HAND_COUNT, LEAF_DEV, LEAF)
        source_charges = jnp.einsum("gxm,fgx->gmf", interp, target_values, precision=exact_answer)
        mid_charges = lift(lift(lift(source_charges, up_one), up_two), up_three)
        rim_charges = padded(mid_charges, ((("leaf", "sub"), 0),), 1)
        middle_field = interact(
            skel_mid, rim_skel, rim_charges, far_three - device + 1, jnp.ones((1,), jnp.int32)
        )
        far_current = mid_charges
        far_climbed = []
        for far_bit_index in range(2):
            far_partner = from_partner(far_current, ("leaf", "sub"), far_bit_index)
            far_upper_side = device >> far_bit_index & 1 == 1
            far_lower_half = jnp.where(far_upper_side, far_partner, far_current)
            far_upper_half = jnp.where(far_upper_side, far_current, far_partner)
            far_node_id = (device >> far_bit_index + 1) + far_bit_index * top_four
            far_current = lift(
                jnp.concatenate([far_lower_half, far_upper_half], 0),
                lax.dynamic_slice_in_dim(up_top, far_node_id, 1, 0),
            )
            far_climbed.append(far_current)
        far_piece_four = lax.dynamic_slice_in_dim(
            far_climbed[0], parity * (RANK // 2), RANK // 2, 1
        )
        far_piece_five = lax.dynamic_slice_in_dim(
            far_climbed[1], quarter * (RANK // 4), RANK // 4, 1
        )
        far_got_four = lax.all_gather(far_piece_four, ("leaf", "sub"), axis=0, tiled=True)
        far_got_five = lax.all_gather(far_piece_five, ("leaf", "sub"), axis=0, tiled=True)
        charge_four = far_got_four.reshape(top_four, RANK, RIGHT_HAND_COUNT)
        charge_five = far_got_five.reshape(top_four // 2, RANK, RIGHT_HAND_COUNT)
        field_top = interact(
            own_upper,
            skel_upper,
            jnp.concatenate([charge_four, charge_five], 0),
            own_lists,
            own_ids,
        )
        down_four = field_top[0:1] + lax.dynamic_slice_in_dim(
            lower(weight_five, field_top[1:2]), node_four & 1, 1, 0
        )
        down_mid = middle_field + lax.dynamic_slice_in_dim(
            lower(weight_four, down_four), parity, 1, 0
        )
        downward_leaf = lower(up_one, lower(up_two, lower(up_three, down_mid)))
        mapped = (
            RIDGE_TERM * direction
            + lax.fori_loop(0, turn_count, add_slot, initial).reshape(RIGHT_HAND_COUNT, block_width)
            + jnp.einsum("uwz,uza->auw", interp, downward_leaf, precision=exact_answer).reshape(
                RIGHT_HAND_COUNT, block_width
            )
        )
        curvature_sum = lax.psum(jnp.sum(direction * mapped, 1), ("leaf", "sub"))
        step_size = norm_now / curvature_sum
        solution = solution + step_size[:, None] * direction
        residual = residual - step_size[:, None] * mapped
        norm_next = residual_norm(residual)
        direction = residual + (norm_next / norm_now)[:, None] * direction
        norm_now = norm_next
    return (solution, residual)


def solution(mesh):
    placed = (
        P(None, ("leaf", "sub")),
        P(None, ("leaf", "sub")),
        P(("leaf", "sub"), None, None),
        P(("leaf", "sub"), None),
        P(("leaf", "sub"), None, None),
        P(("leaf", "sub"), None),
        P(("leaf", "sub"), None, None),
        P(("leaf", "sub"), None),
        P(("leaf", "sub"), None, None),
        P(("leaf", "sub"), None),
        P(),
        P(),
        P(("leaf", "sub"), None),
        P(("leaf", "sub"), None),
        P(),
    )
    return jax.shard_map(
        local,
        mesh=mesh,
        in_specs=placed,
        out_specs=(P(None, ("leaf", "sub")), P(None, ("leaf", "sub"))),
        check_vma=False,
    )
```

profile of v0, /device:TPU:1, one launch (start us, length us, event | category | flops | bytes accessed | tf_op | source)
XLA Modules:
  0.0 1297.0 jit_solution(14617920609084655147)
XLA Ops:
  14.6 3.0 copy.87
  18.2 15.3 %gather_fusion.7 = f32[1024,32]{1,0:T(8,128)} fusion(f32[8,32,512]{1,2,0:T(8,128)} %bitcast.458, s32[1024]{0:T(1024)S(1)} %fusion.237), kind=kCustom, calls=%fused_computation.23 | custom fusion | bytes 270336 | tf_op jit(solution)/shard_map/jit(take_along_axis)/gather | solution.py:117
  35.5 8.0 gather_fusion.8
  44.6 2.6 gather_fusion.9
  52.1 3.5 collective-permute-start.4
  60.8 3.9 collective-permute-start.6
  86.9 43.3 %all-gather.4 = f32[128,64,16]{1,2,0:T(8,128)S(1)} all-gather(f32[1,64,16]{1,2,0:T(8,128)S(1)} %dynamic-slice_bitcast_fusion.3), channel_id=2, replica_groups=mesh['leaf'=16,'sub'=8] {'leaf','sub'}, dimensions={0}, use_global_device_ids=true | all-gather | bytes 528384 | tf_op jit(solution)/shard_map/all_gather | solution.py:221
  133.7 3.2 collective-permute-start
  144.0 5.5 collective-permute-start.2
  149.8 36.8 %all-gather.5 = f32[128,32,16]{1,2,0:T(8,128)S(1)} all-gather(f32[1,32,16]{1,2,0:T(8,128)S(1)} %dynamic-slice_bitcast_fusion.2), channel_id=3, replica_groups=mesh['leaf'=16,'sub'=8] {'leaf','sub'}, dimensions={0}, use_global_device_ids=true | all-gather | bytes 264192 | tf_op jit(solution)/shard_map/all_gather | solution.py:222
  201.4 2.4 gather_fusion.17
  203.8 2.4 gather_fusion.19
  206.2 2.4 gather_fusion.21
  212.0 37.7 %all_gather.19 = f32[128,32,32]{2,1,0:T(8,128)S(1)} all-gather(f32[1,32,32]{2,1,0:T(8,128)S(1)} %copy.105), channel_id=1, replica_groups=mesh['leaf'=16,'sub'=8] {'leaf','sub'}, dimensions={0}, use_global_device_ids=true | all-gather | bytes 528384 | tf_op jit(solution)/shard_map/all_gather | solution.py:142
  249.7 3.1 copy.212
  252.8 13.8 %reshape.695 = f32[32,32,128]{2,1,0:T(8,128)} reshape(f32[32,32,4,32]{3,2,1,0:T(4,128)} %bitcast.450) | data formatting | bytes 1048576 | tf_op jit(solution)/shard_map/reshape | solution.py:152
  271.1 9.1 fusion.276
  280.9 10.1 fusion.76
  291.0 75.7 %while.24 = (s32[]{:T(128)}, f32[16,8,512]{2,0,1:T(8,128)}, s32[]{:T(128)}, s32[8,12]{0,1:T(8,128)}, f32[24,512]{1,0:T(8,128)S(1)}, /*index=5*/f32[8,512]{1,0:T(...) while((s32[]{:T(128)}, f32[16,8,512]{2,0,1:T(8,128)}, ...), condition=%wide.region_6.12_spmd, body=%wide.region_5.11_spmd.sunk | while | flops 1220809728 | bytes 20287980 | solution.py:241
  294.4 9.1 fusion.332
  306.5 9.5 fusion.333
  319.4 9.1 fusion.332
  331.5 9.5 fusion.333
  344.3 9.0 fusion.332
  356.4 9.5 fusion.333
  368.5 4.9 copy.213
  373.4 3.3 reshape.691
  381.0 2.7 gather_fusion.20
  383.7 2.7 gather_fusion.18
  386.3 2.7 gather_fusion.16
  391.1 2.7 gather_fusion.13
  416.9 2.7 convolution_bitcast_fusion.1
  421.5 287.5 %all-reduce = (f32[16]{0:T(128)S(1)}, f32[16]{0:T(128)S(1)}) all-reduce(f32[16]{0:T(128)S(1)} %get-tuple-element.225, f32[16]{0:T(128)S(1)} %get-tuple-element.224), channel_id=1, replica_groups=mesh['leaf'=16,'sub'=8] {'leaf','sub'}, use_global_device_ids=true, to_apply=%region_1.0 | all-reduce | flops 32 | bytes 256 | tf_op jit(solution)/shard_map/psum | solution.py:161
  711.4 63.2 %psum.30 = f32[16]{0:T(128)S(1)} all-reduce(f32[16]{0:T(128)S(1)} %get-tuple-element.278), channel_id=1, replica_groups=mesh['leaf'=16,'sub'=8] {'leaf','sub'}, use_global_device_ids=true, to_apply=%region_18.29 | all-reduce | flops 16 | bytes 128 | tf_op jit(solution)/shard_map/psum | solution.py:161
  785.3 2.6 collective-permute-start.12
  787.9 2.4 collective-permute-start.13
  790.3 3.2 collective-permute-start.14
  797.1 44.0 %all-gather.6 = f32[128,64,16]{1,2,0:T(8,128)S(1)} all-gather(f32[1,64,16]{1,2,0:T(8,128)S(1)} %dynamic-slice_bitcast_fusion.1), channel_id=4, replica_groups=mesh['leaf'=16,'sub'=8] {'leaf','sub'}, dimensions={0}, use_global_device_ids=true | all-gather | bytes 528384 | tf_op jit(solution)/shard_map/all_gather | solution.py:221
  849.7 34.2 %all-gather.7 = f32[128,32,16]{1,2,0:T(8,128)S(1)} all-gather(f32[1,32,16]{1,2,0:T(8,128)S(1)} %dynamic-slice_bitcast_fusion), channel_id=5, replica_groups=mesh['leaf'=16,'sub'=8] {'leaf','sub'}, dimensions={0}, use_global_device_ids=true | all-gather | bytes 264192 | tf_op jit(solution)/shard_map/all_gather | solution.py:222
  911.9 10.1 fusion.77
  922.0 75.9 %while.25 = (s32[]{:T(128)}, f32[16,8,512]{2,0,1:T(8,128)}, s32[]{:T(128)}, s32[8,12]{0,1:T(8,128)}, f32[24,512]{1,0:T(8,128)S(1)}, /*index=5*/f32[8,512]{1,0:T(...) while((s32[]{:T(128)}, f32[16,8,512]{2,0,1:T(8,128)}, ...), condition=%wide.region_20.31_spmd, body=%wide.region_19.30_spmd.sunk | while | flops 1220809728 | bytes 20287980 | solution.py:241
  925.6 9.1 fusion.338
  937.8 9.5 fusion.339
  950.6 9.1 fusion.338
  962.8 9.5 fusion.339
  975.7 9.1 fusion.338
  987.8 9.5 fusion.339
  1000.1 287.7 %psum.31 = f32[16]{0:T(128)S(1)} all-reduce(f32[16]{0:T(128)S(1)} %multiply_reduce_fusion.1), channel_id=1, replica_groups=mesh['leaf'=16,'sub'=8] {'leaf','sub'}, use_global_device_ids=true, to_apply=%region_22.33 | all-reduce | flops 16 | bytes 128 | tf_op jit(solution)/shard_map/psum | solution.py:246
  (323 shorter events, 196.8 us)
Async XLA Ops:
  7.2 50.3 %copy-start = (f32[8,512,128]{2,1,0:T(8,128)S(1)}, f32[8,512,128]{2,1,0:T(8,128)}, u32[]{:S(2)}) copy-start(f32[8,512,128]{2,1,0:T(8,128)} %param.41) | copy-start | bytes 6291460
  7.2 52.6 %copy-start.3 = (f32[4,256,128]{2,1,0:T(8,128)S(1)}, f32[4,256,128]{2,1,0:T(8,128)}, u32[]{:S(2)}) copy-start(f32[4,256,128]{2,1,0:T(8,128)} %param.43) | copy-start | bytes 1572868
  7.2 53.0 %copy-start.7 = (f32[2,256,128]{2,1,0:T(8,128)S(1)}, f32[2,256,128]{2,1,0:T(8,128)}, u32[]{:S(2)}) copy-start(f32[2,256,128]{2,1,0:T(8,128)} %param.45) | copy-start | bytes 786436
  7.2 53.3 %copy-start.12 = (f32[1,256,128]{2,1,0:T(8,128)S(1)}, f32[1,256,128]{2,1,0:T(8,128)}, u32[]{:S(2)}) copy-start(f32[1,256,128]{2,1,0:T(8,128)} %param.47) | copy-start | bytes 393220
  7.2 361.3 %all-gather.10.cloned.1.call-start = ((), (), s32[]{:S(2)}) async-start(), calls=%async_computation | async-start | bytes 2113536 | tf_op jit(solution)/shard_map/all_gather | solution.py:141
  18.2 125.8 %copy-start.2 = (f32[16,4096]{1,0:T(8,128)S(1)}, f32[16,4096]{1,0:T(8,128)}, u32[]{:S(2)}) copy-start(f32[16,4096]{1,0:T(8,128)} %param.40) | copy-start | bytes 786436
  50.6 89.5 %collective-permute-start.8 = (f32[1,32,128]{1,2,0:T(8,128)}, f32[1,32,128]{1,2,0:T(8,128)}, u32[]{:S(2)}, u32[]{:S(2)}) collective-permute-start(f32[1,32,128]{1,2,0:T(8,128)} %get-tuple-element.285), channel_id=1, source_target_pairs={{0,1},{1,0},{2,3},{3,2},{4,5},{5,4},{6,7},{7,6},{8,9},{9,8},{10,11... | collective-permute-start | bytes 49160 | tf_op jit(solution)/shard_map/ppermute | solution.py:35
  52.1 137.8 %collective-permute-start.4 = (f32[1,32,128]{1,2,0:T(8,128)}, f32[1,32,128]{1,2,0:T(8,128)}, u32[]{:S(2)}, u32[]{:S(2)}) collective-permute-start(f32[1,32,128]{1,2,0:T(8,128)} %get-tuple-element.285), channel_id=1, source_target_pairs={{0,1},{1,2},{2,3},{3,4},{4,5},{5,6},{6,7},{7,8},{8,9},{9,10},{10,1... | collective-permute-start | bytes 49160 | tf_op jit(solution)/shard_map/ppermute | solution.py:24
  55.6 137.2 %collective-permute-start.5 = (f32[1,32,128]{1,2,0:T(8,128)}, f32[1,32,128]{1,2,0:T(8,128)}, u32[]{:S(2)}, u32[]{:S(2)}) collective-permute-start(f32[1,32,128]{1,2,0:T(8,128)} %get-tuple-element.285), channel_id=1, source_target_pairs={{1,0},{2,1},{3,2},{4,3},{5,4},{6,5},{7,6},{8,7},{9,8},{10,9},{11,1... | collective-permute-start | bytes 49160 | tf_op jit(solution)/shard_map/ppermute | solution.py:27
  60.7 24.0 %collective-permute-start.10 = (f32[1,128,16]{1,2,0:T(8,128)S(1)}, f32[1,128,16]{1,2,0:T(8,128)S(1)}, u32[]{:S(2)}, u32[]{:S(2)}) collective-permute-start(f32[1,128,16]{1,2,0:T(8,128)S(1)} %convolution_bitcast_fusion.14), channel_id=1, source_target_pairs={{0,1},{1,0},{2,3},{3,2},{4,5},{5,4},{6,7},{7,6},{8,9},{9,8},{10,11... | collective-permute-start | bytes 24584 | tf_op jit(solution)/shard_map/ppermute | solution.py:35
  60.8 72.9 %collective-permute-start.6 = (f32[1,128,16]{1,2,0:T(8,128)S(1)}, f32[1,128,16]{1,2,0:T(8,128)}, u32[]{:S(2)}, u32[]{:S(2)}) collective-permute-start(f32[1,128,16]{1,2,0:T(8,128)S(1)} %convolution_bitcast_fusion.14), channel_id=1, source_target_pairs={{0,1},{1,2},{2,3},{3,4},{4,5},{5,6},{6,7},{7,8},{8,9},{9,10},{10,1... | collective-permute-start | bytes 24584 | tf_op jit(solution)/shard_map/ppermute | solution.py:24
  64.8 6.6 copy-start.31
  72.9 14.0 %copy-start.8 = (f32[1,256,128]{2,1,0:T(8,128)}, f32[1,256,128]{2,1,0:T(8,128)S(1)}, u32[]{:S(2)}) copy-start(f32[1,256,128]{2,1,0:T(8,128)S(1)} %get-tuple-element.287) | copy-start | bytes 393220
  72.9 176.8 %copy-start.9 = (f32[1,256,128]{2,1,0:T(8,128)}, f32[1,256,128]{2,1,0:T(8,128)S(1)}, u32[]{:S(2)}) copy-start(f32[1,256,128]{2,1,0:T(8,128)S(1)} %get-tuple-element.286) | copy-start | bytes 393220
  84.7 52.2 %collective-permute-start.7 = (f32[1,128,16]{1,2,0:T(8,128)S(1)}, f32[1,128,16]{1,2,0:T(8,128)}, u32[]{:S(2)}, u32[]{:S(2)}) collective-permute-start(f32[1,128,16]{1,2,0:T(8,128)S(1)} %convolution_bitcast_fusion.14), channel_id=1, source_target_pairs={{1,0},{2,1},{3,2},{4,3},{5,4},{6,5},{7,6},{8,7},{9,8},{10,9},{11,1... | collective-permute-start | bytes 24584 | tf_op jit(solution)/shard_map/ppermute | solution.py:27
  133.7 134.9 %collective-permute-start = (f32[32,4096]{1,0:T(8,128)}, f32[32,4096]{1,0:T(8,128)}, u32[]{:S(2)}, u32[]{:S(2)}) collective-permute-start(f32[32,4096]{1,0:T(8,128)} %param.39), channel_id=1, source_target_pairs={{0,1},{1,2},{2,3},{3,4},{4,5},{5,6},{6,7},{7,8},{8,9},{9,10},{10,1... | collective-permute-start | bytes 1572872 | tf_op jit(solution)/shard_map/ppermute | solution.py:24
  136.9 132.8 %collective-permute-start.1 = (f32[32,4096]{1,0:T(8,128)}, f32[32,4096]{1,0:T(8,128)}, u32[]{:S(2)}, u32[]{:S(2)}) collective-permute-start(f32[32,4096]{1,0:T(8,128)} %param.39), channel_id=1, source_target_pairs={{1,0},{2,1},{3,2},{4,3},{5,4},{6,5},{7,6},{8,7},{9,8},{10,9},{11,1... | collective-permute-start | bytes 1572872 | tf_op jit(solution)/shard_map/ppermute | solution.py:27
  140.2 3.8 collective-permute-start.11
  142.5 7.3 copy-start.22
  143.3 6.6 copy-start.23
  144.0 122.6 %collective-permute-start.2 = (f32[16,4096]{1,0:T(8,128)S(1)}, f32[16,4096]{1,0:T(8,128)}, u32[]{:S(2)}, u32[]{:S(2)}) collective-permute-start(f32[16,4096]{1,0:T(8,128)S(1)} %copy-done.2), channel_id=1, source_target_pairs={{0,1},{1,2},{2,3},{3,4},{4,5},{5,6},{6,7},{7,8},{8,9},{9,10},{10,1... | collective-permute-start | bytes 786440 | tf_op jit(solution)/shard_map/ppermute | solution.py:24
  188.0 81.7 %copy-start.11 = (f32[32,4096]{1,0:T(8,128)S(1)}, f32[32,4096]{1,0:T(8,128)}, u32[]{:S(2)}) copy-start(f32[32,4096]{1,0:T(8,128)} %param.39) | copy-start | bytes 1572868
  189.8 76.8 %collective-permute-start.3 = (f32[16,4096]{1,0:T(8,128)S(1)}, f32[16,4096]{1,0:T(8,128)S(1)}, u32[]{:S(2)}, u32[]{:S(2)}) collective-permute-start(f32[16,4096]{1,0:T(8,128)S(1)} %copy-done.2), channel_id=1, source_target_pairs={{1,0},{2,1},{3,2},{4,3},{5,4},{6,5},{7,6},{8,7},{9,8},{10,9},{11,1... | collective-permute-start | bytes 786440 | tf_op jit(solution)/shard_map/ppermute | solution.py:27
  192.8 15.8 %collective-permute-start.9 = (f32[1,32,128]{1,2,0:T(8,128)}, f32[1,32,128]{1,2,0:T(8,128)S(1)}, u32[]{:S(2)}, u32[]{:S(2)}) collective-permute-start(f32[1,32,128]{1,2,0:T(8,128)} %copy-done.23), channel_id=1, source_target_pairs={{0,2},{1,3},{2,0},{3,1},{4,6},{5,7},{6,4},{7,5},{8,10},{9,11},{10,... | collective-permute-start | bytes 49160 | tf_op jit(solution)/shard_map/ppermute | solution.py:35
  197.9 72.8 %copy-start.16 = (f32[128,128]{1,0:T(8,128)}, f32[128,128]{1,0:T(8,128)S(1)}, u32[]{:S(2)}) copy-start(f32[128,128]{1,0:T(8,128)S(1)} %fusion.107) | copy-start | bytes 196612
  271.1 9.1 copy-start.1
  366.8 37.2 %copy-start.15 = (f32[2,128,16]{1,2,0:T(8,128)S(1)}, f32[2,128,16]{1,2,0:T(8,128)}, u32[]{:S(2)}) copy-start(f32[2,128,16]{1,2,0:T(8,128)} %gather_fusion.17) | copy-start | bytes 49156
  366.8 38.2 %copy-start.14 = (f32[2,128,16]{1,2,0:T(8,128)S(1)}, f32[2,128,16]{1,2,0:T(8,128)}, u32[]{:S(2)}) copy-start(f32[2,128,16]{1,2,0:T(8,128)} %gather_fusion.19) | copy-start | bytes 49156
  366.8 39.2 %copy-start.13 = (f32[2,128,16]{1,2,0:T(8,128)S(1)}, f32[2,128,16]{1,2,0:T(8,128)}, u32[]{:S(2)}) copy-start(f32[2,128,16]{1,2,0:T(8,128)} %gather_fusion.21) | copy-start | bytes 49156
  366.8 47.5 %copy-start.4 = (f32[4,256,128]{2,1,0:T(8,128)S(1)}, f32[4,256,128]{2,1,0:T(8,128)}, u32[]{:S(2)}) copy-start(f32[4,256,128]{2,1,0:T(8,128)} %param.43) | copy-start | bytes 1572868
  397.6 13.9 %copy-start.19 = (f32[2,128,128]{2,1,0:T(8,128)}, f32[2,128,128]{2,1,0:T(8,128)S(1)}, u32[]{:S(2)}) copy-start(f32[2,128,128]{2,1,0:T(8,128)S(1)} %fusion.82) | copy-start | bytes 393220
  398.9 13.9 %copy-start.20 = (f32[2,128,128]{2,1,0:T(8,128)}, f32[2,128,128]{2,1,0:T(8,128)S(1)}, u32[]{:S(2)}) copy-start(f32[2,128,128]{2,1,0:T(8,128)S(1)} %fusion.87) | copy-start | bytes 393220
  401.1 11.7 copy-start.21
  403.0 7.3 copy-start.18
  411.5 436.1 %copy-start.17 = (f32[128,128]{1,0:T(8,128)S(1)}, f32[128,128]{1,0:T(8,128)}, u32[]{:S(2)}) copy-start(f32[128,128]{1,0:T(8,128)} %copy-done.16) | copy-start | bytes 196612
  783.5 113.2 %copy-start.28 = (pred[2]{0:T(512)(128)(4,1)S(1)}, pred[2]{0:T(512)(128)(4,1)}, u32[]{:S(2)}) copy-start(pred[2]{0:T(512)(128)(4,1)} %get-tuple-element.310) | copy-start | bytes 10
  783.5 114.4 %copy-start.27 = (pred[2]{0:T(512)(128)(4,1)S(1)}, pred[2]{0:T(512)(128)(4,1)}, u32[]{:S(2)}) copy-start(pred[2]{0:T(512)(128)(4,1)} %get-tuple-element.314) | copy-start | bytes 10
  783.5 115.7 %copy-start.26 = (pred[2]{0:T(512)(128)(4,1)S(1)}, pred[2]{0:T(512)(128)(4,1)}, u32[]{:S(2)}) copy-start(pred[2]{0:T(512)(128)(4,1)} %get-tuple-element.312) | copy-start | bytes 10
  783.5 116.9 %copy-start.25 = (pred[2]{0:T(512)(128)(4,1)S(1)}, pred[2]{0:T(512)(128)(4,1)}, u32[]{:S(2)}) copy-start(pred[2]{0:T(512)(128)(4,1)} %get-tuple-element.307) | copy-start | bytes 10
  784.6 10.8 collective-permute-start.16
  785.3 125.4 %collective-permute-start.12 = (f32[16,4096]{1,0:T(8,128)}, f32[16,4096]{1,0:T(8,128)}, u32[]{:S(2)}, u32[]{:S(2)}) collective-permute-start(f32[16,4096]{1,0:T(8,128)} %copy-done.5), channel_id=1, source_target_pairs={{0,1},{1,2},{2,3},{3,4},{4,5},{5,6},{6,7},{7,8},{8,9},{9,10},{10,1... | collective-permute-start | bytes 786440 | tf_op jit(solution)/shard_map/ppermute | solution.py:24
  787.9 122.8 %collective-permute-start.13 = (f32[16,4096]{1,0:T(8,128)}, f32[16,4096]{1,0:T(8,128)}, u32[]{:S(2)}, u32[]{:S(2)}) collective-permute-start(f32[16,4096]{1,0:T(8,128)} %copy-done.5), channel_id=1, source_target_pairs={{1,0},{2,1},{3,2},{4,3},{5,4},{6,5},{7,6},{8,7},{9,8},{10,9},{11,1... | collective-permute-start | bytes 786440 | tf_op jit(solution)/shard_map/ppermute | solution.py:27
  790.3 56.6 %collective-permute-start.14 = (f32[1,128,16]{1,2,0:T(8,128)S(1)}, f32[1,128,16]{1,2,0:T(8,128)}, u32[]{:S(2)}, u32[]{:S(2)}) collective-permute-start(f32[1,128,16]{1,2,0:T(8,128)S(1)} %convolution_bitcast_fusion.13), channel_id=1, source_target_pairs={{0,1},{1,2},{2,3},{3,4},{4,5},{5,6},{6,7},{7,8},{8,9},{9,10},{10,1... | collective-permute-start | bytes 24584 | tf_op jit(solution)/shard_map/ppermute | solution.py:24
  793.5 53.4 %collective-permute-start.15 = (f32[1,128,16]{1,2,0:T(8,128)S(1)}, f32[1,128,16]{1,2,0:T(8,128)}, u32[]{:S(2)}, u32[]{:S(2)}) collective-permute-start(f32[1,128,16]{1,2,0:T(8,128)S(1)} %convolution_bitcast_fusion.13), channel_id=1, source_target_pairs={{1,0},{2,1},{3,2},{4,3},{5,4},{6,5},{7,6},{8,7},{9,8},{10,9},{11,1... | collective-permute-start | bytes 24584 | tf_op jit(solution)/shard_map/ppermute | solution.py:27
  796.6 51.2 %collective-permute-start.17 = (f32[1,128,16]{1,2,0:T(8,128)S(1)}, f32[1,128,16]{1,2,0:T(8,128)}, u32[]{:S(2)}, u32[]{:S(2)}) collective-permute-start(f32[1,128,16]{1,2,0:T(8,128)S(1)} %bitcast.487), channel_id=1, source_target_pairs={{0,2},{1,3},{2,0},{3,1},{4,6},{5,7},{6,4},{7,5},{8,10},{9,11},{10,... | collective-permute-start | bytes 24584 | tf_op jit(solution)/shard_map/ppermute | solution.py:35
  911.9 10.1 copy-start.6
  922.0 365.9 %copy-start.33 = (f32[16]{0:T(128)S(1)}, f32[16]{0:T(128)}, u32[]{:S(2)}) copy-start(f32[16]{0:T(128)} %copy-done.32) | copy-start | bytes 196
  922.0 365.9 %copy-start.30 = (f32[16]{0:T(128)S(1)}, f32[16]{0:T(128)}, u32[]{:S(2)}) copy-start(f32[16]{0:T(128)} %copy-done.29) | copy-start | bytes 196
  (5 other events, 10.2 us)
Sparse Core Ops, SparseCore 0:
  144.1 66.9 all-gather.9
where the time goes:
time: 1310 us; the launch traced here: 1300 us
  blocking collectives  834 us (64%)
  matrix products  186 us (14%)
  local copies, waits for them, and re-layouts  161 us (12%)
  other arithmetic  51.1 us (4%)
  starting transfers between devices  38 us (3%)
  between operations  20.3 us (2%)
    psum x2, blocking collectives, residual_norm(): return lax.psum(jnp.sum(field_now * field_now, 1), ('leaf', 'sub'))  351 us
    psum x1, blocking collectives, local(): curvature_sum = lax.psum(jnp.sum(direction * mapped, 1), ('leaf', 'sub'))  288 us
    all_gather x2, blocking collectives, local(): lax.all_gather(far_piece_four, ('leaf', 'sub'), axis=0, tiled=True)  87.3 us
    all_gather x2, blocking collectives, local(): lax.all_gather(far_piece_five, ('leaf', 'sub'), axis=0, tiled=True)  71 us
    dot_general x7, matrix products, kernel_blocks(): jnp.einsum('dlm,dln->lmn', left_pts, right_pts, precision=exact_answer)  63.6 us
    dot_general x6, matrix products, add_slot(): jnp.einsum('rlj,lji->rli', jnp.take(ext_values, where_now, axis=1), block...  56.8 us
    all_gather x1, blocking collectives, local(): lax.all_gather(piece_five, ('leaf', 'sub'), axis=0, tiled=True)  37.7 us
  transfers between devices with their start and end apart: 19, of which 0 were waited for; matrix products, arithmetic and copies ran while one was open for 16% of the time, Pallas kernels for 0%

commit v1 on v0

v1 whole, which is shorter than its diff:
```python
import functools
import math

import jax
import jax.numpy as jnp
from jax import lax
from jax.experimental import pallas as pl
from jax.experimental.pallas import tpu as pltpu
from jax.sharding import PartitionSpec as P

LEAF = 512
DIMS = 32
RHS = 16
RANK = 128
LEAVES_HERE = 8
SLOTS = 12
WIDTH = LEAVES_HERE * LEAF
DEVICES = 128
NODES_FOUR = 64
TOP_SLOTS = 4

RIDGE_TERM = 12.0
COORD_SCALE = math.sqrt(2.0 * math.log2(math.e) / 24.0)

AXES = ("leaf", "sub")
BF = jnp.bfloat16
F = jnp.float32
NN = (((1,), (0,)), ((), ()))
NT = (((1,), (1,)), ((), ()))
VMEM = pl.BlockSpec(memory_space=pltpu.VMEM)
SMEM = pl.BlockSpec(memory_space=pltpu.SMEM)
ANY = pl.BlockSpec(memory_space=pl.ANY)


def shape(dims, dtype=F):
    return jax.ShapeDtypeStruct(dims, dtype)


def mm(a, b, dims=NN):
    return lax.dot_general(a, b, dims, preferred_element_type=F)


def split_two(x):
    high = x.astype(BF)
    return high, (x - high.astype(F)).astype(BF)


def split_three(x):
    high = x.astype(BF)
    rest = x - high.astype(F)
    mid = rest.astype(BF)
    return high, mid, (rest - mid.astype(F)).astype(BF)


def dot_split(a, w, dims=NN):
    ah, am = split_two(a)
    wh, wm = split_two(w)
    both = mm(jnp.concatenate([ah, am], 0), wh, dims)
    return both[:RHS] + both[RHS:] + mm(ah, wm, dims)


def operands(y):
    n = y.shape[1]
    h, m, l = split_three(y)
    half = 0.5 * jnp.sum(y * y, 0, keepdims=True)
    parts = [p.astype(F) for p in split_three(half)]
    one = [jnp.ones((1, n), F)] * 3
    pad = [jnp.zeros((10, n), F)]
    tail_left = jnp.concatenate(parts + one + pad, 0).astype(BF)
    tail_right = jnp.concatenate([-p for p in one + parts] + pad, 0).astype(BF)
    zero = jnp.zeros((48, n), BF)
    left = jnp.concatenate([h, h, m, h, l, m, tail_left, zero], 0)
    right = jnp.concatenate([h, m, h, l, h, m, tail_right, zero], 0)
    return left, right


def pick(parts, chosen):
    n = parts.shape[1]
    rows = lax.broadcasted_iota(jnp.int32, (n, RANK), 0)
    hot = jnp.where(rows == chosen, 1.0, 0.0).astype(BF)
    return mm(parts, hot).astype(BF)


def joined(parts):
    return parts[0:32].astype(F) + parts[32:64].astype(F) + parts[64:96].astype(F)


def parts_of(y):
    return jnp.concatenate(split_three(y), 0)


def prep_kernel(x_ref, leaf_ref, one_ref, two_ref, three_ref, right_ref, left_ref, skel_ref):
    level = []
    for a in range(LEAVES_HERE):
        y = x_ref[:, a * LEAF : (a + 1) * LEAF] * COORD_SCALE
        left, right = operands(y)
        left_ref[a] = left
        right_ref[a] = right.T
        level.append(pick(parts_of(y), leaf_ref[a : a + 1, :]))
    for ref in (one_ref, two_ref, three_ref):
        level = [
            pick(jnp.concatenate([level[2 * n], level[2 * n + 1]], 1), ref[n : n + 1, :])
            for n in range(len(level) // 2)
        ]
    skel_ref[...] = joined(level[0])


def prep(points, leaf_skel, skel_one, skel_two, skel_three):
    return pl.pallas_call(
        prep_kernel,
        out_shape=[
            shape((LEAVES_HERE, LEAF, 256), BF),
            shape((LEAVES_HERE, 256, LEAF), BF),
            shape((DIMS, RANK)),
        ],
        in_specs=[VMEM] * 5,
        out_specs=[VMEM] * 3,
        compiler_params=pltpu.CompilerParams(vmem_limit_bytes=40 << 20),
        cost_estimate=pl.CostEstimate(flops=2 * 10**9, bytes_accessed=5 << 20, transcendentals=0),
        name="prep_own",
    )(points, leaf_skel, skel_one, skel_two, skel_three)


def prep_near_kernel(low_ref, high_ref, right_ref):
    for side, ref in enumerate((low_ref, high_ref)):
        for a in range(LEAVES_HERE):
            y = ref[:, a * LEAF : (a + 1) * LEAF] * COORD_SCALE
            right_ref[side * LEAVES_HERE + a] = operands(y)[1].T


def prep_near(low, high):
    return pl.pallas_call(
        prep_near_kernel,
        out_shape=shape((2 * LEAVES_HERE, LEAF, 256), BF),
        in_specs=[VMEM] * 2,
        out_specs=VMEM,
        compiler_params=pltpu.CompilerParams(vmem_limit_bytes=40 << 20),
        cost_estimate=pl.CostEstimate(flops=2 * 10**9, bytes_accessed=5 << 20, transcendentals=0),
        name="prep_beside",
    )(low, high)


def near_kernel(cross, *refs):
    if cross:
        (dev_ref, list_ref, right_ref, left_ref, low_ref, high_ref, start_ref, out_ref) = refs[:8]
        sources = (low_ref, high_ref)
    else:
        (dev_ref, list_ref, right_ref, left_ref, own_ref, out_ref) = refs[:6]
        sources = (own_ref,)
    total, values, ea, eb, targets, origins = refs[-6:]
    count = len(sources) * LEAVES_HERE
    first = dev_ref[0] * LEAVES_HERE

    for side, ref in enumerate(sources):
        for a in range(LEAVES_HERE):
            values[side * LEAVES_HERE + a] = jnp.concatenate(
                split_three(ref[:, a * LEAF : (a + 1) * LEAF]), 0
            )
    values[count] = jnp.zeros((3 * RHS, LEAF), BF)
    total[...] = jnp.zeros_like(total)

    def collect(a, n):
        if not cross:
            targets[n] = a
            origins[n] = a
            n = n + 1
        for slot in range(SLOTS):
            place = list_ref[a, slot] - first
            inside = (place >= 0) & (place < LEAVES_HERE)
            if cross:
                use = jnp.logical_not(inside)
                origin = jnp.where(place < 0, place + LEAVES_HERE, place)
            else:
                use = inside & (place != a)
                origin = place
            targets[n] = a
            origins[n] = origin
            n = n + use.astype(jnp.int32)
        return n

    filled = lax.fori_loop(0, LEAVES_HERE, collect, jnp.int32(0))
    for extra in range(3):
        targets[filled + extra] = 0
        origins[filled + extra] = count

    def exponent(t):
        return mm(right_ref[jnp.minimum(origins[t], count - 1)], left_ref[targets[t]])

    def add(t, e):
        a = targets[t]
        v = values[origins[t]]
        block = jnp.exp2(e)
        high = block.astype(BF)
        low = (block - high.astype(F)).astype(BF)
        total[a, 0:32] += mm(v[:32], high)
        total[a, 0:16] += mm(v[:16], low)

    ea[...] = exponent(0)

    def pair(p, carry):
        t = 2 * p
        eb[...] = exponent(t + 1)
        add(t, ea[...])
        ea[...] = exponent(t + 2)
        add(t + 1, eb[...])
        return carry

    lax.fori_loop(0, (filled + 1) // 2, pair, 0)
    for a in range(LEAVES_HERE):
        cols = slice(a * LEAF, (a + 1) * LEAF)
        result = total[a, 0:16] + total[a, 16:32]
        if cross:
            result = start_ref[:, cols] + result
        out_ref[:, cols] = result


def near(cross, device, near_list, right, left, *fields):
    count = LEAVES_HERE * (2 if cross else 1)
    return pl.pallas_call(
        functools.partial(near_kernel, cross),
        out_shape=shape((RHS, WIDTH)),
        in_specs=[SMEM, SMEM] + [VMEM] * (2 + len(fields)),
        out_specs=VMEM,
        scratch_shapes=[
            pltpu.VMEM((LEAVES_HERE, 32, LEAF), F),
            pltpu.VMEM((count + 1, 3 * RHS, LEAF), BF),
            pltpu.VMEM((LEAF, LEAF), F),
            pltpu.VMEM((LEAF, LEAF), F),
            pltpu.SMEM((LEAVES_HERE * (SLOTS + 1) + 8,), jnp.int32),
            pltpu.SMEM((LEAVES_HERE * (SLOTS + 1) + 8,), jnp.int32),
        ],
        compiler_params=pltpu.CompilerParams(vmem_limit_bytes=40 << 20),
        cost_estimate=pl.CostEstimate(
            flops=20 * 10**9, bytes_accessed=8 << 20, transcendentals=30 * LEAF * LEAF
        ),
        name="near_beside" if cross else "near_own",
    )(device, near_list, right, left, *fields)


def row_of_sums(products):
    folded = []
    for value in products:
        piece = value[:, 0:RANK]
        for t in range(1, WIDTH // RANK):
            piece = piece + value[:, t * RANK : (t + 1) * RANK]
        folded.append(piece)
    rest = RANK - RHS * len(folded)
    stacked = jnp.concatenate(folded + [jnp.zeros((rest, RANK), F)], 0)
    return jnp.sum(stacked.T, 0, keepdims=True)


def up_kernel(sums, *refs):
    if sums:
        v_ref, base_ref, interp_ref, one_ref, two_ref, three_ref, out_ref = refs
    else:
        v_ref, interp_ref, one_ref, two_ref, three_ref, out_ref = refs
    level = [
        dot_split(v_ref[:, a * LEAF : (a + 1) * LEAF], interp_ref[a]) for a in range(LEAVES_HERE)
    ]
    for ref in (one_ref, two_ref, three_ref):
        level = [
            dot_split(jnp.concatenate([level[2 * n], level[2 * n + 1]], 1), ref[n])
            for n in range(len(level) // 2)
        ]
    message = level[0]
    if sums:
        base = base_ref[...]
        row = row_of_sums([base * base, base * v_ref[...]])
        message = jnp.concatenate([message, row, jnp.zeros((7, RANK), F)], 0)
    out_ref[...] = jnp.broadcast_to(message[None], out_ref.shape)


def up(sums, fields, interp, up_one, up_two, up_three):
    rows = RHS + (8 if sums else 0)
    return pl.pallas_call(
        functools.partial(up_kernel, sums),
        out_shape=shape((DEVICES, rows, RANK)),
        in_specs=[VMEM] * (len(fields) + 4),
        out_specs=VMEM,
        compiler_params=pltpu.CompilerParams(vmem_limit_bytes=40 << 20),
        cost_estimate=pl.CostEstimate(flops=10**9, bytes_accessed=5 << 20, transcendentals=0),
        name="up_sums" if sums else "up",
    )(*fields, interp, up_one, up_two, up_three)


def skel_kernel(dev_ref, three_ref, top_ref, skel_ref, index_ref, out_ref):
    dev = dev_ref[0]

    def base(n):
        return parts_of(skel_ref[n])

    def four(n):
        both = jnp.concatenate([base(2 * n), base(2 * n + 1)], 1)
        return pick(both, index_ref[pl.ds(n, 1), :])

    def five(n):
        both = jnp.concatenate([four(2 * n), four(2 * n + 1)], 1)
        return pick(both, index_ref[pl.ds(NODES_FOUR + n, 1), :])

    def block(slot, own_left, other, weight):
        right = operands(joined(other))[1]
        out_ref[slot] = jnp.exp2(mm(right.T, own_left)) * weight

    node_four = dev // 2
    node_five = dev // 4
    left = operands(skel_ref[dev])[0]
    for s in range(2):
        other = three_ref[0, s]
        block(s, left, base(other), jnp.where(other != dev, 1.0, 0.0))
    left = operands(joined(four(node_four)))[0]
    for s in range(TOP_SLOTS):
        other = top_ref[node_four, s]
        block(2 + s, left, four(other), jnp.where(other != node_four, 1.0, 0.0))
    left = operands(joined(five(node_five)))[0]
    for s in range(TOP_SLOTS):
        other = top_ref[NODES_FOUR + node_five, s] - NODES_FOUR
        block(6 + s, left, five(other), jnp.where(other != node_five, 1.0, 0.0))


def skeleton_blocks(device, far_three, far_top, skels, skel_top):
    return pl.pallas_call(
        skel_kernel,
        out_shape=shape((2 + 2 * TOP_SLOTS, RANK, RANK)),
        in_specs=[SMEM, SMEM, SMEM, VMEM, VMEM],
        out_specs=VMEM,
        compiler_params=pltpu.CompilerParams(vmem_limit_bytes=40 << 20),
        cost_estimate=pl.CostEstimate(flops=10**9, bytes_accessed=4 << 20, transcendentals=163840),
        name="skeleton_blocks",
    )(device, far_three, far_top, skels, skel_top)


def down_kernel(last, *refs):
    (dev_ref, three_ref, top_ref, message_ref, block_ref, up_top_ref) = refs[:6]
    (interp_ref, one_ref, two_ref, up_three_ref, field_ref, near_ref) = refs[6:12]
    if last:
        base_ref, out_ref, row_ref, weights, arrived = refs[12:]
    else:
        out_ref, weights, arrived = refs[12:]
    dev = dev_ref[0]
    node_four = dev // 2
    node_five = dev // 4
    fours = [top_ref[node_four, s] for s in range(TOP_SLOTS)]
    fives = [top_ref[NODES_FOUR + node_five, s] - NODES_FOUR for s in range(TOP_SLOTS)]
    wanted = []
    for n in fives:
        wanted += [2 * n, 2 * n + 1, NODES_FOUR + n]
    wanted += fours
    wanted += [NODES_FOUR + node_five, node_four]
    copies = [
        pltpu.make_async_copy(up_top_ref.at[n], weights.at[i], arrived.at[i])
        for i, n in enumerate(wanted)
    ]
    for copy in copies:
        copy.start()

    def charge(n):
        return message_ref[n, 0:RHS, :]

    def lift(n, weight):
        return dot_split(jnp.concatenate([charge(2 * n), charge(2 * n + 1)], 1), weight)

    field_three = jnp.zeros((RHS, RANK), F)
    for s in range(2):
        field_three = field_three + dot_split(charge(three_ref[0, s]), block_ref[s])
    for copy in copies:
        copy.wait()
    field_five = jnp.zeros((RHS, RANK), F)
    for s, n in enumerate(fives):
        low = lift(2 * n, weights[3 * s])
        high = lift(2 * n + 1, weights[3 * s + 1])
        q = dot_split(jnp.concatenate([low, high], 1), weights[3 * s + 2])
        field_five = field_five + dot_split(q, block_ref[6 + s])
    field_four = jnp.zeros((RHS, RANK), F)
    for s, n in enumerate(fours):
        q = lift(n, weights[12 + s])
        field_four = field_four + dot_split(q, block_ref[2 + s])

    def half(i, side):
        return weights[i, pl.ds(pl.multiple_of(side * RANK, RANK), RANK), :]

    field_four = field_four + dot_split(field_five, half(16, node_four % 2), NT)
    level = [field_three + dot_split(field_four, half(17, dev % 2), NT)]
    for ref in (up_three_ref, two_ref, one_ref):
        spread = [dot_split(h, ref[n], NT) for n, h in enumerate(level)]
        level = [s[:, side * RANK : (side + 1) * RANK] for s in spread for side in range(2)]
    for a in range(LEAVES_HERE):
        cols = slice(a * LEAF, (a + 1) * LEAF)
        far = dot_split(level[a], interp_ref[a], NT)
        out_ref[:, cols] = RIDGE_TERM * field_ref[:, cols] + near_ref[:, cols] + far
    if last:
        step = first_step(jnp.sum(message_ref[:, RHS : RHS + 8, :], 0))
        image = field_ref[...]
        residual = base_ref[...] - step * image
        moved = image - step * out_ref[...]
        row = row_of_sums(
            [residual * residual, residual * moved, base_ref[...] * moved, residual * image]
        )
        row_ref[...] = jnp.broadcast_to(row, row_ref.shape)


def columns(row_block):
    return row_block.T[:, 0:1]


def first_step(row_block):
    sums = columns(row_block)
    return sums[0:RHS] / sums[RHS : 2 * RHS]


def down(last, device, far_three, far_top, message, blocks, up_top, weights, field, near_part, base):
    out = [shape((RHS, WIDTH))]
    extra = []
    if last:
        out.append(shape((DEVICES, RANK)))
        extra = [base]
    return pl.pallas_call(
        functools.partial(down_kernel, last),
        out_shape=out,
        in_specs=[SMEM] * 3 + [VMEM] * 2 + [ANY] + [VMEM] * (6 + len(extra)),
        out_specs=[VMEM] * len(out),
        scratch_shapes=[pltpu.VMEM((18, 2 * RANK, RANK), F), pltpu.SemaphoreType.DMA((18,))],
        compiler_params=pltpu.CompilerParams(vmem_limit_bytes=40 << 20),
        cost_estimate=pl.CostEstimate(flops=10**9, bytes_accessed=9 << 20, transcendentals=0),
        name="down_sums" if last else "down",
    )(device, far_three, far_top, message, blocks, up_top, *weights, field, near_part, *extra)


def finish_kernel(rows_ref, message_ref, base_ref, image_ref, second_ref, solution_ref, residual_ref):
    before = columns(jnp.sum(message_ref[:, RHS : RHS + 8, :], 0))
    rows = jnp.sum(rows_ref[...], 0, keepdims=True)
    after = columns(jnp.broadcast_to(rows, (8, RANK)))
    norm, curvature = before[0:RHS], before[RHS : 2 * RHS]
    step = norm / curvature
    norm_next, rm, bm, ri = [after[q * RHS : (q + 1) * RHS] for q in range(4)]
    turn = norm_next / norm
    second_curvature = rm + turn * (bm + ri + turn * curvature)
    second_step = norm_next / second_curvature
    base = base_ref[...]
    image = image_ref[...]
    residual = base - step * image
    direction = residual + turn * base
    moved = image - step * second_ref[...] + turn * image
    solution_ref[...] = step * base + second_step * direction
    residual_ref[...] = residual - second_step * moved


def finish(rows, message, base, image, second):
    return pl.pallas_call(
        finish_kernel,
        out_shape=[shape((RHS, WIDTH))] * 2,
        in_specs=[VMEM] * 5,
        out_specs=[VMEM] * 2,
        compiler_params=pltpu.CompilerParams(vmem_limit_bytes=40 << 20),
        cost_estimate=pl.CostEstimate(flops=10**6, bytes_accessed=4 << 20, transcendentals=0),
        name="finish",
    )(rows, message, base, image, second)


def beside(value):
    forward = [(i, i + 1) for i in range(DEVICES - 1)]
    backward = [(target, source) for source, target in forward]
    return lax.ppermute(value, AXES, forward), lax.ppermute(value, AXES, backward)


def everyone(copies):
    return lax.all_to_all(copies, AXES, 0, 0, tiled=True)


def local(
    points,
    right_side,
    interp,
    leaf_skel,
    up_one,
    skel_one,
    up_two,
    skel_two,
    up_three,
    skel_three,
    up_top,
    skel_top,
    near_list,
    far_three,
    far_top,
):
    device = lax.axis_index(AXES).astype(jnp.int32).reshape(1)
    weights = (interp, up_one, up_two, up_three)
    points_low, points_high = beside(points)
    base_low, base_high = beside(right_side)
    right, left, skel = prep(points, leaf_skel, skel_one, skel_two, skel_three)
    skels = everyone(jnp.broadcast_to(skel[None], (DEVICES, DIMS, RANK)))
    message = everyone(up(False, (right_side,), *weights))
    part = near(False, device, near_list, right, left, right_side)
    right_beside = prep_near(points_low, points_high)
    part = near(True, device, near_list, right_beside, left, base_low, base_high, part)
    blocks = skeleton_blocks(device, far_three, far_top, skels, skel_top)
    (image,) = down(
        False, device, far_three, far_top, message, blocks, up_top, weights, right_side, part, None
    )
    image_low, image_high = beside(image)
    message = everyone(up(True, (image, right_side), *weights))
    part = near(False, device, near_list, right, left, image)
    part = near(True, device, near_list, right_beside, left, image_low, image_high, part)
    second, rows = down(
        True, device, far_three, far_top, message, blocks, up_top, weights, image, part, right_side
    )
    rows = everyone(rows)
    return tuple(finish(rows, message, right_side, image, second))


def solution(mesh):
    both = ("leaf", "sub")
    placed = (
        P(None, both),
        P(None, both),
        P(both, None, None),
        P(both, None),
        P(both, None, None),
        P(both, None),
        P(both, None, None),
        P(both, None),
        P(both, None, None),
        P(both, None),
        P(),
        P(),
        P(both, None),
        P(both, None),
        P(),
    )
    return jax.shard_map(
        local,
        mesh=mesh,
        in_specs=placed,
        out_specs=(P(None, both), P(None, both)),
        check_vma=False,
    )
```

time: 1310 us -> 196 us (0.15); the launches traced: 1300 us -> 197 us
  blocking collectives: 834 us -> 17 us
  matrix products: 186 us -> 0 us
  local copies, waits for them, and re-layouts: 161 us -> 33.4 us
  Pallas kernels: 0 us -> 85 us
  other arithmetic: 51.1 us -> 0 us
  between operations: 20.3 us -> 1.03 us
  starting transfers between devices: 38 us -> 51.5 us
    psum x3 -> x0, blocking collectives: 638 us -> none  [the longest x2 351 us: residual_norm(): return lax.psum(jnp.sum(field_now * field_now, 1), ('leaf', 'sub'))]
    all_gather x5 -> x0, blocking collectives: 196 us -> none  [the longest x2 87.3 us: local(): lax.all_gather(far_piece_four, ('leaf', 'sub'), axis=0, tiled=True)]
    dot_general x57 -> x0, matrix products: 186 us -> none  [the longest x7 63.6 us: kernel_blocks(): jnp.einsum('dlm,dln->lmn', left_pts, right_pts, precision=exact_answer)]
    pallas_call x0 -> x12, Pallas kernels: none -> 85 us  [the longest x4 60.2 us: near(): pl.pallas_call(functools.partial(near_kernel, cross), out_shape=shape((RH...]
    gather x38 -> x0, local copies, waits for them, and re-layouts: 83.7 us -> none  [the longest x8 16.2 us: interact(): jnp.take(pool_charges, other_ids, axis=0)]
    reshape x23 -> x0, local copies, waits for them, and re-layouts: 40.8 us -> none  [the longest x1 13.8 us: local(): skel_five = got_five.reshape(top_four // 2, 4, DIMS, RANK // 4).transpose...]
    all_to_all x0 -> x3, starting transfers between devices: none -> 34.1 us  [everyone(): return lax.all_to_all(copies, AXES, 0, 0, tiled=True)]
    ppermute x18 -> x6, starting transfers between devices: 37.9 us -> 17.5 us  [the longest x3 10.5 us: beside(): lax.ppermute(value, AXES, forward)]
  transfers between devices with their start and end apart: 19 -> 9, of which waited for: 0 -> 2; matrix products, arithmetic and copies ran while one was open for 16% -> 1% of each run, Pallas kernels for 0% -> 35%
where the time goes in v1:
time: 196 us; the launch traced here: 197 us
  Pallas kernels  85 us (43%)
  starting transfers between devices  51.5 us (26%)
  local copies, waits for them, and re-layouts  33.4 us (17%)
  blocking collectives  17 us (9%)
  waiting for transfers between devices  9.21 us (5%)
    pallas_call x4, Pallas kernels, near(): pl.pallas_call(functools.partial(near_kernel, cross), out_shape=shape((RH...  60.2 us
    all_to_all x3, starting transfers between devices, everyone(): return lax.all_to_all(copies, AXES, 0, 0, tiled=True)  34.1 us
    unnamed x79, local copies, waits for them, and re-layouts  31.7 us
    all_to_all x1, blocking collectives, everyone(): return lax.all_to_all(copies, AXES, 0, 0, tiled=True)  17 us
    pallas_call x2, Pallas kernels, down(): pl.pallas_call(functools.partial(down_kernel, last), out_shape=out, in_sp...  13.1 us
    ppermute x3, starting transfers between devices, beside(): lax.ppermute(value, AXES, forward)  10.5 us
    all_to_all x3, waiting for transfers between devices, everyone(): return lax.all_to_all(copies, AXES, 0, 0, tiled=True)  9.19 us
    ppermute x3, starting transfers between devices, beside(): lax.ppermute(value, AXES, backward)  6.95 us
  transfers between devices with their start and end apart: 9, of which 2 were waited for; matrix products, arithmetic and copies ran while one was open for 1% of the time, Pallas kernels for 35%

profile of v1, /device:TPU:1, one launch (start us, length us, event | category | flops | bytes accessed | tf_op | source)
XLA Modules:
  0.0 197.1 jit_solution(5227503759357572264)
XLA Ops:
  0.6 4.9 %collective-permute-start = (f32[32,4096]{1,0:T(8,128)}, f32[32,4096]{1,0:T(8,128)}, u32[]{:S(2)}, u32[]{:S(2)}) collective-permute-start(f32[32,4096]{1,0:T(8,128)} %x_ref.1), channel_id=1, source_target_pairs={{0,1},{1,2},{2,3},{3,4},{4,5},{5,6},{6,7},{7,8},{8,9},{9,10},{10,1... | collective-permute-start | bytes 1572872 | tf_op jit(solution)/shard_map/ppermute | solution.py:462
  5.6 1.9 collective-permute-start.1
  7.5 3.6 %collective-permute-start.2 = (f32[16,4096]{1,0:T(8,128)}, f32[16,4096]{1,0:T(8,128)}, u32[]{:S(2)}, u32[]{:S(2)}) collective-permute-start(f32[16,4096]{1,0:T(8,128)} %base_ref.1), channel_id=1, source_target_pairs={{0,1},{1,2},{2,3},{3,4},{4,5},{5,6},{6,7},{7,8},{8,9},{9,10},{10,1... | collective-permute-start | bytes 786440 | tf_op jit(solution)/shard_map/ppermute | solution.py:462
  11.2 1.9 collective-permute-start.3
  13.1 1.0 copy-done.18
  16.8 1.0 prep_own.1
  17.8 1.4 copy-done.28
  19.2 1.4 copy-done.33
  20.6 1.7 broadcast_in_dim.2
  22.3 13.0 %all-to-all-start.1 = ((f32[128,32,128]{2,1,0:T(8,128)}), f32[128,32,128]{2,1,0:T(8,128)}, u32[]{:S(2)}, u32[]{:S(2)}) async-start(f32[128,32,128]{2,1,0:T(8,128)} %broadcast_in_dim.2), calls=%async_computation.1 | async-start | bytes 4194304 | tf_op jit(solution)/shard_map/all_to_all | solution.py:466
  35.3 1.6 copy-done.29
  36.9 1.6 copy-done.34
  38.5 14.7 %near_own.2.refs_6_ = f32[16,4096]{1,0:T(8,128)S(1)} custom-call(s32[1]{0:T(128)} %bitcast.dev_ref.refs_0_, s32[8,12]{1,0:T(8,128)S(1)} %copy-done.21, bf16[8,512,256]{2,1,0:T(8,128)(2,1)S(1)} %copy-done.34, bf16[8,256,512]{2,1,0:T(8,128)(2,1)S(1)} %copy-done.29, f32[16,4096]{1,0:T(8,128)S(1)} %copy-done.2), custom_call_target="tpu_custom_call" | custom-call | flops 20000000000 | bytes 8388608 | tf_op jit(solution)/shard_map/near_own/pallas_call | solution.py:219
  53.3 0.7 copy.22.top_ref.refs_2_
  54.0 0.9 up.1
  54.9 1.0 copy-done.5
  55.9 2.4 %prep_beside.1.refs_2_ = bf16[16,512,256]{2,1,0:T(8,128)(2,1)S(1)} custom-call(f32[32,4096]{1,0:T(8,128)} %collective-permute-done.low_ref, f32[32,4096]{1,0:T(8,128)} %collective-permute-done.1.high_ref), custom_call_target="tpu_custom_call" | custom-call | flops 2000000000 | bytes 5242880 | tf_op jit(solution)/shard_map/prep_beside/pallas_call | solution.py:132
  58.2 2.0 copy-done.25
  60.2 5.2 %all-to-all-done.1.skel_ref = f32[128,32,128]{2,1,0:T(8,128)} async-done(((f32[128,32,128]{2,1,0:T(8,128)}), f32[128,32,128]{2,1,0:T(8,128)}, u32[]{:S(2)}, u32[]{:S(2)}) %all-to-all-start.1) | async-done | bytes 2097184 | tf_op jit(solution)/shard_map/all_to_all | solution.py:466
  65.4 7.0 %all-to-all-start = ((f32[128,16,128]{2,1,0:T(8,128)}), f32[128,16,128]{2,1,0:T(8,128)}, u32[]{:S(2)}, u32[]{:S(2)}) async-start(f32[128,16,128]{2,1,0:T(8,128)} %copy-done.5), calls=%async_computation | async-start | bytes 2097152 | tf_op jit(solution)/shard_map/all_to_all | solution.py:466
  72.5 2.2 %copy-done.26 = bf16[16,512,256]{2,1,0:T(8,128)(2,1)S(1)} copy-done((bf16[16,512,256]{2,1,0:T(8,128)(2,1)S(1)}, bf16[16,512,256]{2,1,0:T(8,128)(2,1)}, u32[]{:S(2)}) %copy-start.26) | copy-done | bytes 4194328
  74.7 1.6 copy-done.30
  76.3 15.2 %near_beside.2.refs_11_ = f32[16,4096]{1,0:T(8,128)S(1)} custom-call(s32[1]{0:T(128)} %bitcast.dev_ref.refs_0_, s32[8,12]{1,0:T(8,128)S(1)} %copy-done.21, bf16[16,512,256]{2,1,0:T(8,128)(2,1)S(1)} %copy-done.26, bf16[8,256,512]{2,1,0:T(8,128)(2,1)S(1)} %copy-done.30, f32[16,4096]{1,0:T(8,128)} %collective-permute-done.2.refs_4_, ...), custom_call_target="tpu_custom_call" | custom-call | flops 20000000000 | bytes 8388608 | tf_op jit(solution)/shard_map/near_beside/pallas_call | solution.py:219
  91.5 0.7 copy-done.15
  92.2 3.9 %skeleton_blocks.1.refs_4_ = f32[10,128,128]{2,1,0:T(8,128)S(1)} custom-call(s32[1]{0:T(128)} %bitcast.dev_ref.refs_0_, s32[1,2]{1,0:T(1,128)S(1)} %copy-done.17, s32[96,4]{1,0:T(8,128)S(1)} %copy-done.10, f32[128,32,128]{2,1,0:T(8,128)} %all-to-all-done.1.skel_ref, s32[96,128]{1,0:T(8,128)S(1)} %copy-done.19), custom_call_target="tpu_custom_call" | custom-call | flops 1000000000 | bytes 4194304 | tf_op jit(solution)/shard_map/skeleton_blocks/pallas_call | solution.py:321
  96.1 0.8 copy-done.6
  96.9 1.1 copy-done.7
  98.0 0.8 copy-done.11
  98.8 0.9 copy-done.16
  99.8 6.6 %down.1.refs_0_.refs_4_.refs_10_.image_ref = f32[16,4096]{1,0:T(8,128)S(1)} custom-call(s32[1]{0:T(128)} %bitcast.dev_ref.refs_0_, s32[1,2]{1,0:T(1,128)S(1)} %copy-done.17, s32[96,4]{1,0:T(8,128)S(1)} %copy-done.11, f32[128,16,128]{2,1,0:T(8,128)} %all-to-all-done.refs_3_, f32[10,128,128]{2,1,0:T(8,128)S(1)} %copy-done.7, f32[96,256,128]{2,1,0:T(8,128)} %refs_5_.5, ...), custom_call_target="tpu_custom_call" | custom-call | flops 1000000000 | bytes 9437184 | tf_op jit(solution)/shard_map/down/pallas_call | solution.py:416
  106.3 1.9 collective-permute-start.4
  108.3 3.1 %collective-permute-start.5 = (f32[16,4096]{1,0:T(8,128)S(1)}, f32[16,4096]{1,0:T(8,128)}, u32[]{:S(2)}, u32[]{:S(2)}) collective-permute-start(f32[16,4096]{1,0:T(8,128)S(1)} %down.1.refs_0_.refs_4_.refs_10_.image_ref), channel_id=1, source_target_pairs={{1,0},{2,1},{3,2},{4,3},{5,4},{6,5},{7,6},{8,7},{9,8},{10,9},{11,1... | collective-permute-start | bytes 786440 | tf_op jit(solution)/shard_map/ppermute | solution.py:462
  111.4 15.1 %near_own.3.refs_6_ = f32[16,4096]{1,0:T(8,128)S(1)} custom-call(s32[1]{0:T(128)} %bitcast.dev_ref.refs_0_, s32[8,12]{1,0:T(8,128)S(1)} %copy-done.21, bf16[8,512,256]{2,1,0:T(8,128)(2,1)S(1)} %copy-done.35, bf16[8,256,512]{2,1,0:T(8,128)(2,1)S(1)} %copy-done.31, f32[16,4096]{1,0:T(8,128)S(1)} %down.1.refs_0_.refs_4_.refs_10_.image_ref), custom_call_target="tpu_custom_call" | custom-call | flops 20000000000 | bytes 8388608 | tf_op jit(solution)/shard_map/near_own/pallas_call | solution.py:219
  126.6 0.7 copy-done.36
  127.3 0.9 up_sums.1
  128.1 1.2 copy-done.3
  129.4 14.1 %all-to-all-start.2 = ((f32[128,24,128]{2,1,0:T(8,128)}), f32[128,24,128]{2,1,0:T(8,128)}, u32[]{:S(2)}, u32[]{:S(2)}) async-start(f32[128,24,128]{2,1,0:T(8,128)} %copy-done.3), calls=%async_computation.2 | async-start | bytes 3145728 | tf_op jit(solution)/shard_map/all_to_all | solution.py:466
  143.5 2.2 %copy-done.27 = bf16[16,512,256]{2,1,0:T(8,128)(2,1)S(1)} copy-done((bf16[16,512,256]{2,1,0:T(8,128)(2,1)S(1)}, bf16[16,512,256]{2,1,0:T(8,128)(2,1)}, u32[]{:S(2)}) %copy-start.27) | copy-done | bytes 4194328
  145.7 1.6 copy-done.32
  147.3 0.9 copy-done.37
  148.2 15.2 %near_beside.3.refs_11_ = f32[16,4096]{1,0:T(8,128)S(1)} custom-call(s32[1]{0:T(128)} %bitcast.dev_ref.refs_0_, s32[8,12]{1,0:T(8,128)S(1)} %copy-done.21, bf16[16,512,256]{2,1,0:T(8,128)(2,1)S(1)} %copy-done.27, bf16[8,256,512]{2,1,0:T(8,128)(2,1)S(1)} %copy-done.32, f32[16,4096]{1,0:T(8,128)} %collective-permute-done.4.refs_4_, ...), custom_call_target="tpu_custom_call" | custom-call | flops 20000000000 | bytes 8388608 | tf_op jit(solution)/shard_map/near_beside/pallas_call | solution.py:219
  164.1 4.0 %all-to-all-done.2.refs_3_.message_ref = f32[128,24,128]{2,1,0:T(8,128)} async-done(((f32[128,24,128]{2,1,0:T(8,128)}), f32[128,24,128]{2,1,0:T(8,128)}, u32[]{:S(2)}, u32[]{:S(2)}) %all-to-all-start.2) | async-done | bytes 1572896 | tf_op jit(solution)/shard_map/all_to_all | solution.py:466
  168.1 1.1 copy-done.8
  169.1 0.8 copy-done.12
  169.9 0.9 copy-done.14
  170.9 6.6 %down_sums.1 = (f32[16,4096]{1,0:T(8,128)S(1)}, f32[128,128]{1,0:T(8,128)S(1)}) custom-call(s32[1]{0:T(128)} %bitcast.dev_ref.refs_0_, s32[1,2]{1,0:T(1,128)S(1)} %copy-done.17, s32[96,4]{1,0:T(8,128)S(1)} %copy-done.12, f32[128,24,128]{2,1,0:T(8,128)} %all-to-all-done.2.refs_3_.message_ref, f32[10,128,128]{2,1,0:T(8,128)S(1)} %copy-done.8, ...), custom_call_target="tpu_custom_call" | custom-call | flops 1000000000 | bytes 9437184 | tf_op jit(solution)/shard_map/down_sums/pallas_call | solution.py:416
  177.5 17.0 %all_to_all.26 = f32[128,1,128]{2,1,0:T(1,128)S(1)} all-to-all(f32[128,1,128]{2,1,0:T(1,128)S(1)} %bitcast.6), channel_id=1, replica_groups=mesh['leaf'=16,'sub'=8] {'leaf','sub'}, dimensions={0} | all-to-all | bytes 131072 | tf_op jit(solution)/shard_map/all_to_all | solution.py:466
  194.4 2.6 %finish.1 = (f32[16,4096]{1,0:T(8,128)}, f32[16,4096]{1,0:T(8,128)}) custom-call(f32[128,128]{1,0:T(8,128)S(1)} %bitcast.5, f32[128,24,128]{2,1,0:T(8,128)} %all-to-all-done.2.refs_3_.message_ref, f32[16,4096]{1,0:T(8,128)S(1)} %copy-done.2, f32[16,4096]{1,0:T(8,128)S(1)} %down.1.refs_0_.refs_4_.refs_10_.image_ref, f32[16,4096]{1,0:T(8,128)S(1)} %get-tuple-element.11.second_ref), custom_call_target="tpu_custom_call" | custom-call | flops 1000000 | bytes 4194304 | tf_op jit(solution)/shard_map/finish/pallas_call | solution.py:448
  (63 shorter events, 3.5 us)
Async XLA Ops:
  0.6 55.2 %collective-permute-start = (f32[32,4096]{1,0:T(8,128)}, f32[32,4096]{1,0:T(8,128)}, u32[]{:S(2)}, u32[]{:S(2)}) collective-permute-start(f32[32,4096]{1,0:T(8,128)} %x_ref.1), channel_id=1, source_target_pairs={{0,1},{1,2},{2,3},{3,4},{4,5},{5,6},{6,7},{7,8},{8,9},{9,10},{10,1... | collective-permute-start | bytes 1572872 | tf_op jit(solution)/shard_map/ppermute | solution.py:462
  5.6 50.3 %collective-permute-start.1 = (f32[32,4096]{1,0:T(8,128)}, f32[32,4096]{1,0:T(8,128)}, u32[]{:S(2)}, u32[]{:S(2)}) collective-permute-start(f32[32,4096]{1,0:T(8,128)} %x_ref.1), channel_id=1, source_target_pairs={{1,0},{2,1},{3,2},{4,3},{5,4},{6,5},{7,6},{8,7},{9,8},{10,9},{11,1... | collective-permute-start | bytes 1572872 | tf_op jit(solution)/shard_map/ppermute | solution.py:462
  7.5 65.0 %collective-permute-start.2 = (f32[16,4096]{1,0:T(8,128)}, f32[16,4096]{1,0:T(8,128)}, u32[]{:S(2)}, u32[]{:S(2)}) collective-permute-start(f32[16,4096]{1,0:T(8,128)} %base_ref.1), channel_id=1, source_target_pairs={{0,1},{1,2},{2,3},{3,4},{4,5},{5,6},{6,7},{7,8},{8,9},{9,10},{10,1... | collective-permute-start | bytes 786440 | tf_op jit(solution)/shard_map/ppermute | solution.py:462
  11.2 61.3 %collective-permute-start.3 = (f32[16,4096]{1,0:T(8,128)}, f32[16,4096]{1,0:T(8,128)}, u32[]{:S(2)}, u32[]{:S(2)}) collective-permute-start(f32[16,4096]{1,0:T(8,128)} %base_ref.1), channel_id=1, source_target_pairs={{1,0},{2,1},{3,2},{4,3},{5,4},{6,5},{7,6},{8,7},{9,8},{10,9},{11,1... | collective-permute-start | bytes 786440 | tf_op jit(solution)/shard_map/ppermute | solution.py:462
  13.1 1.0 copy-start.18
  14.1 0.7 copy-start.20
  14.8 0.7 copy-start.22
  15.5 0.7 copy-start.23
  16.2 0.7 copy-start.24
  17.8 1.4 copy-start.28
  19.2 1.4 copy-start.33
  22.3 13.0 %copy-start.2 = (f32[16,4096]{1,0:T(8,128)S(1)}, f32[16,4096]{1,0:T(8,128)}, u32[]{:S(2)}) copy-start(f32[16,4096]{1,0:T(8,128)} %base_ref.1) | copy-start | bytes 786436
  22.3 13.0 %copy-start.21 = (s32[8,12]{1,0:T(8,128)S(1)}, s32[8,12]{1,0:T(8,128)}, u32[]{:S(2)}) copy-start(s32[8,12]{1,0:T(8,128)} %refs_1_.14) | copy-start | bytes 1156
  22.3 43.2 %all-to-all-start.1 = ((f32[128,32,128]{2,1,0:T(8,128)}), f32[128,32,128]{2,1,0:T(8,128)}, u32[]{:S(2)}, u32[]{:S(2)}) async-start(f32[128,32,128]{2,1,0:T(8,128)} %broadcast_in_dim.2), calls=%async_computation.1 | async-start | bytes 4194304 | tf_op jit(solution)/shard_map/all_to_all | solution.py:466
  35.3 1.6 copy-start.29
  36.9 1.6 copy-start.34
  38.5 14.8 %copy-start.38 = (s32[96,4]{0,1:T(4,128)S(1)}, s32[96,4]{0,1:T(4,128)}, u32[]{:S(2)}) copy-start(s32[96,4]{0,1:T(4,128)} %param.29) | copy-start | bytes 4612
  38.5 15.5 %copy-start = (f32[8,512,128]{2,1,0:T(8,128)S(1)}, f32[8,512,128]{2,1,0:T(8,128)}, u32[]{:S(2)}) copy-start(f32[8,512,128]{2,1,0:T(8,128)} %refs_6_.3) | copy-start | bytes 6291460
  38.5 15.5 %copy-start.1 = (f32[4,256,128]{2,1,0:T(8,128)S(1)}, f32[4,256,128]{2,1,0:T(8,128)}, u32[]{:S(2)}) copy-start(f32[4,256,128]{2,1,0:T(8,128)} %refs_7_.3) | copy-start | bytes 1572868
  38.5 15.5 %copy-start.4 = (f32[2,256,128]{2,1,0:T(8,128)S(1)}, f32[2,256,128]{2,1,0:T(8,128)}, u32[]{:S(2)}) copy-start(f32[2,256,128]{2,1,0:T(8,128)} %refs_8_.3) | copy-start | bytes 786436
  38.5 15.5 %copy-start.9 = (f32[1,256,128]{2,1,0:T(8,128)S(1)}, f32[1,256,128]{2,1,0:T(8,128)}, u32[]{:S(2)}) copy-start(f32[1,256,128]{2,1,0:T(8,128)} %refs_9_.3) | copy-start | bytes 393220
  54.9 1.0 copy-start.5
  58.2 2.0 copy-start.25
  65.4 31.5 %all-to-all-start = ((f32[128,16,128]{2,1,0:T(8,128)}), f32[128,16,128]{2,1,0:T(8,128)}, u32[]{:S(2)}, u32[]{:S(2)}) async-start(f32[128,16,128]{2,1,0:T(8,128)} %copy-done.5), calls=%async_computation | async-start | bytes 2097152 | tf_op jit(solution)/shard_map/all_to_all | solution.py:466
  72.4 19.7 %copy-start.10 = (s32[96,4]{1,0:T(8,128)S(1)}, s32[96,4]{1,0:T(8,128)}, u32[]{:S(2)}) copy-start(s32[96,4]{1,0:T(8,128)} %copy.22.top_ref.refs_2_) | copy-start | bytes 4612
  72.4 19.7 %copy-start.17 = (s32[1,2]{1,0:T(1,128)S(1)}, s32[1,2]{1,0:T(1,128)}, u32[]{:S(2)}) copy-start(s32[1,2]{1,0:T(1,128)} %refs_1_.15) | copy-start | bytes 28
  72.4 19.7 %copy-start.19 = (s32[96,128]{1,0:T(8,128)S(1)}, s32[96,128]{1,0:T(8,128)}, u32[]{:S(2)}) copy-start(s32[96,128]{1,0:T(8,128)} %index_ref.1) | copy-start | bytes 147460
  72.5 2.2 %copy-start.26 = (bf16[16,512,256]{2,1,0:T(8,128)(2,1)S(1)}, bf16[16,512,256]{2,1,0:T(8,128)(2,1)}, u32[]{:S(2)}) copy-start(bf16[16,512,256]{2,1,0:T(8,128)(2,1)} %copy-done.25) | copy-start | bytes 12582916
  74.7 1.6 copy-start.30
  91.4 0.7 copy-start.15
  96.1 0.9 copy-start.6
  96.9 1.1 copy-start.7
  98.0 0.8 copy-start.11
  98.8 0.9 copy-start.16
  99.8 11.6 %copy-start.31 = (bf16[8,256,512]{2,1,0:T(8,128)(2,1)S(1)}, bf16[8,256,512]{2,1,0:T(8,128)(2,1)}, u32[]{:S(2)}) copy-start(bf16[8,256,512]{2,1,0:T(8,128)(2,1)} %copy-done.28) | copy-start | bytes 6291460
  99.8 11.6 %copy-start.35 = (bf16[8,512,256]{2,1,0:T(8,128)(2,1)S(1)}, bf16[8,512,256]{2,1,0:T(8,128)(2,1)}, u32[]{:S(2)}) copy-start(bf16[8,512,256]{2,1,0:T(8,128)(2,1)} %copy-done.33) | copy-start | bytes 6291460
  106.3 37.1 %collective-permute-start.4 = (f32[16,4096]{1,0:T(8,128)S(1)}, f32[16,4096]{1,0:T(8,128)}, u32[]{:S(2)}, u32[]{:S(2)}) collective-permute-start(f32[16,4096]{1,0:T(8,128)S(1)} %down.1.refs_0_.refs_4_.refs_10_.image_ref), channel_id=1, source_target_pairs={{0,1},{1,2},{2,3},{3,4},{4,5},{5,6},{6,7},{7,8},{8,9},{9,10},{10,1... | collective-permute-start | bytes 786440 | tf_op jit(solution)/shard_map/ppermute | solution.py:462
  108.3 35.2 %collective-permute-start.5 = (f32[16,4096]{1,0:T(8,128)S(1)}, f32[16,4096]{1,0:T(8,128)}, u32[]{:S(2)}, u32[]{:S(2)}) collective-permute-start(f32[16,4096]{1,0:T(8,128)S(1)} %down.1.refs_0_.refs_4_.refs_10_.image_ref), channel_id=1, source_target_pairs={{1,0},{2,1},{3,2},{4,3},{5,4},{6,5},{7,6},{8,7},{9,8},{10,9},{11,1... | collective-permute-start | bytes 786440 | tf_op jit(solution)/shard_map/ppermute | solution.py:462
  126.6 0.7 copy-start.36
  128.1 1.2 copy-start.3
  129.4 38.7 %all-to-all-start.2 = ((f32[128,24,128]{2,1,0:T(8,128)}), f32[128,24,128]{2,1,0:T(8,128)}, u32[]{:S(2)}, u32[]{:S(2)}) async-start(f32[128,24,128]{2,1,0:T(8,128)} %copy-done.3), calls=%async_computation.2 | async-start | bytes 3145728 | tf_op jit(solution)/shard_map/all_to_all | solution.py:466
  143.5 2.2 %copy-start.27 = (bf16[16,512,256]{2,1,0:T(8,128)(2,1)S(1)}, bf16[16,512,256]{2,1,0:T(8,128)(2,1)}, u32[]{:S(2)}) copy-start(bf16[16,512,256]{2,1,0:T(8,128)(2,1)} %copy-done.25) | copy-start | bytes 12582916
  145.7 1.6 copy-start.32
  147.3 0.9 copy-start.37
  163.4 0.7 copy-start.13
  168.1 1.1 copy-start.8
  169.1 0.8 copy-start.12
  169.9 0.9 copy-start.14

commit v2 on v1

v2 whole, which is shorter than its diff:
```python
import functools
import math

import jax
import jax.numpy as jnp
from jax import lax
from jax.experimental import pallas as pl
from jax.experimental.pallas import tpu as pltpu
from jax.sharding import PartitionSpec as P

LEAF = 512
DIMS = 32
RHS = 16
RANK = 128
LEAVES_HERE = 8
SLOTS = 12
WIDTH = LEAVES_HERE * LEAF
DEVICES = 128
NODES_FOUR = 64
TOP_SLOTS = 4
AT_THREE, AT_FOUR, AT_FIVE, AT_NEAR = 1, 3, 7, 16

RIDGE_TERM = 12.0
COORD_SCALE = math.sqrt(2.0 * math.log2(math.e) / 24.0)

AXES = ("leaf", "sub")
BF = jnp.bfloat16
F = jnp.float32
NN = (((1,), (0,)), ((), ()))
NT = (((1,), (1,)), ((), ()))
SMEM = pl.BlockSpec(memory_space=pltpu.SMEM)
ANY = pl.BlockSpec(memory_space=pl.ANY)


def shape(dims, dtype=F):
    return jax.ShapeDtypeStruct(dims, dtype)


def mm(a, b, dims=NN):
    return lax.dot_general(a, b, dims, preferred_element_type=F)


def split_two(x):
    high = x.astype(BF)
    return high, (x - high.astype(F)).astype(BF)


def split_three(x):
    high = x.astype(BF)
    rest = x - high.astype(F)
    mid = rest.astype(BF)
    return high, mid, (rest - mid.astype(F)).astype(BF)


def dot_split(a, w, dims=NN):
    ah, am = split_two(a)
    wh, wm = split_two(w)
    both = mm(jnp.concatenate([ah, am], 0), wh, dims)
    return both[:RHS] + both[RHS:] + mm(ah, wm, dims)


def operands(y):
    n = y.shape[1]
    h, m, l = split_three(y)
    half = 0.5 * jnp.sum(y * y, 0, keepdims=True)
    parts = [p.astype(F) for p in split_three(half)]
    one = [jnp.ones((1, n), F)] * 3
    pad = [jnp.zeros((10, n), F)]
    tail_left = jnp.concatenate(parts + one + pad, 0).astype(BF)
    tail_right = jnp.concatenate([-p for p in one + parts] + pad, 0).astype(BF)
    zero = jnp.zeros((48, n), BF)
    left = jnp.concatenate([h, h, m, h, l, m, tail_left, zero], 0)
    right = jnp.concatenate([h, m, h, l, h, m, tail_right, zero], 0)
    return left, right


def pick(parts, chosen):
    n = parts.shape[1]
    rows = lax.broadcasted_iota(jnp.int32, (n, RANK), 0)
    hot = jnp.where(rows == chosen, 1.0, 0.0).astype(BF)
    return mm(parts, hot).astype(BF)


def joined(parts):
    return parts[0:32].astype(F) + parts[32:64].astype(F) + parts[64:96].astype(F)


def parts_of(y):
    return jnp.concatenate(split_three(y), 0)


class Copies:
    def __init__(self, semaphores):
        self.semaphores = semaphores
        self.used = 0

    def start(self, source, target):
        copy = pltpu.make_async_copy(source, target, self.semaphores.at[self.used])
        self.used += 1
        copy.start()
        return copy


def wait_all(copies):
    for copy in copies:
        copy.wait()


def call(kernel, name, out, ids, inputs, scratch, flops, transcendentals=0):
    operands_given = ([ids] if ids is not None else []) + list(inputs)
    return pl.pallas_call(
        kernel,
        out_shape=out,
        in_specs=([SMEM] if ids is not None else []) + [ANY] * len(inputs),
        out_specs=[ANY] * len(out),
        scratch_shapes=scratch + [pltpu.SemaphoreType.DMA((48,))],
        compiler_params=pltpu.CompilerParams(vmem_limit_bytes=56 << 20),
        cost_estimate=pl.CostEstimate(
            flops=flops, bytes_accessed=6 << 20, transcendentals=transcendentals
        ),
        name=name,
    )(*operands_given)


def scratch_for(arrays):
    return [pltpu.VMEM(a.shape, a.dtype) for a in arrays]


def cols(a):
    return slice(a * LEAF, (a + 1) * LEAF)


def row_of_sums(products):
    folded = []
    for value in products:
        piece = value[:, 0:RANK]
        for t in range(1, WIDTH // RANK):
            piece = piece + value[:, t * RANK : (t + 1) * RANK]
        folded.append(piece)
    rest = RANK - RHS * len(folded)
    stacked = jnp.concatenate(folded + [jnp.zeros((rest, RANK), F)], 0)
    return jnp.sum(stacked.T, 0, keepdims=True)


def climb(field, interp, transfers):
    level = [dot_split(field[:, cols(a)], interp[a]) for a in range(LEAVES_HERE)]
    for ref in transfers:
        level = [
            dot_split(jnp.concatenate([level[2 * n], level[2 * n + 1]], 1), ref[n])
            for n in range(len(level) // 2)
        ]
    return level[0]


def first_kernel(*refs):
    inputs, (message_out, halo_out) = refs[:10], refs[10:12]
    held, (message, semaphores) = refs[12:22], refs[22:]
    copies = Copies(semaphores)
    arrive = [copies.start(source, target) for source, target in zip(inputs, held)]
    points, field, interp, one, two, three, leaf_pick, one_pick, two_pick, three_pick = held
    wait_all(arrive[0:2])
    leave = [
        copies.start(points, halo_out.at[0:DIMS, :]),
        copies.start(field, halo_out.at[DIMS : DIMS + RHS, :]),
    ]
    wait_all(arrive[6:])
    level = [
        pick(parts_of(points[:, cols(a)] * COORD_SCALE), leaf_pick[a : a + 1, :])
        for a in range(LEAVES_HERE)
    ]
    for ref in (one_pick, two_pick, three_pick):
        level = [
            pick(jnp.concatenate([level[2 * n], level[2 * n + 1]], 1), ref[n : n + 1, :])
            for n in range(len(level) // 2)
        ]
    wait_all(arrive[2:6])
    charges = climb(field, interp, (one, two, three))
    block = jnp.concatenate([charges, joined(level[0])], 0)
    message[...] = jnp.broadcast_to(block[None], message.shape)
    leave += send_copies(copies, message, message_out)
    wait_all(leave)


def send_copies(copies, message, message_out):
    count = message.shape[0]
    return [
        copies.start(message, message_out.at[t * count : (t + 1) * count])
        for t in range(DEVICES // count)
    ]


def first(points, right_side, weights, picks):
    inputs = [points, right_side, *weights, *picks]
    return call(
        first_kernel,
        "first_up",
        [shape((DEVICES, RHS + DIMS, RANK)), shape((DIMS + RHS, WIDTH))],
        None,
        inputs,
        scratch_for(inputs) + [pltpu.VMEM((16, RHS + DIMS, RANK), F)],
        10**9,
    )


def near_kernel(fresh, *refs):
    if fresh:
        ids_ref, points_in, field_in, low_in, high_in, part_out, right_out, left_out = refs[:8]
        points, field, low, high = refs[8:12]
    else:
        ids_ref, right_in, left_in, field_in, low_in, high_in, part_out = refs[:7]
        field, low, high = refs[7:10]
    right, left, total, values, ea, eb, part, targets, origins, semaphores = refs[-10:]
    copies = Copies(semaphores)
    arrive_field = copies.start(field_in, field)
    if fresh:
        arrive_own = [copies.start(points_in, points)]
    else:
        arrive_own = [
            copies.start(left_in, left),
            copies.start(right_in.at[0:LEAVES_HERE], right.at[0:LEAVES_HERE]),
        ]
    arrive_beside = [copies.start(low_in, low), copies.start(high_in, high)]
    if not fresh:
        arrive_beside.append(
            copies.start(
                right_in.at[LEAVES_HERE : 3 * LEAVES_HERE], right.at[LEAVES_HERE : 3 * LEAVES_HERE]
            )
        )
    first = ids_ref[0] * LEAVES_HERE
    empty = 3 * LEAVES_HERE
    beside_at = 128

    def collect(a, counts):
        n, m = counts
        targets[n] = a
        origins[n] = a
        n = n + 1
        for slot in range(SLOTS):
            place = ids_ref[AT_NEAR + a * SLOTS + slot] - first
            inside = (place >= 0) & (place < LEAVES_HERE)
            targets[n] = a
            origins[n] = place
            n = n + (inside & (place != a)).astype(jnp.int32)
            targets[m] = a
            origins[m] = jnp.where(place < 0, place + 2 * LEAVES_HERE, place + LEAVES_HERE)
            m = m + jnp.logical_not(inside).astype(jnp.int32)
        return n, m

    own_end, beside_end = lax.fori_loop(
        0, LEAVES_HERE, collect, (jnp.int32(0), jnp.int32(beside_at))
    )
    for end in (own_end, beside_end):
        for extra in range(3):
            targets[end + extra] = 0
            origins[end + extra] = empty

    def take_values(source, at):
        for a in range(LEAVES_HERE):
            values[at + a] = jnp.concatenate(split_three(source[source.shape[0] - RHS :, cols(a)]), 0)

    def exponent(t):
        origin = origins[t]
        return mm(right[jnp.where(origin == empty, 0, origin)], left[targets[t]])

    def add(t, e):
        a = targets[t]
        v = values[origins[t]]
        block = jnp.exp2(e)
        upper = block.astype(BF)
        lower = (block - upper.astype(F)).astype(BF)
        total[a, 0:32] += mm(v[:32], upper)
        total[a, 0:16] += mm(v[:16], lower)

    def run(start, end):
        ea[...] = exponent(start)

        def pair(p, carry):
            t = start + 2 * p
            eb[...] = exponent(t + 1)
            add(t, ea[...])
            ea[...] = exponent(t + 2)
            add(t + 1, eb[...])
            return carry

        lax.fori_loop(0, (end - start + 1) // 2, pair, 0)

    total[...] = jnp.zeros_like(total)
    values[empty] = jnp.zeros((3 * RHS, LEAF), BF)
    wait_all([arrive_field])
    take_values(field, 0)
    wait_all(arrive_own)
    leave = []
    if fresh:
        for a in range(LEAVES_HERE):
            left_part, right_part = operands(points[:, cols(a)] * COORD_SCALE)
            left[a] = left_part
            right[a] = right_part.T
        leave.append(copies.start(left, left_out))
        leave.append(copies.start(right.at[0:LEAVES_HERE], right_out.at[0:LEAVES_HERE]))
    run(0, own_end)
    wait_all(arrive_beside)
    take_values(low, LEAVES_HERE)
    take_values(high, 2 * LEAVES_HERE)
    if fresh:
        for side, source in enumerate((low, high)):
            for a in range(LEAVES_HERE):
                y = source[0:DIMS, cols(a)] * COORD_SCALE
                right[(side + 1) * LEAVES_HERE + a] = operands(y)[1].T
        beside = slice(LEAVES_HERE, 3 * LEAVES_HERE)
        leave.append(copies.start(right.at[beside], right_out.at[beside]))
    run(beside_at, beside_end)
    for a in range(LEAVES_HERE):
        part[:, cols(a)] = total[a, 0:16] + total[a, 16:32]
    leave.append(copies.start(part, part_out))
    wait_all(leave)


def near(fresh, ids, *inputs):
    right = shape((3 * LEAVES_HERE, LEAF, 256), BF)
    left = shape((LEAVES_HERE, 256, LEAF), BF)
    held = inputs if fresh else inputs[2:]
    return call(
        functools.partial(near_kernel, fresh),
        "near_first" if fresh else "near_second",
        [shape((RHS, WIDTH))] + ([right, left] if fresh else []),
        ids,
        inputs,
        scratch_for(held)
        + scratch_for([right, left])
        + [
            pltpu.VMEM((LEAVES_HERE, 32, LEAF), F),
            pltpu.VMEM((3 * LEAVES_HERE + 1, 3 * RHS, LEAF), BF),
            pltpu.VMEM((LEAF, LEAF), F),
            pltpu.VMEM((LEAF, LEAF), F),
            pltpu.VMEM((RHS, WIDTH), F),
            pltpu.SMEM((256,), jnp.int32),
            pltpu.SMEM((256,), jnp.int32),
        ],
        40 * 10**9,
        50 * LEAF * LEAF,
    )


def first_step(row_block):
    sums = columns(row_block)
    return sums[0:RHS] / sums[RHS : 2 * RHS]


def columns(row_block):
    return row_block.T[:, 0:1]


def down_kernel(fresh, *refs):
    ids_ref, message_in, blocks_in, up_top_in = refs[:4]
    if fresh:
        sources, (image_out, message_out, blocks_out) = refs[4:10], refs[10:13]
        refs = refs[13:]
    else:
        sources, (image_out, rows_out, sums_out) = refs[4:11], refs[11:14]
        refs = refs[14:]
    held, refs = refs[: len(sources)], refs[len(sources) :]
    weights, nodes, image, semaphores = refs[0], refs[1], refs[2], refs[-1]
    copies = Copies(semaphores)
    dev = ids_ref[0]
    node_four = dev // 2
    node_five = dev // 4
    threes = [ids_ref[AT_THREE + s] for s in range(2)]
    fours = [ids_ref[AT_FOUR + s] for s in range(TOP_SLOTS)]
    fives = [ids_ref[AT_FIVE + s] for s in range(TOP_SLOTS)]

    early = []
    if fresh:
        picks, made = refs[3], refs[4]
        early.append(copies.start(blocks_in, picks))
        blocks = made
    else:
        blocks, all_sums, row = refs[3], refs[4], refs[5]
        early.append(copies.start(blocks_in, blocks))
        arrive_sums = copies.start(message_in.at[:, RHS : RHS + 8, :], all_sums)
    for s, n in enumerate(fives):
        early.append(copies.start(message_in.at[pl.ds(4 * n, 4)], nodes.at[4 * s : 4 * s + 4]))
    for s, n in enumerate(fours):
        early.append(
            copies.start(message_in.at[pl.ds(2 * n, 2)], nodes.at[16 + 2 * s : 18 + 2 * s])
        )
    for s, n in enumerate(threes):
        early.append(copies.start(message_in.at[pl.ds(n, 1)], nodes.at[24 + s : 25 + s]))
    if fresh:
        early.append(copies.start(message_in.at[pl.ds(4 * node_five, 4)], nodes.at[26:30]))
    arrive = []
    for s, n in enumerate(fives):
        arrive.append(copies.start(up_top_in.at[pl.ds(2 * n, 2)], weights.at[3 * s : 3 * s + 2]))
        arrive.append(
            copies.start(
                up_top_in.at[pl.ds(NODES_FOUR + n, 1)], weights.at[3 * s + 2 : 3 * s + 3]
            )
        )
    for s, n in enumerate(fours + [node_four, NODES_FOUR + node_five]):
        arrive.append(copies.start(up_top_in.at[pl.ds(n, 1)], weights.at[12 + s : 13 + s]))
    arrive += [copies.start(source, target) for source, target in zip(sources, held)]
    interp, one, two, three, field, near_part = held[:6]
    wait_all(early)

    def pair_of(at, get):
        return jnp.concatenate([get(at), get(at + 1)], 1)

    if fresh:

        def base(at):
            return parts_of(nodes[at, RHS : RHS + DIMS, :])

        def four(at, n):
            return pick(pair_of(at, base), picks[pl.ds(n, 1), :])

        def five(at, n):
            both = jnp.concatenate([four(at, 2 * n), four(at + 2, 2 * n + 1)], 1)
            return pick(both, picks[pl.ds(NODES_FOUR + n, 1), :])

        def block(slot, own_left, other, differs):
            right = operands(joined(other))[1]
            made[slot] = jnp.exp2(mm(right.T, own_left)) * jnp.where(differs, 1.0, 0.0)

        own = operands(nodes[26 + dev % 4, RHS : RHS + DIMS, :])[0]
        for s, n in enumerate(threes):
            block(s, own, base(24 + s), n != dev)
        own = operands(joined(four(26 + 2 * (node_four % 2), node_four)))[0]
        for s, n in enumerate(fours):
            block(2 + s, own, four(16 + 2 * s, n), n != node_four)
        own = operands(joined(five(26, node_five)))[0]
        for s, n in enumerate(fives):
            block(6 + s, own, five(4 * s, n), n != node_five)
        leave = [copies.start(made, blocks_out)]
    else:
        leave = []

    def charge(at):
        return nodes[at, 0:RHS, :]

    field_three = jnp.zeros((RHS, RANK), F)
    for s in range(2):
        field_three = field_three + dot_split(charge(24 + s), blocks[s])
    wait_all(arrive)
    field_five = jnp.zeros((RHS, RANK), F)
    for s in range(TOP_SLOTS):
        lower = dot_split(pair_of(4 * s, charge), weights[3 * s])
        upper = dot_split(pair_of(4 * s + 2, charge), weights[3 * s + 1])
        q = dot_split(jnp.concatenate([lower, upper], 1), weights[3 * s + 2])
        field_five = field_five + dot_split(q, blocks[6 + s])
    field_four = jnp.zeros((RHS, RANK), F)
    for s in range(TOP_SLOTS):
        q = dot_split(pair_of(16 + 2 * s, charge), weights[12 + s])
        field_four = field_four + dot_split(q, blocks[2 + s])

    def half(at, side):
        return weights[at, pl.ds(pl.multiple_of(side * RANK, RANK), RANK), :]

    field_four = field_four + dot_split(field_five, half(17, node_four % 2), NT)
    level = [field_three + dot_split(field_four, half(16, dev % 2), NT)]
    for ref in (three, two, one):
        spread = [dot_split(h, ref[n], NT) for n, h in enumerate(level)]
        level = [s[:, side * RANK : (side + 1) * RANK] for s in spread for side in range(2)]
    for a in range(LEAVES_HERE):
        far = dot_split(level[a], interp[a], NT)
        image[:, cols(a)] = RIDGE_TERM * field[:, cols(a)] + near_part[:, cols(a)] + far
    leave.append(copies.start(image, image_out))
    if fresh:
        message = refs[5]
        charges = climb(image, interp, (one, two, three))
        sums = row_of_sums([field[...] * field[...], field[...] * image[...]])
        block = jnp.concatenate([charges, sums, jnp.zeros((7, RANK), F)], 0)
        message[...] = jnp.broadcast_to(block[None], message.shape)
        leave += send_copies(copies, message, message_out)
    else:
        wait_all([arrive_sums])
        base_field = held[6]
        all_sums[0] = jnp.sum(all_sums[...], 0)
        step = first_step(all_sums[0])
        residual = base_field[...] - step * field[...]
        moved = field[...] - step * image[...]
        sums = row_of_sums(
            [residual * residual, residual * moved, base_field[...] * moved, residual * field[...]]
        )
        row[...] = jnp.broadcast_to(sums, row.shape)
        leave.append(copies.start(row, rows_out))
        leave.append(copies.start(all_sums.at[0], sums_out))
    wait_all(leave)


def down(fresh, ids, message, blocks, up_top, *sources):
    made = shape((2 + 2 * TOP_SLOTS, RANK, RANK))
    rows = message.shape[1]
    scratch = scratch_for(sources) + [
        pltpu.VMEM((18, 2 * RANK, RANK), F),
        pltpu.VMEM((30, rows, RANK), F),
        pltpu.VMEM((RHS, WIDTH), F),
    ]
    if fresh:
        out = [shape((RHS, WIDTH)), shape((DEVICES, RHS + 8, RANK)), made]
        scratch += [
            pltpu.VMEM(blocks.shape, jnp.int32),
            pltpu.VMEM(made.shape, F),
            pltpu.VMEM((16, RHS + 8, RANK), F),
        ]
    else:
        out = [shape((RHS, WIDTH)), shape((DEVICES, RANK)), shape((8, RANK))]
        scratch += [
            pltpu.VMEM(made.shape, F),
            pltpu.VMEM((DEVICES, 8, RANK), F),
            pltpu.VMEM((DEVICES, RANK), F),
        ]
    return call(
        functools.partial(down_kernel, fresh),
        "down_first" if fresh else "down_second",
        out,
        ids,
        [message, blocks, up_top, *sources],
        scratch,
        10**9,
    )


def finish_kernel(*refs):
    inputs, (solution_out, residual_out) = refs[:5], refs[5:7]
    held, (solution_held, residual_held, semaphores) = refs[7:12], refs[12:]
    copies = Copies(semaphores)
    wait_all([copies.start(source, target) for source, target in zip(inputs, held)])
    rows_ref, sums_ref, base_ref, image_ref, second_ref = held
    before = columns(sums_ref[...])
    rows = jnp.sum(rows_ref[...], 0, keepdims=True)
    after = columns(jnp.broadcast_to(rows, (8, RANK)))
    norm, curvature = before[0:RHS], before[RHS : 2 * RHS]
    step = norm / curvature
    norm_next, rm, bm, ri = [after[q * RHS : (q + 1) * RHS] for q in range(4)]
    turn = norm_next / norm
    second_curvature = rm + turn * (bm + ri + turn * curvature)
    second_step = norm_next / second_curvature
    base = base_ref[...]
    image = image_ref[...]
    residual = base - step * image
    direction = residual + turn * base
    moved = image - step * second_ref[...] + turn * image
    solution_held[...] = step * base + second_step * direction
    leave = [copies.start(solution_held, solution_out)]
    residual_held[...] = residual - second_step * moved
    leave.append(copies.start(residual_held, residual_out))
    wait_all(leave)


def finish(*inputs):
    out = [shape((RHS, WIDTH))] * 2
    return call(finish_kernel, "finish", out, None, inputs, scratch_for(inputs) + scratch_for(out), 10**6)


def beside(value):
    forward = [(i, i + 1) for i in range(DEVICES - 1)]
    backward = [(target, source) for source, target in forward]
    return lax.ppermute(value, AXES, forward), lax.ppermute(value, AXES, backward)


def everyone(copies):
    return lax.all_to_all(copies, AXES, 0, 0, tiled=True)


def local(
    points,
    right_side,
    interp,
    leaf_skel,
    up_one,
    skel_one,
    up_two,
    skel_two,
    up_three,
    skel_three,
    up_top,
    skel_top,
    near_list,
    far_three,
    far_top,
):
    device = lax.axis_index(AXES).astype(jnp.int32)
    fours = lax.dynamic_index_in_dim(far_top, device // 2, 0, False)
    fives = lax.dynamic_index_in_dim(far_top, NODES_FOUR + device // 4, 0, False) - NODES_FOUR
    ids = jnp.concatenate(
        [device[None], far_three[0], fours, fives, jnp.zeros((5,), jnp.int32), near_list.reshape(-1)]
    )
    weights = (interp, up_one, up_two, up_three)
    message, halo = first(
        points, right_side, weights, (leaf_skel, skel_one, skel_two, skel_three)
    )
    low, high = beside(halo)
    message = everyone(message)
    part, right, left = near(True, ids, points, right_side, low, high)
    image, own_message, blocks = down(
        True, ids, message, skel_top, up_top, *weights, right_side, part
    )
    low, high = beside(image)
    message = everyone(own_message)
    (part,) = near(False, ids, right, left, image, low, high)
    second, rows, sums = down(
        False, ids, message, blocks, up_top, *weights, image, part, right_side
    )
    return tuple(finish(everyone(rows), sums, right_side, image, second))


def solution(mesh):
    both = ("leaf", "sub")
    placed = (
        P(None, both),
        P(None, both),
        P(both, None, None),
        P(both, None),
        P(both, None, None),
        P(both, None),
        P(both, None, None),
        P(both, None),
        P(both, None, None),
        P(both, None),
        P(),
        P(),
        P(both, None),
        P(both, None),
        P(),
    )
    return jax.shard_map(
        local,
        mesh=mesh,
        in_specs=placed,
        out_specs=(P(None, both), P(None, both)),
        check_vma=False,
    )
```

time: 196 us -> 163 us (0.83)
  local copies, waits for them, and re-layouts: 33.4 us -> 4.41 us
  starting transfers between devices: 51.5 us -> 34.7 us
  blocking collectives: 17 us -> 25 us
  Pallas kernels: 85 us -> 87.2 us
    unnamed x79 -> x14, local copies, waits for them, and re-layouts: 31.7 us -> 3.66 us
    all_to_all x3 -> x2, starting transfers between devices: 34.1 us -> 22.2 us  [everyone(): return lax.all_to_all(copies, AXES, 0, 0, tiled=True)]
    all_to_all x1, blocking collectives: 17 us -> 25 us  [everyone(): return lax.all_to_all(copies, AXES, 0, 0, tiled=True)]
    ppermute x3 -> x2, starting transfers between devices: 10.5 us -> 6.09 us  [beside(): lax.ppermute(value, AXES, forward)]
    pallas_call x12 -> x6, Pallas kernels: 85 us -> 87.2 us  [call(): pl.pallas_call(kernel, out_shape=out, in_specs=([SMEM] if ids is not None...]
    all_to_all x3 -> x2, waiting for transfers between devices: 9.19 us -> 10.4 us  [everyone(): return lax.all_to_all(copies, AXES, 0, 0, tiled=True)]
    ppermute x3 -> x2, starting transfers between devices: 6.95 us -> 6.33 us  [beside(): lax.ppermute(value, AXES, backward)]
  transfers between devices with their start and end apart: 9 -> 6, of which waited for: 2 -> 1; matrix products, arithmetic and copies ran while one was open for 1% -> 1% of each run, Pallas kernels for 35% -> 37%
where the time goes in v2:
time: 163 us
  Pallas kernels  87.2 us (53%)
  starting transfers between devices  34.7 us (21%)
  blocking collectives  25 us (15%)
  waiting for transfers between devices  10.4 us (6%)
  local copies, waits for them, and re-layouts  4.41 us (3%)
    pallas_call x6, Pallas kernels, call(): pl.pallas_call(kernel, out_shape=out, in_specs=([SMEM] if ids is not None...  87.2 us
    all_to_all x1, blocking collectives, everyone(): return lax.all_to_all(copies, AXES, 0, 0, tiled=True)  25 us
    all_to_all x2, starting transfers between devices, everyone(): return lax.all_to_all(copies, AXES, 0, 0, tiled=True)  22.2 us
    all_to_all x2, waiting for transfers between devices, everyone(): return lax.all_to_all(copies, AXES, 0, 0, tiled=True)  10.4 us
    ppermute x2, starting transfers between devices, beside(): lax.ppermute(value, AXES, backward)  6.33 us
    ppermute x2, starting transfers between devices, beside(): lax.ppermute(value, AXES, forward)  6.09 us
    unnamed x14, local copies, waits for them, and re-layouts  3.66 us
  transfers between devices with their start and end apart: 6, of which 1 were waited for; matrix products, arithmetic and copies ran while one was open for 1% of the time, Pallas kernels for 37%

profile of v2, /device:TPU:1, one launch (start us, length us, event | category | flops | bytes accessed | tf_op | source)
XLA Modules:
  0.0 162.9 jit_solution(1961355338112048136)
XLA Ops:
  0.6 5.8 %first_up.1 = (f32[128,48,128]{2,1,0:T(8,128)}, f32[48,4096]{1,0:T(8,128)}) custom-call(f32[32,4096]{1,0:T(8,128)} %refs_1_.3, f32[16,4096]{1,0:T(8,128)} %refs_2_.7, f32[8,512,128]{2,1,0:T(8,128)} %refs_4_.5, f32[4,256,128]{2,1,0:T(8,128)} %refs_5_.5, f32[2,256,128]{2,1,0:T(8,128)} %refs_6_.5, f32[1,256,128]{2,1,0:T(8,128)} %refs_7_.5, s32[8,128]{1,0:T(8,128)} %refs_6_.3, ...), custom_call_target="tpu_custom_call" | custom-call | flops 1000000000 | bytes 6291456 | tf_op jit(solution)/shard_map/first_up/pallas_call | solution.py:111
  6.5 3.3 %collective-permute-start.1 = (f32[48,4096]{1,0:T(8,128)}, f32[48,4096]{1,0:T(8,128)}, u32[]{:S(2)}, u32[]{:S(2)}) collective-permute-start(f32[48,4096]{1,0:T(8,128)} %get-tuple-element.14), channel_id=1, source_target_pairs={{1,0},{2,1},{3,2},{4,3},{5,4},{6,5},{7,6},{8,7},{9,8},{10,9},{11,1... | collective-permute-start | bytes 2359304 | tf_op jit(solution)/shard_map/ppermute | solution.py:557
  9.8 3.5 %collective-permute-start = (f32[48,4096]{1,0:T(8,128)}, f32[48,4096]{1,0:T(8,128)}, u32[]{:S(2)}, u32[]{:S(2)}) collective-permute-start(f32[48,4096]{1,0:T(8,128)} %get-tuple-element.14), channel_id=1, source_target_pairs={{0,1},{1,2},{2,3},{3,4},{4,5},{5,6},{6,7},{7,8},{8,9},{9,10},{10,1... | collective-permute-start | bytes 2359304 | tf_op jit(solution)/shard_map/ppermute | solution.py:557
  13.3 0.0 copy-start.3
  13.4 0.0 copy-start.2
  13.4 0.0 copy-start.4
  13.4 13.7 %all-to-all-start = ((f32[128,48,128]{2,1,0:T(8,128)}), f32[128,48,128]{2,1,0:T(8,128)S(1)}, u32[]{:S(2)}, u32[]{:S(2)}) async-start(f32[128,48,128]{2,1,0:T(8,128)} %get-tuple-element.13), calls=%async_computation | async-start | bytes 6291456 | tf_op jit(solution)/shard_map/all_to_all | solution.py:561
  27.1 0.0 copy-done.3
  27.1 0.1 reshape.11
  27.2 0.0 copy-done.2
  27.2 0.2 add_reduce_fusion
  27.4 0.0 copy-done.4
  27.4 0.7 concatenate.3.refs_0_
  28.1 0.0 collective-permute-done.1.refs_4_
  28.1 0.0 collective-permute-done.refs_3_
  28.1 30.4 %near_first.1 = (f32[16,4096]{1,0:T(8,128)}, bf16[24,512,256]{2,1,0:T(8,128)(2,1)}, bf16[8,256,512]{2,1,0:T(8,128)(2,1)}) custom-call(s32[112]{0:T(128)} %concatenate.3.refs_0_, f32[32,4096]{1,0:T(8,128)} %refs_1_.3, f32[16,4096]{1,0:T(8,128)} %refs_2_.7, f32[48,4096]{1,0:T(8,128)} %collective-permute-done.refs_3_, f32[48,4096]{1,0:T(8,128)} %collective-permute-done.1.refs_4_), custom_call_target="tpu_custom_call" | custom-call | flops 40000000000 | bytes 6291456 | tf_op jit(solution)/shard_map/near_first/pallas_call | solution.py:111
  58.5 10.4 %all-to-all-done.refs_1_ = f32[128,48,128]{2,1,0:T(8,128)S(1)} async-done(((f32[128,48,128]{2,1,0:T(8,128)}), f32[128,48,128]{2,1,0:T(8,128)S(1)}, u32[]{:S(2)}, u32[]{:S(2)}) %all-to-all-start) | async-done | bytes 3145760 | tf_op jit(solution)/shard_map/all_to_all | solution.py:561
  68.9 0.0 copy-start
  68.9 1.7 %copy-done = f32[128,48,128]{2,1,0:T(8,128)} copy-done((f32[128,48,128]{2,1,0:T(8,128)}, f32[128,48,128]{2,1,0:T(8,128)S(1)}, u32[]{:S(2)}) %copy-start) | copy-done | bytes 3145752
  70.6 9.7 %down_first.1 = (f32[16,4096]{1,0:T(8,128)}, f32[128,24,128]{2,1,0:T(8,128)}, f32[10,128,128]{2,1,0:T(8,128)}) custom-call(s32[112]{0:T(128)} %concatenate.3.refs_0_, f32[128,48,128]{2,1,0:T(8,128)} %copy-done, s32[96,128]{1,0:T(8,128)} %refs_2_.6, f32[96,256,128]{2,1,0:T(8,128)} %refs_3_.5, f32[8,512,128]{2,1,0:T(8,128)} %refs_4_.5, ...), custom_call_target="tpu_custom_call" | custom-call | flops 1000000000 | bytes 6291456 | tf_op jit(solution)/shard_map/down_first/pallas_call | solution.py:111
  80.3 3.0 %collective-permute-start.3 = (f32[16,4096]{1,0:T(8,128)}, f32[16,4096]{1,0:T(8,128)S(1)}, u32[]{:S(2)}, u32[]{:S(2)}) collective-permute-start(f32[16,4096]{1,0:T(8,128)} %get-tuple-element.18.refs_3_.refs_8_), channel_id=1, source_target_pairs={{1,0},{2,1},{3,2},{4,3},{5,4},{6,5},{7,6},{8,7},{9,8},{10,9},{11,1... | collective-permute-start | bytes 786440 | tf_op jit(solution)/shard_map/ppermute | solution.py:557
  83.4 2.6 %collective-permute-start.2 = (f32[16,4096]{1,0:T(8,128)}, f32[16,4096]{1,0:T(8,128)S(1)}, u32[]{:S(2)}, u32[]{:S(2)}) collective-permute-start(f32[16,4096]{1,0:T(8,128)} %get-tuple-element.18.refs_3_.refs_8_), channel_id=1, source_target_pairs={{0,1},{1,2},{2,3},{3,4},{4,5},{5,6},{6,7},{7,8},{8,9},{9,10},{10,1... | collective-permute-start | bytes 786440 | tf_op jit(solution)/shard_map/ppermute | solution.py:557
  85.9 8.6 %all-to-all-start.1 = ((f32[128,24,128]{2,1,0:T(8,128)}), f32[128,24,128]{2,1,0:T(8,128)S(1)}, u32[]{:S(2)}, u32[]{:S(2)}) async-start(f32[128,24,128]{2,1,0:T(8,128)} %get-tuple-element.16), calls=%async_computation.1 | async-start | bytes 3145728 | tf_op jit(solution)/shard_map/all_to_all | solution.py:561
  94.5 0.0 collective-permute-done.3.refs_5_
  94.5 0.0 copy-start.5
  94.5 0.0 collective-permute-done.2.refs_4_
  94.5 0.0 copy-start.6
  94.5 0.7 copy-done.5
  95.2 0.1 copy-done.6
  95.3 30.0 %near_second.1.refs_9_ = f32[16,4096]{1,0:T(8,128)} custom-call(s32[112]{0:T(128)} %concatenate.3.refs_0_, bf16[24,512,256]{2,1,0:T(8,128)(2,1)} %get-tuple-element.19.refs_1_, bf16[8,256,512]{2,1,0:T(8,128)(2,1)} %get-tuple-element.20.refs_2_, f32[16,4096]{1,0:T(8,128)} %get-tuple-element.18.refs_3_.refs_8_, f32[16,4096]{1,0:T(8,128)} %copy-done.6, ...), custom_call_target="tpu_custom_call" | custom-call | flops 40000000000 | bytes 6291456 | tf_op jit(solution)/shard_map/near_second/pallas_call | solution.py:111
  125.3 0.0 all-to-all-done.1.refs_1_
  125.3 0.0 copy-start.1
  125.4 1.2 copy-done.1
  126.5 8.5 %down_second.1 = (f32[16,4096]{1,0:T(8,128)}, f32[128,128]{1,0:T(8,128)}, f32[8,128]{1,0:T(8,128)}) custom-call(s32[112]{0:T(128)} %concatenate.3.refs_0_, f32[128,24,128]{2,1,0:T(8,128)} %copy-done.1, f32[10,128,128]{2,1,0:T(8,128)} %get-tuple-element.17.refs_2_, f32[96,256,128]{2,1,0:T(8,128)} %refs_3_.5, f32[8,512,128]{2,1,0:T(8,128)} %refs_4_.5, ...), custom_call_target="tpu_custom_call" | custom-call | flops 1000000000 | bytes 6291456 | tf_op jit(solution)/shard_map/down_second/pallas_call | solution.py:111
  135.1 25.0 %all_to_all.21 = f32[128,1,128]{2,1,0:T(1,128)} all-to-all(f32[128,1,128]{2,1,0:T(1,128)} %bitcast.7), channel_id=1, replica_groups=mesh['leaf'=16,'sub'=8] {'leaf','sub'}, dimensions={0} | all-to-all | bytes 131072 | tf_op jit(solution)/shard_map/all_to_all | solution.py:561
  160.1 2.7 %finish.1 = (f32[16,4096]{1,0:T(8,128)}, f32[16,4096]{1,0:T(8,128)}) custom-call(f32[128,128]{1,0:T(8,128)} %bitcast.6, f32[8,128]{1,0:T(8,128)} %get-tuple-element.22.refs_1_, f32[16,4096]{1,0:T(8,128)} %refs_2_.7, f32[16,4096]{1,0:T(8,128)} %get-tuple-element.18.refs_3_.refs_8_, f32[16,4096]{1,0:T(8,128)} %get-tuple-element.23.refs_4_), custom_call_target="tpu_custom_call" | custom-call | flops 1000000 | bytes 6291456 | tf_op jit(solution)/shard_map/finish/pallas_call | solution.py:111
  (1 shorter events, 0.0 us)
Async XLA Ops:
  6.5 21.6 %collective-permute-start.1 = (f32[48,4096]{1,0:T(8,128)}, f32[48,4096]{1,0:T(8,128)}, u32[]{:S(2)}, u32[]{:S(2)}) collective-permute-start(f32[48,4096]{1,0:T(8,128)} %get-tuple-element.14), channel_id=1, source_target_pairs={{1,0},{2,1},{3,2},{4,3},{5,4},{6,5},{7,6},{8,7},{9,8},{10,9},{11,1... | collective-permute-start | bytes 2359304 | tf_op jit(solution)/shard_map/ppermute | solution.py:557
  9.8 18.3 %collective-permute-start = (f32[48,4096]{1,0:T(8,128)}, f32[48,4096]{1,0:T(8,128)}, u32[]{:S(2)}, u32[]{:S(2)}) collective-permute-start(f32[48,4096]{1,0:T(8,128)} %get-tuple-element.14), channel_id=1, source_target_pairs={{0,1},{1,2},{2,3},{3,4},{4,5},{5,6},{6,7},{7,8},{8,9},{9,10},{10,1... | collective-permute-start | bytes 2359304 | tf_op jit(solution)/shard_map/ppermute | solution.py:557
  13.3 13.8 %copy-start.3 = (s32[8,12]{1,0:T(8,128)S(1)}, s32[8,12]{1,0:T(8,128)}, u32[]{:S(2)}) copy-start(s32[8,12]{1,0:T(8,128)} %param.27) | copy-start | bytes 1156
  13.4 13.8 %copy-start.2 = (s32[96,4]{0,1:T(4,128)S(1)}, s32[96,4]{0,1:T(4,128)}, u32[]{:S(2)}) copy-start(s32[96,4]{0,1:T(4,128)} %param.29) | copy-start | bytes 4612
  13.4 14.1 %copy-start.4 = (s32[1,2]{1,0:T(1,128)S(1)}, s32[1,2]{1,0:T(1,128)}, u32[]{:S(2)}) copy-start(s32[1,2]{1,0:T(1,128)} %param.28) | copy-start | bytes 28
  13.4 55.5 %all-to-all-start = ((f32[128,48,128]{2,1,0:T(8,128)}), f32[128,48,128]{2,1,0:T(8,128)S(1)}, u32[]{:S(2)}, u32[]{:S(2)}) async-start(f32[128,48,128]{2,1,0:T(8,128)} %get-tuple-element.13), calls=%async_computation | async-start | bytes 6291456 | tf_op jit(solution)/shard_map/all_to_all | solution.py:561
  68.9 1.7 %copy-start = (f32[128,48,128]{2,1,0:T(8,128)}, f32[128,48,128]{2,1,0:T(8,128)S(1)}, u32[]{:S(2)}) copy-start(f32[128,48,128]{2,1,0:T(8,128)S(1)} %all-to-all-done.refs_1_) | copy-start | bytes 9437188
  80.3 14.1 %collective-permute-start.3 = (f32[16,4096]{1,0:T(8,128)}, f32[16,4096]{1,0:T(8,128)S(1)}, u32[]{:S(2)}, u32[]{:S(2)}) collective-permute-start(f32[16,4096]{1,0:T(8,128)} %get-tuple-element.18.refs_3_.refs_8_), channel_id=1, source_target_pairs={{1,0},{2,1},{3,2},{4,3},{5,4},{6,5},{7,6},{8,7},{9,8},{10,9},{11,1... | collective-permute-start | bytes 786440 | tf_op jit(solution)/shard_map/ppermute | solution.py:557
  83.4 11.2 %collective-permute-start.2 = (f32[16,4096]{1,0:T(8,128)}, f32[16,4096]{1,0:T(8,128)S(1)}, u32[]{:S(2)}, u32[]{:S(2)}) collective-permute-start(f32[16,4096]{1,0:T(8,128)} %get-tuple-element.18.refs_3_.refs_8_), channel_id=1, source_target_pairs={{0,1},{1,2},{2,3},{3,4},{4,5},{5,6},{6,7},{7,8},{8,9},{9,10},{10,1... | collective-permute-start | bytes 786440 | tf_op jit(solution)/shard_map/ppermute | solution.py:557
  85.9 39.4 %all-to-all-start.1 = ((f32[128,24,128]{2,1,0:T(8,128)}), f32[128,24,128]{2,1,0:T(8,128)S(1)}, u32[]{:S(2)}, u32[]{:S(2)}) async-start(f32[128,24,128]{2,1,0:T(8,128)} %get-tuple-element.16), calls=%async_computation.1 | async-start | bytes 3145728 | tf_op jit(solution)/shard_map/all_to_all | solution.py:561
  94.5 0.7 copy-start.5
  94.5 0.8 copy-start.6
  125.3 1.2 copy-start.1

commit v3 on v2

--- a/solution.py
+++ b/solution.py
@@ -114,7 +114,7 @@
         in_specs=([SMEM] if ids is not None else []) + [ANY] * len(inputs),
         out_specs=[ANY] * len(out),
         scratch_shapes=scratch + [pltpu.SemaphoreType.DMA((48,))],
-        compiler_params=pltpu.CompilerParams(vmem_limit_bytes=56 << 20),
+        compiler_params=pltpu.CompilerParams(vmem_limit_bytes=63 << 20),
         cost_estimate=pl.CostEstimate(
             flops=flops, bytes_accessed=6 << 20, transcendentals=transcendentals
         ),
@@ -204,11 +204,11 @@
 
 def near_kernel(fresh, *refs):
     if fresh:
-        ids_ref, points_in, field_in, low_in, high_in, part_out, right_out, left_out = refs[:8]
-        points, field, low, high = refs[8:12]
+        ids_ref, points_in, field_in, partner_in, other_in, part_out, right_out, left_out = refs[:8]
+        points, field, partner, other = refs[8:12]
     else:
-        ids_ref, right_in, left_in, field_in, low_in, high_in, part_out = refs[:7]
-        field, low, high = refs[7:10]
+        ids_ref, right_in, left_in, field_in, partner_in, other_in, part_out = refs[:7]
+        field, partner, other = refs[7:10]
     right, left, total, values, ea, eb, part, targets, origins, semaphores = refs[-10:]
     copies = Copies(semaphores)
     arrive_field = copies.start(field_in, field)
@@ -219,7 +219,7 @@
             copies.start(left_in, left),
             copies.start(right_in.at[0:LEAVES_HERE], right.at[0:LEAVES_HERE]),
         ]
-    arrive_beside = [copies.start(low_in, low), copies.start(high_in, high)]
+    arrive_beside = [copies.start(partner_in, partner), copies.start(other_in, other)]
     if not fresh:
         arrive_beside.append(
             copies.start(
@@ -229,6 +229,9 @@
     first = ids_ref[0] * LEAVES_HERE
     empty = 3 * LEAVES_HERE
     beside_at = 128
+    odd = ids_ref[0] % 2 == 1
+    shift_low = jnp.where(odd, 2 * LEAVES_HERE, 3 * LEAVES_HERE)
+    shift_high = jnp.where(odd, LEAVES_HERE, 0)
 
     def collect(a, counts):
         n, m = counts
@@ -242,7 +245,7 @@
             origins[n] = place
             n = n + (inside & (place != a)).astype(jnp.int32)
             targets[m] = a
-            origins[m] = jnp.where(place < 0, place + 2 * LEAVES_HERE, place + LEAVES_HERE)
+            origins[m] = place + jnp.where(place < 0, shift_low, shift_high)
             m = m + jnp.logical_not(inside).astype(jnp.int32)
         return n, m
 
@@ -250,7 +253,7 @@
         0, LEAVES_HERE, collect, (jnp.int32(0), jnp.int32(beside_at))
     )
     for end in (own_end, beside_end):
-        for extra in range(3):
+        for extra in range(4):
             targets[end + extra] = 0
             origins[end + extra] = empty
 
@@ -274,15 +277,25 @@
     def run(start, end):
         ea[...] = exponent(start)
 
-        def pair(p, carry):
-            t = start + 2 * p
+        def pair(t):
             eb[...] = exponent(t + 1)
             add(t, ea[...])
             ea[...] = exponent(t + 2)
             add(t + 1, eb[...])
+
+        def four(p, carry):
+            pair(start + 4 * p)
+            pair(start + 4 * p + 2)
             return carry
 
-        lax.fori_loop(0, (end - start + 1) // 2, pair, 0)
+        def two(p, carry):
+            pair(middle + 2 * p)
+            return carry
+
+        fours = (end - start) // 4
+        middle = start + 4 * fours
+        lax.fori_loop(0, fours, four, 0)
+        lax.fori_loop(0, (end - middle + 1) // 2, two, 0)
 
     total[...] = jnp.zeros_like(total)
     values[empty] = jnp.zeros((3 * RHS, LEAF), BF)
@@ -299,10 +312,10 @@
         leave.append(copies.start(right.at[0:LEAVES_HERE], right_out.at[0:LEAVES_HERE]))
     run(0, own_end)
     wait_all(arrive_beside)
-    take_values(low, LEAVES_HERE)
-    take_values(high, 2 * LEAVES_HERE)
-    if fresh:
-        for side, source in enumerate((low, high)):
+    take_values(partner, LEAVES_HERE)
+    take_values(other, 2 * LEAVES_HERE)
+    if fresh:
+        for side, source in enumerate((partner, other)):
             for a in range(LEAVES_HERE):
                 y = source[0:DIMS, cols(a)] * COORD_SCALE
                 right[(side + 1) * LEAVES_HERE + a] = operands(y)[1].T
@@ -552,9 +565,10 @@
 
 
 def beside(value):
-    forward = [(i, i + 1) for i in range(DEVICES - 1)]
-    backward = [(target, source) for source, target in forward]
-    return lax.ppermute(value, AXES, forward), lax.ppermute(value, AXES, backward)
+    partner = [(i, i ^ 1) for i in range(DEVICES)]
+    forward = [(i, i + 1) for i in range(1, DEVICES - 1, 2)]
+    other = forward + [(target, source) for source, target in forward]
+    return lax.ppermute(value, AXES, partner), lax.ppermute(value, AXES, other)
 
 
 def everyone(copies):
@@ -588,15 +602,15 @@
     message, halo = first(
         points, right_side, weights, (leaf_skel, skel_one, skel_two, skel_three)
     )
-    low, high = beside(halo)
+    partner, other = beside(halo)
     message = everyone(message)
-    part, right, left = near(True, ids, points, right_side, low, high)
+    part, right, left = near(True, ids, points, right_side, partner, other)
     image, own_message, blocks = down(
         True, ids, message, skel_top, up_top, *weights, right_side, part
     )
-    low, high = beside(image)
+    partner, other = beside(image)
     message = everyone(own_message)
-    (part,) = near(False, ids, right, left, image, low, high)
+    (part,) = near(False, ids, right, left, image, partner, other)
     second, rows, sums = down(
         False, ids, message, blocks, up_top, *weights, image, part, right_side
     )

time: 163 us -> 150 us (0.920); the launches traced: 163 us -> 148 us
  Pallas kernels: 87.2 us -> 57.7 us
  waiting for transfers between devices: 10.4 us -> 32.5 us
  starting transfers between devices: 34.7 us -> 27.7 us
  local copies, waits for them, and re-layouts: 4.41 us -> 2.44 us
    pallas_call x6, Pallas kernels: 87.2 us -> 57.7 us  [call(): pl.pallas_call(kernel, out_shape=out, in_specs=([SMEM] if ids is not None...]
    all_to_all x2, waiting for transfers between devices: 10.4 us -> 32.5 us  [everyone(): return lax.all_to_all(copies, AXES, 0, 0, tiled=True)]
    ppermute x4, starting transfers between devices: 12.4 us -> 7.75 us  [the longest x2 7.58 us: beside(): lax.ppermute(value, AXES, other)]
    all_to_all x2, starting transfers between devices: 22.2 us -> 19.9 us  [everyone(): return lax.all_to_all(copies, AXES, 0, 0, tiled=True)]
    unnamed x14 -> x12, local copies, waits for them, and re-layouts: 3.66 us -> 1.69 us
  transfers between devices with their start and end apart: 6 -> 6, of which waited for: 1 -> 2; matrix products, arithmetic and copies ran while one was open for 1% -> 1% of each run, Pallas kernels for 37% -> 21%
where the time goes in v3:
time: 150 us; the launch traced here: 148 us
  Pallas kernels  57.7 us (38%)
  waiting for transfers between devices  32.5 us (22%)
  starting transfers between devices  27.7 us (18%)
  blocking collectives  26 us (17%)
  local copies, waits for them, and re-layouts  2.44 us (2%)
    pallas_call x6, Pallas kernels, call(): pl.pallas_call(kernel, out_shape=out, in_specs=([SMEM] if ids is not None...  57.7 us
    all_to_all x2, waiting for transfers between devices, everyone(): return lax.all_to_all(copies, AXES, 0, 0, tiled=True)  32.5 us
    all_to_all x1, blocking collectives, everyone(): return lax.all_to_all(copies, AXES, 0, 0, tiled=True)  26 us
    all_to_all x2, starting transfers between devices, everyone(): return lax.all_to_all(copies, AXES, 0, 0, tiled=True)  19.9 us
    ppermute x2, starting transfers between devices, beside(): lax.ppermute(value, AXES, other)  7.58 us
  transfers between devices with their start and end apart: 6, of which 2 were waited for; matrix products, arithmetic and copies ran while one was open for 1% of the time, Pallas kernels for 21%

profile of v3, /device:TPU:1, one launch (start us, length us, event | category | flops | bytes accessed | tf_op | source)
XLA Modules:
  0.0 147.5 jit_solution(16872343089293428110)
XLA Ops:
  0.6 5.8 %first_up.1 = (f32[128,48,128]{2,1,0:T(8,128)}, f32[48,4096]{1,0:T(8,128)}) custom-call(f32[32,4096]{1,0:T(8,128)} %refs_1_.3, f32[16,4096]{1,0:T(8,128)} %refs_2_.7, f32[8,512,128]{2,1,0:T(8,128)} %refs_4_.5, f32[4,256,128]{2,1,0:T(8,128)} %refs_5_.5, f32[2,256,128]{2,1,0:T(8,128)} %refs_6_.5, f32[1,256,128]{2,1,0:T(8,128)} %refs_7_.5, s32[8,128]{1,0:T(8,128)} %refs_6_.3, ...), custom_call_target="tpu_custom_call" | custom-call | flops 1000000000 | bytes 6291456 | tf_op jit(solution)/shard_map/first_up/pallas_call | solution.py:111
  6.4 4.9 %collective-permute-start.1 = (f32[48,4096]{1,0:T(8,128)}, f32[48,4096]{1,0:T(8,128)S(1)}, u32[]{:S(2)}, u32[]{:S(2)}) collective-permute-start(f32[48,4096]{1,0:T(8,128)} %get-tuple-element.14), channel_id=1, source_target_pairs={{1,2},{3,4},{5,6},{7,8},{9,10},{11,12},{13,14},{15,16},{17,18},{19... | collective-permute-start | bytes 2359304 | tf_op jit(solution)/shard_map/ppermute | solution.py:571
  11.4 0.1 collective-permute-start
  11.4 0.0 copy-start.1
  11.5 0.0 copy-start
  11.5 0.0 copy-start.2
  11.5 10.4 %all-to-all-start = ((f32[128,48,128]{2,1,0:T(8,128)}), f32[128,48,128]{2,1,0:T(8,128)}, u32[]{:S(2)}, u32[]{:S(2)}) async-start(f32[128,48,128]{2,1,0:T(8,128)} %get-tuple-element.13), calls=%async_computation | async-start | bytes 6291456 | tf_op jit(solution)/shard_map/all_to_all | solution.py:575
  21.9 0.0 copy-done.1
  21.9 0.1 reshape.11
  22.0 0.0 copy-done
  22.0 0.2 add_reduce_fusion
  22.2 0.0 copy-done.2
  22.3 0.7 concatenate.3.refs_0_
  22.9 0.0 collective-permute-done.1.refs_4_
  22.9 0.0 copy-start.3
  22.9 0.0 collective-permute-done.refs_3_
  22.9 0.9 copy-done.3
  23.8 15.8 %near_first.1 = (f32[16,4096]{1,0:T(8,128)}, bf16[24,512,256]{2,1,0:T(8,128)(2,1)}, bf16[8,256,512]{2,1,0:T(8,128)(2,1)}) custom-call(s32[112]{0:T(128)} %concatenate.3.refs_0_, f32[32,4096]{1,0:T(8,128)} %refs_1_.3, f32[16,4096]{1,0:T(8,128)} %refs_2_.7, f32[48,4096]{1,0:T(8,128)} %collective-permute-done.refs_3_, f32[48,4096]{1,0:T(8,128)} %copy-done.3), custom_call_target="tpu_custom_call" | custom-call | flops 40000000000 | bytes 6291456 | tf_op jit(solution)/shard_map/near_first/pallas_call | solution.py:111
  39.6 23.8 %all-to-all-done.refs_1_ = f32[128,48,128]{2,1,0:T(8,128)} async-done(((f32[128,48,128]{2,1,0:T(8,128)}), f32[128,48,128]{2,1,0:T(8,128)}, u32[]{:S(2)}, u32[]{:S(2)}) %all-to-all-start) | async-done | bytes 3145760 | tf_op jit(solution)/shard_map/all_to_all | solution.py:575
  63.4 9.8 %down_first.1 = (f32[16,4096]{1,0:T(8,128)}, f32[128,24,128]{2,1,0:T(8,128)}, f32[10,128,128]{2,1,0:T(8,128)}) custom-call(s32[112]{0:T(128)} %concatenate.3.refs_0_, f32[128,48,128]{2,1,0:T(8,128)} %all-to-all-done.refs_1_, s32[96,128]{1,0:T(8,128)} %refs_2_.6, f32[96,256,128]{2,1,0:T(8,128)} %refs_3_.5, f32[8,512,128]{2,1,0:T(8,128)} %refs_4_.5, ...), custom_call_target="tpu_custom_call" | custom-call | flops 1000000000 | bytes 6291456 | tf_op jit(solution)/shard_map/down_first/pallas_call | solution.py:111
  73.2 2.6 %collective-permute-start.3 = (f32[16,4096]{1,0:T(8,128)}, f32[16,4096]{1,0:T(8,128)S(1)}, u32[]{:S(2)}, u32[]{:S(2)}) collective-permute-start(f32[16,4096]{1,0:T(8,128)} %get-tuple-element.18.refs_3_.refs_8_), channel_id=1, source_target_pairs={{1,2},{3,4},{5,6},{7,8},{9,10},{11,12},{13,14},{15,16},{17,18},{19... | collective-permute-start | bytes 786440 | tf_op jit(solution)/shard_map/ppermute | solution.py:571
  75.9 0.1 collective-permute-start.2
  76.0 9.5 %all-to-all-start.1 = ((f32[128,24,128]{2,1,0:T(8,128)}), f32[128,24,128]{2,1,0:T(8,128)}, u32[]{:S(2)}, u32[]{:S(2)}) async-start(f32[128,24,128]{2,1,0:T(8,128)} %get-tuple-element.16), calls=%async_computation.1 | async-start | bytes 3145728 | tf_op jit(solution)/shard_map/all_to_all | solution.py:575
  85.5 0.0 collective-permute-done.3.refs_5_
  85.5 0.0 copy-start.4
  85.5 0.0 collective-permute-done.2.refs_4_
  85.5 0.0 copy-start.5
  85.5 0.7 copy-done.4
  86.2 0.1 copy-done.5
  86.3 15.1 %near_second.1.refs_9_ = f32[16,4096]{1,0:T(8,128)} custom-call(s32[112]{0:T(128)} %concatenate.3.refs_0_, bf16[24,512,256]{2,1,0:T(8,128)(2,1)} %get-tuple-element.19.refs_1_, bf16[8,256,512]{2,1,0:T(8,128)(2,1)} %get-tuple-element.20.refs_2_, f32[16,4096]{1,0:T(8,128)} %get-tuple-element.18.refs_3_.refs_8_, f32[16,4096]{1,0:T(8,128)} %copy-done.5, ...), custom_call_target="tpu_custom_call" | custom-call | flops 40000000000 | bytes 6291456 | tf_op jit(solution)/shard_map/near_second/pallas_call | solution.py:111
  101.4 8.7 %all-to-all-done.1.refs_1_ = f32[128,24,128]{2,1,0:T(8,128)} async-done(((f32[128,24,128]{2,1,0:T(8,128)}), f32[128,24,128]{2,1,0:T(8,128)}, u32[]{:S(2)}, u32[]{:S(2)}) %all-to-all-start.1) | async-done | bytes 1572896 | tf_op jit(solution)/shard_map/all_to_all | solution.py:575
  110.1 8.5 %down_second.1 = (f32[16,4096]{1,0:T(8,128)}, f32[128,128]{1,0:T(8,128)}, f32[8,128]{1,0:T(8,128)}) custom-call(s32[112]{0:T(128)} %concatenate.3.refs_0_, f32[128,24,128]{2,1,0:T(8,128)} %all-to-all-done.1.refs_1_, f32[10,128,128]{2,1,0:T(8,128)} %get-tuple-element.17.refs_2_, f32[96,256,128]{2,1,0:T(8,128)} %refs_3_.5, f32[8,512,128]{2,1,0:T(8,128)} %refs_4_.5, ...), custom_call_target="tpu_custom_call" | custom-call | flops 1000000000 | bytes 6291456 | tf_op jit(solution)/shard_map/down_second/pallas_call | solution.py:111
  118.7 26.0 %all_to_all.21 = f32[128,1,128]{2,1,0:T(1,128)} all-to-all(f32[128,1,128]{2,1,0:T(1,128)} %bitcast.7), channel_id=1, replica_groups=mesh['leaf'=16,'sub'=8] {'leaf','sub'}, dimensions={0} | all-to-all | bytes 131072 | tf_op jit(solution)/shard_map/all_to_all | solution.py:575
  144.7 2.7 %finish.1 = (f32[16,4096]{1,0:T(8,128)}, f32[16,4096]{1,0:T(8,128)}) custom-call(f32[128,128]{1,0:T(8,128)} %bitcast.6, f32[8,128]{1,0:T(8,128)} %get-tuple-element.22.refs_1_, f32[16,4096]{1,0:T(8,128)} %refs_2_.7, f32[16,4096]{1,0:T(8,128)} %get-tuple-element.18.refs_3_.refs_8_, f32[16,4096]{1,0:T(8,128)} %get-tuple-element.23.refs_4_), custom_call_target="tpu_custom_call" | custom-call | flops 1000000 | bytes 6291456 | tf_op jit(solution)/shard_map/finish/pallas_call | solution.py:111
  (1 shorter events, 0.0 us)
Async XLA Ops:
  6.4 16.5 %collective-permute-start.1 = (f32[48,4096]{1,0:T(8,128)}, f32[48,4096]{1,0:T(8,128)S(1)}, u32[]{:S(2)}, u32[]{:S(2)}) collective-permute-start(f32[48,4096]{1,0:T(8,128)} %get-tuple-element.14), channel_id=1, source_target_pairs={{1,2},{3,4},{5,6},{7,8},{9,10},{11,12},{13,14},{15,16},{17,18},{19... | collective-permute-start | bytes 2359304 | tf_op jit(solution)/shard_map/ppermute | solution.py:571
  11.4 11.6 %collective-permute-start = (f32[48,4096]{1,0:T(8,128)}, f32[48,4096]{1,0:T(8,128)}, u32[]{:S(2)}, u32[]{:S(2)}) collective-permute-start(f32[48,4096]{1,0:T(8,128)} %get-tuple-element.14), channel_id=1, source_target_pairs={{0,1},{1,0},{2,3},{3,2},{4,5},{5,4},{6,7},{7,6},{8,9},{9,8},{10,11... | collective-permute-start | bytes 2359304 | tf_op jit(solution)/shard_map/ppermute | solution.py:571
  11.4 10.5 %copy-start.1 = (s32[8,12]{1,0:T(8,128)S(1)}, s32[8,12]{1,0:T(8,128)}, u32[]{:S(2)}) copy-start(s32[8,12]{1,0:T(8,128)} %param.27) | copy-start | bytes 1156
  11.5 10.6 %copy-start = (s32[96,4]{0,1:T(4,128)S(1)}, s32[96,4]{0,1:T(4,128)}, u32[]{:S(2)}) copy-start(s32[96,4]{0,1:T(4,128)} %param.29) | copy-start | bytes 4612
  11.5 10.8 %copy-start.2 = (s32[1,2]{1,0:T(1,128)S(1)}, s32[1,2]{1,0:T(1,128)}, u32[]{:S(2)}) copy-start(s32[1,2]{1,0:T(1,128)} %param.28) | copy-start | bytes 28
  11.5 52.0 %all-to-all-start = ((f32[128,48,128]{2,1,0:T(8,128)}), f32[128,48,128]{2,1,0:T(8,128)}, u32[]{:S(2)}, u32[]{:S(2)}) async-start(f32[128,48,128]{2,1,0:T(8,128)} %get-tuple-element.13), calls=%async_computation | async-start | bytes 6291456 | tf_op jit(solution)/shard_map/all_to_all | solution.py:575
  22.9 0.9 copy-start.3
  73.2 12.3 %collective-permute-start.3 = (f32[16,4096]{1,0:T(8,128)}, f32[16,4096]{1,0:T(8,128)S(1)}, u32[]{:S(2)}, u32[]{:S(2)}) collective-permute-start(f32[16,4096]{1,0:T(8,128)} %get-tuple-element.18.refs_3_.refs_8_), channel_id=1, source_target_pairs={{1,2},{3,4},{5,6},{7,8},{9,10},{11,12},{13,14},{15,16},{17,18},{19... | collective-permute-start | bytes 786440 | tf_op jit(solution)/shard_map/ppermute | solution.py:571
  75.9 9.6 %collective-permute-start.2 = (f32[16,4096]{1,0:T(8,128)}, f32[16,4096]{1,0:T(8,128)S(1)}, u32[]{:S(2)}, u32[]{:S(2)}) collective-permute-start(f32[16,4096]{1,0:T(8,128)} %get-tuple-element.18.refs_3_.refs_8_), channel_id=1, source_target_pairs={{0,1},{1,0},{2,3},{3,2},{4,5},{5,4},{6,7},{7,6},{8,9},{9,8},{10,11... | collective-permute-start | bytes 786440 | tf_op jit(solution)/shard_map/ppermute | solution.py:571
  76.0 34.1 %all-to-all-start.1 = ((f32[128,24,128]{2,1,0:T(8,128)}), f32[128,24,128]{2,1,0:T(8,128)}, u32[]{:S(2)}, u32[]{:S(2)}) async-start(f32[128,24,128]{2,1,0:T(8,128)} %get-tuple-element.16), calls=%async_computation.1 | async-start | bytes 3145728 | tf_op jit(solution)/shard_map/all_to_all | solution.py:575
  85.5 0.7 copy-start.4
  85.5 0.8 copy-start.5

commit v4 on v3

--- a/solution.py
+++ b/solution.py
@@ -153,16 +153,12 @@
 
 
 def first_kernel(*refs):
-    inputs, (message_out, halo_out) = refs[:10], refs[10:12]
-    held, (message, semaphores) = refs[12:22], refs[22:]
+    inputs, message_out = refs[:10], refs[10]
+    held, (message, semaphores) = refs[11:21], refs[21:]
     copies = Copies(semaphores)
     arrive = [copies.start(source, target) for source, target in zip(inputs, held)]
     points, field, interp, one, two, three, leaf_pick, one_pick, two_pick, three_pick = held
     wait_all(arrive[0:2])
-    leave = [
-        copies.start(points, halo_out.at[0:DIMS, :]),
-        copies.start(field, halo_out.at[DIMS : DIMS + RHS, :]),
-    ]
     wait_all(arrive[6:])
     level = [
         pick(parts_of(points[:, cols(a)] * COORD_SCALE), leaf_pick[a : a + 1, :])
@@ -177,8 +173,7 @@
     charges = climb(field, interp, (one, two, three))
     block = jnp.concatenate([charges, joined(level[0])], 0)
     message[...] = jnp.broadcast_to(block[None], message.shape)
-    leave += send_copies(copies, message, message_out)
-    wait_all(leave)
+    wait_all(send_copies(copies, message, message_out))
 
 
 def send_copies(copies, message, message_out):
@@ -194,7 +189,7 @@
     return call(
         first_kernel,
         "first_up",
-        [shape((DEVICES, RHS + DIMS, RANK)), shape((DIMS + RHS, WIDTH))],
+        [shape((DEVICES, RHS + DIMS, RANK))],
         None,
         inputs,
         scratch_for(inputs) + [pltpu.VMEM((16, RHS + DIMS, RANK), F)],
@@ -204,8 +199,10 @@
 
 def near_kernel(fresh, *refs):
     if fresh:
-        ids_ref, points_in, field_in, partner_in, other_in, part_out, right_out, left_out = refs[:8]
-        points, field, partner, other = refs[8:12]
+        ids_ref, points_in, field_in, partner_in, other_in, beside_in = refs[0:5] + (refs[5:7],)
+        part_out, right_out, left_out = refs[7:10]
+        points, field, partner, other = refs[10:14]
+        beside_points = refs[14:16]
     else:
         ids_ref, right_in, left_in, field_in, partner_in, other_in, part_out = refs[:7]
         field, partner, other = refs[7:10]
@@ -220,7 +217,9 @@
             copies.start(right_in.at[0:LEAVES_HERE], right.at[0:LEAVES_HERE]),
         ]
     arrive_beside = [copies.start(partner_in, partner), copies.start(other_in, other)]
-    if not fresh:
+    if fresh:
+        arrive_beside += [copies.start(*pair) for pair in zip(beside_in, beside_points)]
+    else:
         arrive_beside.append(
             copies.start(
                 right_in.at[LEAVES_HERE : 3 * LEAVES_HERE], right.at[LEAVES_HERE : 3 * LEAVES_HERE]
@@ -259,7 +258,7 @@
 
     def take_values(source, at):
         for a in range(LEAVES_HERE):
-            values[at + a] = jnp.concatenate(split_three(source[source.shape[0] - RHS :, cols(a)]), 0)
+            values[at + a] = jnp.concatenate(split_three(source[:, cols(a)]), 0)
 
     def exponent(t):
         origin = origins[t]
@@ -315,9 +314,9 @@
     take_values(partner, LEAVES_HERE)
     take_values(other, 2 * LEAVES_HERE)
     if fresh:
-        for side, source in enumerate((partner, other)):
+        for side, source in enumerate(beside_points):
             for a in range(LEAVES_HERE):
-                y = source[0:DIMS, cols(a)] * COORD_SCALE
+                y = source[:, cols(a)] * COORD_SCALE
                 right[(side + 1) * LEAVES_HERE + a] = operands(y)[1].T
         beside = slice(LEAVES_HERE, 3 * LEAVES_HERE)
         leave.append(copies.start(right.at[beside], right_out.at[beside]))
@@ -599,12 +598,11 @@
         [device[None], far_three[0], fours, fives, jnp.zeros((5,), jnp.int32), near_list.reshape(-1)]
     )
     weights = (interp, up_one, up_two, up_three)
-    message, halo = first(
-        points, right_side, weights, (leaf_skel, skel_one, skel_two, skel_three)
-    )
-    partner, other = beside(halo)
+    (message,) = first(points, right_side, weights, (leaf_skel, skel_one, skel_two, skel_three))
     message = everyone(message)
-    part, right, left = near(True, ids, points, right_side, partner, other)
+    part, right, left = near(
+        True, ids, points, right_side, *beside(right_side), *beside(points)
+    )
     image, own_message, blocks = down(
         True, ids, message, skel_top, up_top, *weights, right_side, part
     )

time: 150 us -> 159 us (1.060)
  starting transfers between devices: 27.7 us -> 33.5 us
  Pallas kernels: 57.7 us -> 53.3 us
  waiting for transfers between devices: 32.5 us -> 36.8 us
  blocking collectives: 26 us -> 29.8 us
    pallas_call x6, Pallas kernels: 57.7 us -> 53.3 us  [call(): pl.pallas_call(kernel, out_shape=out, in_specs=([SMEM] if ids is not None...]
    all_to_all x2, waiting for transfers between devices: 32.5 us -> 36.7 us  [everyone(): return lax.all_to_all(copies, AXES, 0, 0, tiled=True)]
    all_to_all x1, blocking collectives: 26 us -> 29.8 us  [everyone(): return lax.all_to_all(copies, AXES, 0, 0, tiled=True)]
    all_to_all x2, starting transfers between devices: 19.9 us -> 23.5 us  [everyone(): return lax.all_to_all(copies, AXES, 0, 0, tiled=True)]
    ppermute x2 -> x3, starting transfers between devices: 7.58 us -> 8.38 us  [beside(): lax.ppermute(value, AXES, other)]
  transfers between devices with their start and end apart: 6 -> 8, of which waited for: 2 -> 2; matrix products, arithmetic and copies ran while one was open for 1% -> 1% of each run, Pallas kernels for 21% -> 21%
where the time goes in v4:
time: 159 us; the launch traced here: 157 us
  Pallas kernels  53.3 us (34%)
  waiting for transfers between devices  36.8 us (23%)
  starting transfers between devices  33.5 us (21%)
  blocking collectives  29.8 us (19%)
  local copies, waits for them, and re-layouts  2.35 us (1%)
    pallas_call x6, Pallas kernels, call(): pl.pallas_call(kernel, out_shape=out, in_specs=([SMEM] if ids is not None...  53.3 us
    all_to_all x2, waiting for transfers between devices, everyone(): return lax.all_to_all(copies, AXES, 0, 0, tiled=True)  36.7 us
    all_to_all x1, blocking collectives, everyone(): return lax.all_to_all(copies, AXES, 0, 0, tiled=True)  29.8 us
    all_to_all x2, starting transfers between devices, everyone(): return lax.all_to_all(copies, AXES, 0, 0, tiled=True)  23.5 us
    ppermute x3, starting transfers between devices, beside(): lax.ppermute(value, AXES, other)  8.38 us
  transfers between devices with their start and end apart: 8, of which 2 were waited for; matrix products, arithmetic and copies ran while one was open for 1% of the time, Pallas kernels for 21%

profile of v4, /device:TPU:1, one launch (start us, length us, event | category | flops | bytes accessed | tf_op | source)
XLA Modules:
  0.0 157.0 jit_solution(14713147130619751893)
XLA Ops:
  0.6 1.5 collective-permute-start.2
  2.1 3.5 %collective-permute-start.3 = (f32[32,4096]{1,0:T(8,128)}, f32[32,4096]{1,0:T(8,128)}, u32[]{:S(2)}, u32[]{:S(2)}) collective-permute-start(f32[32,4096]{1,0:T(8,128)} %refs_1_.3), channel_id=1, source_target_pairs={{1,2},{3,4},{5,6},{7,8},{9,10},{11,12},{13,14},{15,16},{17,18},{19... | collective-permute-start | bytes 1572872 | tf_op jit(solution)/shard_map/ppermute | solution.py:570
  5.7 2.0 %collective-permute-start.1 = (f32[16,4096]{1,0:T(8,128)}, f32[16,4096]{1,0:T(8,128)S(1)}, u32[]{:S(2)}, u32[]{:S(2)}) collective-permute-start(f32[16,4096]{1,0:T(8,128)} %refs_2_.7), channel_id=1, source_target_pairs={{1,2},{3,4},{5,6},{7,8},{9,10},{11,12},{13,14},{15,16},{17,18},{19... | collective-permute-start | bytes 786440 | tf_op jit(solution)/shard_map/ppermute | solution.py:570
  7.7 0.1 collective-permute-start
  7.8 5.6 %first_up.1 = f32[128,48,128]{2,1,0:T(8,128)} custom-call(f32[32,4096]{1,0:T(8,128)} %refs_1_.3, f32[16,4096]{1,0:T(8,128)} %refs_2_.7, f32[8,512,128]{2,1,0:T(8,128)} %refs_4_.5, f32[4,256,128]{2,1,0:T(8,128)} %refs_5_.5, f32[2,256,128]{2,1,0:T(8,128)} %refs_6_.5, f32[1,256,128]{2,1,0:T(8,128)} %refs_7_.5, s32[8,128]{1,0:T(8,128)} %refs_6_.3, ...), custom_call_target="tpu_custom_call" | custom-call | flops 1000000000 | bytes 6291456 | tf_op jit(solution)/shard_map/first_up/pallas_call | solution.py:111
  13.4 0.0 copy-start.1
  13.4 0.0 copy-start
  13.4 0.0 copy-start.2
  13.5 15.0 %all-to-all-start = ((f32[128,48,128]{2,1,0:T(8,128)}), f32[128,48,128]{2,1,0:T(8,128)}, u32[]{:S(2)}, u32[]{:S(2)}) async-start(f32[128,48,128]{2,1,0:T(8,128)} %first_up.1), calls=%async_computation | async-start | bytes 6291456 | tf_op jit(solution)/shard_map/all_to_all | solution.py:574
  28.5 0.0 copy-done.1
  28.5 0.1 reshape.11
  28.6 0.0 copy-done
  28.6 0.2 add_reduce_fusion
  28.8 0.0 copy-done.2
  28.8 0.6 concatenate.3.refs_0_
  29.4 0.0 collective-permute-done.1.refs_4_
  29.5 0.0 copy-start.4
  29.5 0.0 collective-permute-done.refs_3_
  29.5 0.0 collective-permute-done.2.refs_5_
  29.5 0.0 copy-start.3
  29.5 0.0 collective-permute-done.3.refs_6_
  29.5 0.7 copy-done.4
  30.2 0.2 copy-done.3
  30.4 13.7 %near_first.1 = (f32[16,4096]{1,0:T(8,128)}, bf16[24,512,256]{2,1,0:T(8,128)(2,1)}, bf16[8,256,512]{2,1,0:T(8,128)(2,1)}) custom-call(s32[112]{0:T(128)} %concatenate.3.refs_0_, f32[32,4096]{1,0:T(8,128)} %refs_1_.3, f32[16,4096]{1,0:T(8,128)} %refs_2_.7, f32[16,4096]{1,0:T(8,128)} %collective-permute-done.refs_3_, f32[16,4096]{1,0:T(8,128)} %copy-done.4, ...), custom_call_target="tpu_custom_call" | custom-call | flops 40000000000 | bytes 6291456 | tf_op jit(solution)/shard_map/near_first/pallas_call | solution.py:111
  44.1 25.9 %all-to-all-done.refs_1_ = f32[128,48,128]{2,1,0:T(8,128)} async-done(((f32[128,48,128]{2,1,0:T(8,128)}), f32[128,48,128]{2,1,0:T(8,128)}, u32[]{:S(2)}, u32[]{:S(2)}) %all-to-all-start) | async-done | bytes 3145760 | tf_op jit(solution)/shard_map/all_to_all | solution.py:574
  70.0 9.7 %down_first.1 = (f32[16,4096]{1,0:T(8,128)}, f32[128,24,128]{2,1,0:T(8,128)}, f32[10,128,128]{2,1,0:T(8,128)}) custom-call(s32[112]{0:T(128)} %concatenate.3.refs_0_, f32[128,48,128]{2,1,0:T(8,128)} %all-to-all-done.refs_1_, s32[96,128]{1,0:T(8,128)} %refs_2_.6, f32[96,256,128]{2,1,0:T(8,128)} %refs_3_.5, f32[8,512,128]{2,1,0:T(8,128)} %refs_4_.5, ...), custom_call_target="tpu_custom_call" | custom-call | flops 1000000000 | bytes 6291456 | tf_op jit(solution)/shard_map/down_first/pallas_call | solution.py:111
  79.8 2.8 %collective-permute-start.5 = (f32[16,4096]{1,0:T(8,128)}, f32[16,4096]{1,0:T(8,128)S(1)}, u32[]{:S(2)}, u32[]{:S(2)}) collective-permute-start(f32[16,4096]{1,0:T(8,128)} %get-tuple-element.14.refs_3_.refs_8_), channel_id=1, source_target_pairs={{1,2},{3,4},{5,6},{7,8},{9,10},{11,12},{13,14},{15,16},{17,18},{19... | collective-permute-start | bytes 786440 | tf_op jit(solution)/shard_map/ppermute | solution.py:570
  82.6 0.1 collective-permute-start.4
  82.7 8.5 %all-to-all-start.1 = ((f32[128,24,128]{2,1,0:T(8,128)}), f32[128,24,128]{2,1,0:T(8,128)}, u32[]{:S(2)}, u32[]{:S(2)}) async-start(f32[128,24,128]{2,1,0:T(8,128)} %get-tuple-element.12), calls=%async_computation.1 | async-start | bytes 3145728 | tf_op jit(solution)/shard_map/all_to_all | solution.py:574
  91.2 0.0 collective-permute-done.5.refs_5_
  91.2 0.0 copy-start.5
  91.2 0.0 collective-permute-done.4.refs_4_
  91.2 0.0 copy-start.6
  91.2 0.7 copy-done.5
  91.9 0.1 copy-done.6
  92.0 13.0 %near_second.1.refs_9_ = f32[16,4096]{1,0:T(8,128)} custom-call(s32[112]{0:T(128)} %concatenate.3.refs_0_, bf16[24,512,256]{2,1,0:T(8,128)(2,1)} %get-tuple-element.15.refs_1_, bf16[8,256,512]{2,1,0:T(8,128)(2,1)} %get-tuple-element.16.refs_2_, f32[16,4096]{1,0:T(8,128)} %get-tuple-element.14.refs_3_.refs_8_, f32[16,4096]{1,0:T(8,128)} %copy-done.6, ...), custom_call_target="tpu_custom_call" | custom-call | flops 40000000000 | bytes 6291456 | tf_op jit(solution)/shard_map/near_second/pallas_call | solution.py:111
  105.0 10.8 %all-to-all-done.1.refs_1_ = f32[128,24,128]{2,1,0:T(8,128)} async-done(((f32[128,24,128]{2,1,0:T(8,128)}), f32[128,24,128]{2,1,0:T(8,128)}, u32[]{:S(2)}, u32[]{:S(2)}) %all-to-all-start.1) | async-done | bytes 1572896 | tf_op jit(solution)/shard_map/all_to_all | solution.py:574
  115.8 8.5 %down_second.1 = (f32[16,4096]{1,0:T(8,128)}, f32[128,128]{1,0:T(8,128)}, f32[8,128]{1,0:T(8,128)}) custom-call(s32[112]{0:T(128)} %concatenate.3.refs_0_, f32[128,24,128]{2,1,0:T(8,128)} %all-to-all-done.1.refs_1_, f32[10,128,128]{2,1,0:T(8,128)} %get-tuple-element.13.refs_2_, f32[96,256,128]{2,1,0:T(8,128)} %refs_3_.5, f32[8,512,128]{2,1,0:T(8,128)} %refs_4_.5, ...), custom_call_target="tpu_custom_call" | custom-call | flops 1000000000 | bytes 6291456 | tf_op jit(solution)/shard_map/down_second/pallas_call | solution.py:111
  124.3 29.8 %all_to_all.21 = f32[128,1,128]{2,1,0:T(1,128)} all-to-all(f32[128,1,128]{2,1,0:T(1,128)} %bitcast.7), channel_id=1, replica_groups=mesh['leaf'=16,'sub'=8] {'leaf','sub'}, dimensions={0} | all-to-all | bytes 131072 | tf_op jit(solution)/shard_map/all_to_all | solution.py:574
  154.2 2.7 %finish.1 = (f32[16,4096]{1,0:T(8,128)}, f32[16,4096]{1,0:T(8,128)}) custom-call(f32[128,128]{1,0:T(8,128)} %bitcast.6, f32[8,128]{1,0:T(8,128)} %get-tuple-element.18.refs_1_, f32[16,4096]{1,0:T(8,128)} %refs_2_.7, f32[16,4096]{1,0:T(8,128)} %get-tuple-element.14.refs_3_.refs_8_, f32[16,4096]{1,0:T(8,128)} %get-tuple-element.19.refs_4_), custom_call_target="tpu_custom_call" | custom-call | flops 1000000 | bytes 6291456 | tf_op jit(solution)/shard_map/finish/pallas_call | solution.py:111
  (1 shorter events, 0.0 us)
Async XLA Ops:
  0.6 28.8 %collective-permute-start.2 = (f32[32,4096]{1,0:T(8,128)}, f32[32,4096]{1,0:T(8,128)S(1)}, u32[]{:S(2)}, u32[]{:S(2)}) collective-permute-start(f32[32,4096]{1,0:T(8,128)} %refs_1_.3), channel_id=1, source_target_pairs={{0,1},{1,0},{2,3},{3,2},{4,5},{5,4},{6,7},{7,6},{8,9},{9,8},{10,11... | collective-permute-start | bytes 1572872 | tf_op jit(solution)/shard_map/ppermute | solution.py:570
  2.1 27.4 %collective-permute-start.3 = (f32[32,4096]{1,0:T(8,128)}, f32[32,4096]{1,0:T(8,128)}, u32[]{:S(2)}, u32[]{:S(2)}) collective-permute-start(f32[32,4096]{1,0:T(8,128)} %refs_1_.3), channel_id=1, source_target_pairs={{1,2},{3,4},{5,6},{7,8},{9,10},{11,12},{13,14},{15,16},{17,18},{19... | collective-permute-start | bytes 1572872 | tf_op jit(solution)/shard_map/ppermute | solution.py:570
  5.7 23.8 %collective-permute-start.1 = (f32[16,4096]{1,0:T(8,128)}, f32[16,4096]{1,0:T(8,128)S(1)}, u32[]{:S(2)}, u32[]{:S(2)}) collective-permute-start(f32[16,4096]{1,0:T(8,128)} %refs_2_.7), channel_id=1, source_target_pairs={{1,2},{3,4},{5,6},{7,8},{9,10},{11,12},{13,14},{15,16},{17,18},{19... | collective-permute-start | bytes 786440 | tf_op jit(solution)/shard_map/ppermute | solution.py:570
  7.7 21.8 %collective-permute-start = (f32[16,4096]{1,0:T(8,128)}, f32[16,4096]{1,0:T(8,128)}, u32[]{:S(2)}, u32[]{:S(2)}) collective-permute-start(f32[16,4096]{1,0:T(8,128)} %refs_2_.7), channel_id=1, source_target_pairs={{0,1},{1,0},{2,3},{3,2},{4,5},{5,4},{6,7},{7,6},{8,9},{9,8},{10,11... | collective-permute-start | bytes 786440 | tf_op jit(solution)/shard_map/ppermute | solution.py:570
  13.4 15.1 %copy-start.1 = (s32[8,12]{1,0:T(8,128)S(1)}, s32[8,12]{1,0:T(8,128)}, u32[]{:S(2)}) copy-start(s32[8,12]{1,0:T(8,128)} %param.27) | copy-start | bytes 1156
  13.4 15.2 %copy-start = (s32[96,4]{0,1:T(4,128)S(1)}, s32[96,4]{0,1:T(4,128)}, u32[]{:S(2)}) copy-start(s32[96,4]{0,1:T(4,128)} %param.29) | copy-start | bytes 4612
  13.4 15.4 %copy-start.2 = (s32[1,2]{1,0:T(1,128)S(1)}, s32[1,2]{1,0:T(1,128)}, u32[]{:S(2)}) copy-start(s32[1,2]{1,0:T(1,128)} %param.28) | copy-start | bytes 28
  13.5 56.6 %all-to-all-start = ((f32[128,48,128]{2,1,0:T(8,128)}), f32[128,48,128]{2,1,0:T(8,128)}, u32[]{:S(2)}, u32[]{:S(2)}) async-start(f32[128,48,128]{2,1,0:T(8,128)} %first_up.1), calls=%async_computation | async-start | bytes 6291456 | tf_op jit(solution)/shard_map/all_to_all | solution.py:574
  29.5 0.7 copy-start.4
  29.5 0.9 copy-start.3
  79.8 11.4 %collective-permute-start.5 = (f32[16,4096]{1,0:T(8,128)}, f32[16,4096]{1,0:T(8,128)S(1)}, u32[]{:S(2)}, u32[]{:S(2)}) collective-permute-start(f32[16,4096]{1,0:T(8,128)} %get-tuple-element.14.refs_3_.refs_8_), channel_id=1, source_target_pairs={{1,2},{3,4},{5,6},{7,8},{9,10},{11,12},{13,14},{15,16},{17,18},{19... | collective-permute-start | bytes 786440 | tf_op jit(solution)/shard_map/ppermute | solution.py:570
  82.6 8.6 %collective-permute-start.4 = (f32[16,4096]{1,0:T(8,128)}, f32[16,4096]{1,0:T(8,128)S(1)}, u32[]{:S(2)}, u32[]{:S(2)}) collective-permute-start(f32[16,4096]{1,0:T(8,128)} %get-tuple-element.14.refs_3_.refs_8_), channel_id=1, source_target_pairs={{0,1},{1,0},{2,3},{3,2},{4,5},{5,4},{6,7},{7,6},{8,9},{9,8},{10,11... | collective-permute-start | bytes 786440 | tf_op jit(solution)/shard_map/ppermute | solution.py:570
  82.7 33.1 %all-to-all-start.1 = ((f32[128,24,128]{2,1,0:T(8,128)}), f32[128,24,128]{2,1,0:T(8,128)}, u32[]{:S(2)}, u32[]{:S(2)}) async-start(f32[128,24,128]{2,1,0:T(8,128)} %get-tuple-element.12), calls=%async_computation.1 | async-start | bytes 3145728 | tf_op jit(solution)/shard_map/all_to_all | solution.py:574
  91.2 0.7 copy-start.5
  91.2 0.8 copy-start.6

commit v5 on v3

--- a/solution.py
+++ b/solution.py
@@ -153,16 +153,12 @@
 
 
 def first_kernel(*refs):
-    inputs, (message_out, halo_out) = refs[:10], refs[10:12]
-    held, (message, semaphores) = refs[12:22], refs[22:]
+    inputs, message_out = refs[:10], refs[10]
+    held, (message, semaphores) = refs[11:21], refs[21:]
     copies = Copies(semaphores)
     arrive = [copies.start(source, target) for source, target in zip(inputs, held)]
     points, field, interp, one, two, three, leaf_pick, one_pick, two_pick, three_pick = held
     wait_all(arrive[0:2])
-    leave = [
-        copies.start(points, halo_out.at[0:DIMS, :]),
-        copies.start(field, halo_out.at[DIMS : DIMS + RHS, :]),
-    ]
     wait_all(arrive[6:])
     level = [
         pick(parts_of(points[:, cols(a)] * COORD_SCALE), leaf_pick[a : a + 1, :])
@@ -173,20 +169,39 @@
             pick(jnp.concatenate([level[2 * n], level[2 * n + 1]], 1), ref[n : n + 1, :])
             for n in range(len(level) // 2)
         ]
+    message[:, RHS : RHS + DIMS, :] = jnp.broadcast_to(
+        joined(level[0])[None], (message.shape[0], DIMS, RANK)
+    )
+    leave = send_copies(copies, message, message_out, slice(RHS, RHS + DIMS))
     wait_all(arrive[2:6])
     charges = climb(field, interp, (one, two, three))
-    block = jnp.concatenate([charges, joined(level[0])], 0)
-    message[...] = jnp.broadcast_to(block[None], message.shape)
-    leave += send_copies(copies, message, message_out)
+    message[:, 0:RHS, :] = jnp.broadcast_to(charges[None], (message.shape[0], RHS, RANK))
+    leave += send_copies(copies, message, message_out, slice(0, RHS))
     wait_all(leave)
 
 
-def send_copies(copies, message, message_out):
+def send_copies(copies, message, message_out, rows):
     count = message.shape[0]
     return [
-        copies.start(message, message_out.at[t * count : (t + 1) * count])
+        copies.start(message.at[:, rows], message_out.at[t * count : (t + 1) * count, rows])
         for t in range(DEVICES // count)
     ]
+
+
+def halo_kernel(points_in, field_in, out, held, semaphores):
+    copies = Copies(semaphores)
+    wait_all(
+        [
+            copies.start(points_in, held.at[0:DIMS, :]),
+            copies.start(field_in, held.at[DIMS : DIMS + RHS, :]),
+        ]
+    )
+    wait_all([copies.start(held, out)])
+
+
+def halo(points, right_side):
+    out = shape((DIMS + RHS, WIDTH))
+    return call(halo_kernel, "halo", [out], None, [points, right_side], scratch_for([out]), 1000)[0]
 
 
 def first(points, right_side, weights, picks):
@@ -194,7 +209,7 @@
     return call(
         first_kernel,
         "first_up",
-        [shape((DEVICES, RHS + DIMS, RANK)), shape((DIMS + RHS, WIDTH))],
+        [shape((DEVICES, RHS + DIMS, RANK))],
         None,
         inputs,
         scratch_for(inputs) + [pltpu.VMEM((16, RHS + DIMS, RANK), F)],
@@ -283,18 +298,18 @@
             ea[...] = exponent(t + 2)
             add(t + 1, eb[...])
 
-        def four(p, carry):
-            pair(start + 4 * p)
-            pair(start + 4 * p + 2)
+        def eight(p, carry):
+            for u in range(4):
+                pair(start + 8 * p + 2 * u)
             return carry
 
         def two(p, carry):
             pair(middle + 2 * p)
             return carry
 
-        fours = (end - start) // 4
-        middle = start + 4 * fours
-        lax.fori_loop(0, fours, four, 0)
+        eights = (end - start) // 8
+        middle = start + 8 * eights
+        lax.fori_loop(0, eights, eight, 0)
         lax.fori_loop(0, (end - middle + 1) // 2, two, 0)
 
     total[...] = jnp.zeros_like(total)
@@ -410,7 +425,7 @@
         )
     for s, n in enumerate(fours + [node_four, NODES_FOUR + node_five]):
         arrive.append(copies.start(up_top_in.at[pl.ds(n, 1)], weights.at[12 + s : 13 + s]))
-    arrive += [copies.start(source, target) for source, target in zip(sources, held)]
+    arrive_held = [copies.start(source, target) for source, target in zip(sources, held)]
     interp, one, two, three, field, near_part = held[:6]
     wait_all(early)
 
@@ -469,6 +484,7 @@
 
     field_four = field_four + dot_split(field_five, half(17, node_four % 2), NT)
     level = [field_three + dot_split(field_four, half(16, dev % 2), NT)]
+    wait_all(arrive_held)
     for ref in (three, two, one):
         spread = [dot_split(h, ref[n], NT) for n, h in enumerate(level)]
         level = [s[:, side * RANK : (side + 1) * RANK] for s in spread for side in range(2)]
@@ -482,7 +498,7 @@
         sums = row_of_sums([field[...] * field[...], field[...] * image[...]])
         block = jnp.concatenate([charges, sums, jnp.zeros((7, RANK), F)], 0)
         message[...] = jnp.broadcast_to(block[None], message.shape)
-        leave += send_copies(copies, message, message_out)
+        leave += send_copies(copies, message, message_out, slice(0, RHS + 8))
     else:
         wait_all([arrive_sums])
         base_field = held[6]
@@ -599,12 +615,9 @@
         [device[None], far_three[0], fours, fives, jnp.zeros((5,), jnp.int32), near_list.reshape(-1)]
     )
     weights = (interp, up_one, up_two, up_three)
-    message, halo = first(
-        points, right_side, weights, (leaf_skel, skel_one, skel_two, skel_three)
-    )
-    partner, other = beside(halo)
+    (message,) = first(points, right_side, weights, (leaf_skel, skel_one, skel_two, skel_three))
     message = everyone(message)
-    part, right, left = near(True, ids, points, right_side, partner, other)
+    part, right, left = near(True, ids, points, right_side, *beside(halo(points, right_side)))
     image, own_message, blocks = down(
         True, ids, message, skel_top, up_top, *weights, right_side, part
     )

time: 150 us -> 151 us (level); the launches traced: 148 us -> 153 us
  Pallas kernels: 57.7 us -> 87.9 us
  waiting for transfers between devices: 32.5 us -> 9.82 us
    pallas_call x6 -> x7, Pallas kernels: 57.7 us -> 87.9 us  [call(): pl.pallas_call(kernel, out_shape=out, in_specs=([SMEM] if ids is not None...]
    all_to_all x2, waiting for transfers between devices: 32.5 us -> 9.81 us  [everyone(): return lax.all_to_all(copies, AXES, 0, 0, tiled=True)]
  transfers between devices with their start and end apart: 6 -> 6, of which waited for: 2 -> 1; matrix products, arithmetic and copies ran while one was open for 1% -> 1% of each run, Pallas kernels for 21% -> 42%
where the time goes in v5:
time: 151 us; the launch traced here: 153 us
  Pallas kernels  87.9 us (58%)
  starting transfers between devices  26.7 us (18%)
  blocking collectives  25.4 us (17%)
  waiting for transfers between devices  9.82 us (7%)
  local copies, waits for them, and re-layouts  2.35 us (2%)
    pallas_call x7, Pallas kernels, call(): pl.pallas_call(kernel, out_shape=out, in_specs=([SMEM] if ids is not None...  87.9 us
    all_to_all x1, blocking collectives, everyone(): return lax.all_to_all(copies, AXES, 0, 0, tiled=True)  25.4 us
    all_to_all x2, starting transfers between devices, everyone(): return lax.all_to_all(copies, AXES, 0, 0, tiled=True)  18.8 us
    all_to_all x2, waiting for transfers between devices, everyone(): return lax.all_to_all(copies, AXES, 0, 0, tiled=True)  9.81 us
    ppermute x2, starting transfers between devices, beside(): lax.ppermute(value, AXES, other)  7.68 us
  transfers between devices with their start and end apart: 6, of which 1 were waited for; matrix products, arithmetic and copies ran while one was open for 1% of the time, Pallas kernels for 42%

profile of v5, /device:TPU:1, one launch (start us, length us, event | category | flops | bytes accessed | tf_op | source)
XLA Modules:
  0.0 153.5 jit_solution(2278397038062017410)
XLA Ops:
  0.6 2.5 %halo.1 = f32[48,4096]{1,0:T(8,128)} custom-call(f32[32,4096]{1,0:T(8,128)} %refs_1_.3, f32[16,4096]{1,0:T(8,128)} %refs_2_.7), custom_call_target="tpu_custom_call" | custom-call | flops 1000 | bytes 6291456 | tf_op jit(solution)/shard_map/halo/pallas_call | solution.py:111
  3.1 4.9 %collective-permute-start.1 = (f32[48,4096]{1,0:T(8,128)}, f32[48,4096]{1,0:T(8,128)S(1)}, u32[]{:S(2)}, u32[]{:S(2)}) collective-permute-start(f32[48,4096]{1,0:T(8,128)} %halo.1), channel_id=1, source_target_pairs={{1,2},{3,4},{5,6},{7,8},{9,10},{11,12},{13,14},{15,16},{17,18},{19... | collective-permute-start | bytes 2359304 | tf_op jit(solution)/shard_map/ppermute | solution.py:587
  8.1 0.1 collective-permute-start
  8.2 5.0 %first_up.1 = f32[128,48,128]{2,1,0:T(8,128)} custom-call(f32[32,4096]{1,0:T(8,128)} %refs_1_.3, f32[16,4096]{1,0:T(8,128)} %refs_2_.7, f32[8,512,128]{2,1,0:T(8,128)} %refs_4_.5, f32[4,256,128]{2,1,0:T(8,128)} %refs_5_.5, f32[2,256,128]{2,1,0:T(8,128)} %refs_6_.5, f32[1,256,128]{2,1,0:T(8,128)} %refs_7_.5, s32[8,128]{1,0:T(8,128)} %refs_6_.3, ...), custom_call_target="tpu_custom_call" | custom-call | flops 1000000000 | bytes 6291456 | tf_op jit(solution)/shard_map/first_up/pallas_call | solution.py:111
  13.1 0.0 copy-start.1
  13.2 0.0 copy-start
  13.2 0.0 copy-start.2
  13.2 10.4 %all-to-all-start = ((f32[128,48,128]{2,1,0:T(8,128)}), f32[128,48,128]{2,1,0:T(8,128)}, u32[]{:S(2)}, u32[]{:S(2)}) async-start(f32[128,48,128]{2,1,0:T(8,128)} %first_up.1), calls=%async_computation | async-start | bytes 6291456 | tf_op jit(solution)/shard_map/all_to_all | solution.py:591
  23.7 0.0 copy-done.1
  23.7 0.1 reshape.11
  23.7 0.0 copy-done
  23.7 0.2 add_reduce_fusion
  24.0 0.0 copy-done.2
  24.0 0.6 concatenate.3.refs_0_
  24.6 0.0 collective-permute-done.1.refs_4_
  24.6 0.0 copy-start.3
  24.6 0.0 collective-permute-done.refs_3_
  24.6 0.9 copy-done.3
  25.5 29.9 %near_first.1 = (f32[16,4096]{1,0:T(8,128)}, bf16[24,512,256]{2,1,0:T(8,128)(2,1)}, bf16[8,256,512]{2,1,0:T(8,128)(2,1)}) custom-call(s32[112]{0:T(128)} %concatenate.3.refs_0_, f32[32,4096]{1,0:T(8,128)} %refs_1_.3, f32[16,4096]{1,0:T(8,128)} %refs_2_.7, f32[48,4096]{1,0:T(8,128)} %collective-permute-done.refs_3_, f32[48,4096]{1,0:T(8,128)} %copy-done.3), custom_call_target="tpu_custom_call" | custom-call | flops 40000000000 | bytes 6291456 | tf_op jit(solution)/shard_map/near_first/pallas_call | solution.py:111
  55.4 9.8 %all-to-all-done.refs_1_ = f32[128,48,128]{2,1,0:T(8,128)} async-done(((f32[128,48,128]{2,1,0:T(8,128)}), f32[128,48,128]{2,1,0:T(8,128)}, u32[]{:S(2)}, u32[]{:S(2)}) %all-to-all-start) | async-done | bytes 3145760 | tf_op jit(solution)/shard_map/all_to_all | solution.py:591
  65.2 10.0 %down_first.1 = (f32[16,4096]{1,0:T(8,128)}, f32[128,24,128]{2,1,0:T(8,128)}, f32[10,128,128]{2,1,0:T(8,128)}) custom-call(s32[112]{0:T(128)} %concatenate.3.refs_0_, f32[128,48,128]{2,1,0:T(8,128)} %all-to-all-done.refs_1_, s32[96,128]{1,0:T(8,128)} %refs_2_.6, f32[96,256,128]{2,1,0:T(8,128)} %refs_3_.5, f32[8,512,128]{2,1,0:T(8,128)} %refs_4_.5, ...), custom_call_target="tpu_custom_call" | custom-call | flops 1000000000 | bytes 6291456 | tf_op jit(solution)/shard_map/down_first/pallas_call | solution.py:111
  75.1 2.7 %collective-permute-start.3 = (f32[16,4096]{1,0:T(8,128)}, f32[16,4096]{1,0:T(8,128)S(1)}, u32[]{:S(2)}, u32[]{:S(2)}) collective-permute-start(f32[16,4096]{1,0:T(8,128)} %get-tuple-element.14.refs_3_.refs_8_), channel_id=1, source_target_pairs={{1,2},{3,4},{5,6},{7,8},{9,10},{11,12},{13,14},{15,16},{17,18},{19... | collective-permute-start | bytes 786440 | tf_op jit(solution)/shard_map/ppermute | solution.py:587
  77.9 0.1 collective-permute-start.2
  78.0 8.4 %all-to-all-start.1 = ((f32[128,24,128]{2,1,0:T(8,128)}), f32[128,24,128]{2,1,0:T(8,128)}, u32[]{:S(2)}, u32[]{:S(2)}) async-start(f32[128,24,128]{2,1,0:T(8,128)} %get-tuple-element.12), calls=%async_computation.1 | async-start | bytes 3145728 | tf_op jit(solution)/shard_map/all_to_all | solution.py:591
  86.4 0.0 collective-permute-done.3.refs_5_
  86.4 0.0 copy-start.4
  86.4 0.0 collective-permute-done.2.refs_4_
  86.4 0.0 copy-start.5
  86.5 0.7 copy-done.4
  87.1 0.1 copy-done.5
  87.2 29.3 %near_second.1.refs_9_ = f32[16,4096]{1,0:T(8,128)} custom-call(s32[112]{0:T(128)} %concatenate.3.refs_0_, bf16[24,512,256]{2,1,0:T(8,128)(2,1)} %get-tuple-element.15.refs_1_, bf16[8,256,512]{2,1,0:T(8,128)(2,1)} %get-tuple-element.16.refs_2_, f32[16,4096]{1,0:T(8,128)} %get-tuple-element.14.refs_3_.refs_8_, f32[16,4096]{1,0:T(8,128)} %copy-done.5, ...), custom_call_target="tpu_custom_call" | custom-call | flops 40000000000 | bytes 6291456 | tf_op jit(solution)/shard_map/near_second/pallas_call | solution.py:111
  116.5 0.0 all-to-all-done.1.refs_1_
  116.5 8.6 %down_second.1 = (f32[16,4096]{1,0:T(8,128)}, f32[128,128]{1,0:T(8,128)}, f32[8,128]{1,0:T(8,128)}) custom-call(s32[112]{0:T(128)} %concatenate.3.refs_0_, f32[128,24,128]{2,1,0:T(8,128)} %all-to-all-done.1.refs_1_, f32[10,128,128]{2,1,0:T(8,128)} %get-tuple-element.13.refs_2_, f32[96,256,128]{2,1,0:T(8,128)} %refs_3_.5, f32[8,512,128]{2,1,0:T(8,128)} %refs_4_.5, ...), custom_call_target="tpu_custom_call" | custom-call | flops 1000000000 | bytes 6291456 | tf_op jit(solution)/shard_map/down_second/pallas_call | solution.py:111
  125.2 25.4 %all_to_all.21 = f32[128,1,128]{2,1,0:T(1,128)} all-to-all(f32[128,1,128]{2,1,0:T(1,128)} %bitcast.7), channel_id=1, replica_groups=mesh['leaf'=16,'sub'=8] {'leaf','sub'}, dimensions={0} | all-to-all | bytes 131072 | tf_op jit(solution)/shard_map/all_to_all | solution.py:591
  150.6 2.7 %finish.1 = (f32[16,4096]{1,0:T(8,128)}, f32[16,4096]{1,0:T(8,128)}) custom-call(f32[128,128]{1,0:T(8,128)} %bitcast.6, f32[8,128]{1,0:T(8,128)} %get-tuple-element.18.refs_1_, f32[16,4096]{1,0:T(8,128)} %refs_2_.7, f32[16,4096]{1,0:T(8,128)} %get-tuple-element.14.refs_3_.refs_8_, f32[16,4096]{1,0:T(8,128)} %get-tuple-element.19.refs_4_), custom_call_target="tpu_custom_call" | custom-call | flops 1000000 | bytes 6291456 | tf_op jit(solution)/shard_map/finish/pallas_call | solution.py:111
  (1 shorter events, 0.0 us)
Async XLA Ops:
  3.1 21.4 %collective-permute-start.1 = (f32[48,4096]{1,0:T(8,128)}, f32[48,4096]{1,0:T(8,128)S(1)}, u32[]{:S(2)}, u32[]{:S(2)}) collective-permute-start(f32[48,4096]{1,0:T(8,128)} %halo.1), channel_id=1, source_target_pairs={{1,2},{3,4},{5,6},{7,8},{9,10},{11,12},{13,14},{15,16},{17,18},{19... | collective-permute-start | bytes 2359304 | tf_op jit(solution)/shard_map/ppermute | solution.py:587
  8.1 16.5 %collective-permute-start = (f32[48,4096]{1,0:T(8,128)}, f32[48,4096]{1,0:T(8,128)}, u32[]{:S(2)}, u32[]{:S(2)}) collective-permute-start(f32[48,4096]{1,0:T(8,128)} %halo.1), channel_id=1, source_target_pairs={{0,1},{1,0},{2,3},{3,2},{4,5},{5,4},{6,7},{7,6},{8,9},{9,8},{10,11... | collective-permute-start | bytes 2359304 | tf_op jit(solution)/shard_map/ppermute | solution.py:587
  13.1 10.5 %copy-start.1 = (s32[8,12]{1,0:T(8,128)S(1)}, s32[8,12]{1,0:T(8,128)}, u32[]{:S(2)}) copy-start(s32[8,12]{1,0:T(8,128)} %param.27) | copy-start | bytes 1156
  13.2 10.6 %copy-start = (s32[96,4]{0,1:T(4,128)S(1)}, s32[96,4]{0,1:T(4,128)}, u32[]{:S(2)}) copy-start(s32[96,4]{0,1:T(4,128)} %param.29) | copy-start | bytes 4612
  13.2 10.8 %copy-start.2 = (s32[1,2]{1,0:T(1,128)S(1)}, s32[1,2]{1,0:T(1,128)}, u32[]{:S(2)}) copy-start(s32[1,2]{1,0:T(1,128)} %param.28) | copy-start | bytes 28
  13.2 52.0 %all-to-all-start = ((f32[128,48,128]{2,1,0:T(8,128)}), f32[128,48,128]{2,1,0:T(8,128)}, u32[]{:S(2)}, u32[]{:S(2)}) async-start(f32[128,48,128]{2,1,0:T(8,128)} %first_up.1), calls=%async_computation | async-start | bytes 6291456 | tf_op jit(solution)/shard_map/all_to_all | solution.py:591
  24.6 0.9 copy-start.3
  75.1 11.3 %collective-permute-start.3 = (f32[16,4096]{1,0:T(8,128)}, f32[16,4096]{1,0:T(8,128)S(1)}, u32[]{:S(2)}, u32[]{:S(2)}) collective-permute-start(f32[16,4096]{1,0:T(8,128)} %get-tuple-element.14.refs_3_.refs_8_), channel_id=1, source_target_pairs={{1,2},{3,4},{5,6},{7,8},{9,10},{11,12},{13,14},{15,16},{17,18},{19... | collective-permute-start | bytes 786440 | tf_op jit(solution)/shard_map/ppermute | solution.py:587
  77.9 8.5 %collective-permute-start.2 = (f32[16,4096]{1,0:T(8,128)}, f32[16,4096]{1,0:T(8,128)S(1)}, u32[]{:S(2)}, u32[]{:S(2)}) collective-permute-start(f32[16,4096]{1,0:T(8,128)} %get-tuple-element.14.refs_3_.refs_8_), channel_id=1, source_target_pairs={{0,1},{1,0},{2,3},{3,2},{4,5},{5,4},{6,7},{7,6},{8,9},{9,8},{10,11... | collective-permute-start | bytes 786440 | tf_op jit(solution)/shard_map/ppermute | solution.py:587
  78.0 38.5 %all-to-all-start.1 = ((f32[128,24,128]{2,1,0:T(8,128)}), f32[128,24,128]{2,1,0:T(8,128)}, u32[]{:S(2)}, u32[]{:S(2)}) async-start(f32[128,24,128]{2,1,0:T(8,128)} %get-tuple-element.12), calls=%async_computation.1 | async-start | bytes 3145728 | tf_op jit(solution)/shard_map/all_to_all | solution.py:591
  86.4 0.7 copy-start.4
  86.4 0.8 copy-start.5

commit v6 on v5

--- a/solution.py
+++ b/solution.py
@@ -153,12 +153,16 @@
 
 
 def first_kernel(*refs):
-    inputs, message_out = refs[:10], refs[10]
-    held, (message, semaphores) = refs[11:21], refs[21:]
+    inputs, (message_out, halo_out) = refs[:10], refs[10:12]
+    held, (message, semaphores) = refs[12:22], refs[22:]
     copies = Copies(semaphores)
     arrive = [copies.start(source, target) for source, target in zip(inputs, held)]
     points, field, interp, one, two, three, leaf_pick, one_pick, two_pick, three_pick = held
     wait_all(arrive[0:2])
+    leave = [
+        copies.start(points, halo_out.at[0:DIMS, :]),
+        copies.start(field, halo_out.at[DIMS : DIMS + RHS, :]),
+    ]
     wait_all(arrive[6:])
     level = [
         pick(parts_of(points[:, cols(a)] * COORD_SCALE), leaf_pick[a : a + 1, :])
@@ -172,7 +176,7 @@
     message[:, RHS : RHS + DIMS, :] = jnp.broadcast_to(
         joined(level[0])[None], (message.shape[0], DIMS, RANK)
     )
-    leave = send_copies(copies, message, message_out, slice(RHS, RHS + DIMS))
+    leave += send_copies(copies, message, message_out, slice(RHS, RHS + DIMS))
     wait_all(arrive[2:6])
     charges = climb(field, interp, (one, two, three))
     message[:, 0:RHS, :] = jnp.broadcast_to(charges[None], (message.shape[0], RHS, RANK))
@@ -188,28 +192,12 @@
     ]
 
 
-def halo_kernel(points_in, field_in, out, held, semaphores):
-    copies = Copies(semaphores)
-    wait_all(
-        [
-            copies.start(points_in, held.at[0:DIMS, :]),
-            copies.start(field_in, held.at[DIMS : DIMS + RHS, :]),
-        ]
-    )
-    wait_all([copies.start(held, out)])
-
-
-def halo(points, right_side):
-    out = shape((DIMS + RHS, WIDTH))
-    return call(halo_kernel, "halo", [out], None, [points, right_side], scratch_for([out]), 1000)[0]
-
-
 def first(points, right_side, weights, picks):
     inputs = [points, right_side, *weights, *picks]
     return call(
         first_kernel,
         "first_up",
-        [shape((DEVICES, RHS + DIMS, RANK))],
+        [shape((DEVICES, RHS + DIMS, RANK)), shape((DIMS + RHS, WIDTH))],
         None,
         inputs,
         scratch_for(inputs) + [pltpu.VMEM((16, RHS + DIMS, RANK), F)],
@@ -217,30 +205,29 @@
     )
 
 
-def near_kernel(fresh, *refs):
-    if fresh:
-        ids_ref, points_in, field_in, partner_in, other_in, part_out, right_out, left_out = refs[:8]
-        points, field, partner, other = refs[8:12]
-    else:
-        ids_ref, right_in, left_in, field_in, partner_in, other_in, part_out = refs[:7]
-        field, partner, other = refs[7:10]
+def near_kernel(form, *refs):
     right, left, total, values, ea, eb, part, targets, origins, semaphores = refs[-10:]
     copies = Copies(semaphores)
-    arrive_field = copies.start(field_in, field)
-    if fresh:
+    own_rights = right.at[0:LEAVES_HERE]
+    beside_rights = right.at[LEAVES_HERE : 3 * LEAVES_HERE]
+    if form == "own":
+        ids_ref, points_in, field_in, part_out, right_out, left_out, points, field = refs[:8]
+        arrive_field = copies.start(field_in, field)
         arrive_own = [copies.start(points_in, points)]
+    elif form == "beside":
+        ids_ref, left_in, part_in, partner_in, other_in, part_out, right_out = refs[:7]
+        partner, other = refs[7:9]
     else:
-        arrive_own = [
-            copies.start(left_in, left),
-            copies.start(right_in.at[0:LEAVES_HERE], right.at[0:LEAVES_HERE]),
-        ]
-    arrive_beside = [copies.start(partner_in, partner), copies.start(other_in, other)]
-    if not fresh:
-        arrive_beside.append(
-            copies.start(
-                right_in.at[LEAVES_HERE : 3 * LEAVES_HERE], right.at[LEAVES_HERE : 3 * LEAVES_HERE]
-            )
-        )
+        ids_ref, right_in, right_beside_in, left_in, field_in, partner_in, other_in, part_out = refs[:8]
+        field, partner, other = refs[8:11]
+        arrive_field = copies.start(field_in, field)
+        arrive_own = [copies.start(left_in, left), copies.start(right_in, own_rights)]
+    if form != "own":
+        arrive_beside = [copies.start(partner_in, partner), copies.start(other_in, other)]
+    if form == "beside":
+        arrive_own = [copies.start(left_in, left), copies.start(part_in, part)]
+    if form == "all":
+        arrive_beside.append(copies.start(right_beside_in, beside_rights))
     first = ids_ref[0] * LEAVES_HERE
     empty = 3 * LEAVES_HERE
     beside_at = 128
@@ -278,7 +265,7 @@
 
     def exponent(t):
         origin = origins[t]
-        return mm(right[jnp.where(origin == empty, 0, origin)], left[targets[t]])
+        return mm(right[jnp.where(origin == empty, LEAVES_HERE if form == "beside" else 0, origin)], left[targets[t]])
 
     def add(t, e):
         a = targets[t]
@@ -314,43 +301,56 @@
 
     total[...] = jnp.zeros_like(total)
     values[empty] = jnp.zeros((3 * RHS, LEAF), BF)
-    wait_all([arrive_field])
-    take_values(field, 0)
+    leave = []
+    if form != "beside":
+        wait_all([arrive_field])
+        take_values(field, 0)
+    if form != "own":
+        wait_all(arrive_beside[:2])
+        take_values(partner, LEAVES_HERE)
+        take_values(other, 2 * LEAVES_HERE)
+    if form == "beside":
+        for side, source in enumerate((partner, other)):
+            for a in range(LEAVES_HERE):
+                y = source[0:DIMS, cols(a)] * COORD_SCALE
+                right[(side + 1) * LEAVES_HERE + a] = operands(y)[1].T
+        leave.append(copies.start(beside_rights, right_out))
     wait_all(arrive_own)
-    leave = []
-    if fresh:
+    if form == "own":
         for a in range(LEAVES_HERE):
             left_part, right_part = operands(points[:, cols(a)] * COORD_SCALE)
             left[a] = left_part
             right[a] = right_part.T
         leave.append(copies.start(left, left_out))
-        leave.append(copies.start(right.at[0:LEAVES_HERE], right_out.at[0:LEAVES_HERE]))
-    run(0, own_end)
-    wait_all(arrive_beside)
-    take_values(partner, LEAVES_HERE)
-    take_values(other, 2 * LEAVES_HERE)
-    if fresh:
-        for side, source in enumerate((partner, other)):
-            for a in range(LEAVES_HERE):
-                y = source[0:DIMS, cols(a)] * COORD_SCALE
-                right[(side + 1) * LEAVES_HERE + a] = operands(y)[1].T
-        beside = slice(LEAVES_HERE, 3 * LEAVES_HERE)
-        leave.append(copies.start(right.at[beside], right_out.at[beside]))
-    run(beside_at, beside_end)
+        leave.append(copies.start(own_rights, right_out))
+    if form != "beside":
+        run(0, own_end)
+    if form == "all":
+        wait_all(arrive_beside[2:])
+    if form != "own":
+        run(beside_at, beside_end)
     for a in range(LEAVES_HERE):
-        part[:, cols(a)] = total[a, 0:16] + total[a, 16:32]
+        result = total[a, 0:16] + total[a, 16:32]
+        if form == "beside":
+            result = part[:, cols(a)] + result
+        part[:, cols(a)] = result
     leave.append(copies.start(part, part_out))
     wait_all(leave)
 
 
-def near(fresh, ids, *inputs):
+def near(form, ids, *inputs):
     right = shape((3 * LEAVES_HERE, LEAF, 256), BF)
     left = shape((LEAVES_HERE, 256, LEAF), BF)
-    held = inputs if fresh else inputs[2:]
+    held = {"own": inputs, "beside": inputs[2:], "all": inputs[3:]}[form]
+    made = {
+        "own": [shape((LEAVES_HERE, LEAF, 256), BF), left],
+        "beside": [shape((2 * LEAVES_HERE, LEAF, 256), BF)],
+        "all": [],
+    }[form]
     return call(
-        functools.partial(near_kernel, fresh),
-        "near_first" if fresh else "near_second",
-        [shape((RHS, WIDTH))] + ([right, left] if fresh else []),
+        functools.partial(near_kernel, form),
+        "near_" + form,
+        [shape((RHS, WIDTH))] + made,
         ids,
         inputs,
         scratch_for(held)
@@ -615,15 +615,19 @@
         [device[None], far_three[0], fours, fives, jnp.zeros((5,), jnp.int32), near_list.reshape(-1)]
     )
     weights = (interp, up_one, up_two, up_three)
-    (message,) = first(points, right_side, weights, (leaf_skel, skel_one, skel_two, skel_three))
+    message, halo = first(
+        points, right_side, weights, (leaf_skel, skel_one, skel_two, skel_three)
+    )
+    partner, other = beside(halo)
     message = everyone(message)
-    part, right, left = near(True, ids, points, right_side, *beside(halo(points, right_side)))
+    part, right, left = near("own", ids, points, right_side)
+    part, right_beside = near("beside", ids, left, part, partner, other)
     image, own_message, blocks = down(
         True, ids, message, skel_top, up_top, *weights, right_side, part
     )
     partner, other = beside(image)
     message = everyone(own_message)
-    (part,) = near(False, ids, right, left, image, partner, other)
+    (part,) = near("all", ids, right, right_beside, left, image, partner, other)
     second, rows, sums = down(
         False, ids, message, blocks, up_top, *weights, image, part, right_side
     )

time: 151 us -> 147 us (0.974); the launches traced: 153 us -> 148 us
  Pallas kernels: 87.9 us -> 57.5 us
  waiting for transfers between devices: 9.82 us -> 32.2 us
    pallas_call x7, Pallas kernels: 87.9 us -> 57.5 us  [call(): pl.pallas_call(kernel, out_shape=out, in_specs=([SMEM] if ids is not None...]
    all_to_all x2, waiting for transfers between devices: 9.81 us -> 32.2 us  [everyone(): return lax.all_to_all(copies, AXES, 0, 0, tiled=True)]
  transfers between devices with their start and end apart: 6 -> 6, of which waited for: 1 -> 2; matrix products, arithmetic and copies ran while one was open for 1% -> 1% of each run, Pallas kernels for 42% -> 21%
where the time goes in v6:
time: 147 us; the launch traced here: 148 us
  Pallas kernels  57.5 us (39%)
  waiting for transfers between devices  32.2 us (22%)
  starting transfers between devices  27.7 us (19%)
  blocking collectives  26.7 us (18%)
  local copies, waits for them, and re-layouts  2.44 us (2%)
    pallas_call x7, Pallas kernels, call(): pl.pallas_call(kernel, out_shape=out, in_specs=([SMEM] if ids is not None...  57.5 us
    all_to_all x2, waiting for transfers between devices, everyone(): return lax.all_to_all(copies, AXES, 0, 0, tiled=True)  32.2 us
    all_to_all x1, blocking collectives, everyone(): return lax.all_to_all(copies, AXES, 0, 0, tiled=True)  26.7 us
    all_to_all x2, starting transfers between devices, everyone(): return lax.all_to_all(copies, AXES, 0, 0, tiled=True)  19.6 us
    ppermute x2, starting transfers between devices, beside(): lax.ppermute(value, AXES, other)  7.9 us
  transfers between devices with their start and end apart: 6, of which 2 were waited for; matrix products, arithmetic and copies ran while one was open for 1% of the time, Pallas kernels for 21%

profile of v6, /device:TPU:1, one launch (start us, length us, event | category | flops | bytes accessed | tf_op | source)
XLA Modules:
  0.0 147.8 jit_solution(9532409262017044765)
XLA Ops:
  0.6 5.1 %first_up.1 = (f32[128,48,128]{2,1,0:T(8,128)}, f32[48,4096]{1,0:T(8,128)}) custom-call(f32[32,4096]{1,0:T(8,128)} %refs_1_.3, f32[16,4096]{1,0:T(8,128)} %refs_2_.7, f32[8,512,128]{2,1,0:T(8,128)} %refs_4_.5, f32[4,256,128]{2,1,0:T(8,128)} %refs_5_.5, f32[2,256,128]{2,1,0:T(8,128)} %refs_6_.5, f32[1,256,128]{2,1,0:T(8,128)} %refs_7_.5, s32[8,128]{1,0:T(8,128)} %refs_6_.3, ...), custom_call_target="tpu_custom_call" | custom-call | flops 1000000000 | bytes 6291456 | tf_op jit(solution)/shard_map/first_up/pallas_call | solution.py:111
  5.8 4.9 %collective-permute-start.1 = (f32[48,4096]{1,0:T(8,128)}, f32[48,4096]{1,0:T(8,128)S(1)}, u32[]{:S(2)}, u32[]{:S(2)}) collective-permute-start(f32[48,4096]{1,0:T(8,128)} %get-tuple-element.18), channel_id=1, source_target_pairs={{1,2},{3,4},{5,6},{7,8},{9,10},{11,12},{13,14},{15,16},{17,18},{19... | collective-permute-start | bytes 2359304 | tf_op jit(solution)/shard_map/ppermute | solution.py:587
  10.7 0.1 collective-permute-start
  10.8 0.0 copy-start.1
  10.8 0.0 copy-start
  10.8 0.0 copy-start.2
  10.8 10.4 %all-to-all-start = ((f32[128,48,128]{2,1,0:T(8,128)}), f32[128,48,128]{2,1,0:T(8,128)}, u32[]{:S(2)}, u32[]{:S(2)}) async-start(f32[128,48,128]{2,1,0:T(8,128)} %get-tuple-element.15), calls=%async_computation | async-start | bytes 6291456 | tf_op jit(solution)/shard_map/all_to_all | solution.py:591
  21.3 0.0 copy-done.1
  21.3 0.1 reshape.11
  21.4 0.0 copy-done
  21.4 0.2 add_reduce_fusion
  21.6 0.0 copy-done.2
  21.6 0.7 concatenate.3.refs_0_
  22.3 9.8 %near_own.1 = (f32[16,4096]{1,0:T(8,128)}, bf16[8,512,256]{2,1,0:T(8,128)(2,1)}, bf16[8,256,512]{2,1,0:T(8,128)(2,1)}) custom-call(s32[112]{0:T(128)} %concatenate.3.refs_0_, f32[32,4096]{1,0:T(8,128)} %refs_1_.3, f32[16,4096]{1,0:T(8,128)} %refs_2_.7), custom_call_target="tpu_custom_call" | custom-call | flops 40000000000 | bytes 6291456 | tf_op jit(solution)/shard_map/near_own/pallas_call | solution.py:111
  32.1 0.0 collective-permute-done.1.refs_4_
  32.1 0.0 copy-start.3
  32.1 0.0 collective-permute-done.refs_3_
  32.2 0.9 copy-done.3
  33.0 7.6 %near_beside.1 = (f32[16,4096]{1,0:T(8,128)}, bf16[16,512,256]{2,1,0:T(8,128)(2,1)}) custom-call(s32[112]{0:T(128)} %concatenate.3.refs_0_, bf16[8,256,512]{2,1,0:T(8,128)(2,1)} %get-tuple-element.16.refs_1_.refs_3_, f32[16,4096]{1,0:T(8,128)} %get-tuple-element.17.refs_2_, f32[48,4096]{1,0:T(8,128)} %collective-permute-done.refs_3_, f32[48,4096]{1,0:T(8,128)} %copy-done.3), custom_call_target="tpu_custom_call" | custom-call | flops 40000000000 | bytes 6291456 | tf_op jit(solution)/shard_map/near_beside/pallas_call | solution.py:111
  40.7 22.1 %all-to-all-done.refs_1_ = f32[128,48,128]{2,1,0:T(8,128)} async-done(((f32[128,48,128]{2,1,0:T(8,128)}), f32[128,48,128]{2,1,0:T(8,128)}, u32[]{:S(2)}, u32[]{:S(2)}) %all-to-all-start) | async-done | bytes 3145760 | tf_op jit(solution)/shard_map/all_to_all | solution.py:591
  62.8 10.0 %down_first.1 = (f32[16,4096]{1,0:T(8,128)}, f32[128,24,128]{2,1,0:T(8,128)}, f32[10,128,128]{2,1,0:T(8,128)}) custom-call(s32[112]{0:T(128)} %concatenate.3.refs_0_, f32[128,48,128]{2,1,0:T(8,128)} %all-to-all-done.refs_1_, s32[96,128]{1,0:T(8,128)} %refs_2_.6, f32[96,256,128]{2,1,0:T(8,128)} %refs_3_.5, f32[8,512,128]{2,1,0:T(8,128)} %refs_4_.5, ...), custom_call_target="tpu_custom_call" | custom-call | flops 1000000000 | bytes 6291456 | tf_op jit(solution)/shard_map/down_first/pallas_call | solution.py:111
  72.8 3.0 %collective-permute-start.3 = (f32[16,4096]{1,0:T(8,128)}, f32[16,4096]{1,0:T(8,128)S(1)}, u32[]{:S(2)}, u32[]{:S(2)}) collective-permute-start(f32[16,4096]{1,0:T(8,128)} %get-tuple-element.22.refs_4_.refs_8_.refs_3_), channel_id=1, source_target_pairs={{1,2},{3,4},{5,6},{7,8},{9,10},{11,12},{13,14},{15,16},{17,18},{19... | collective-permute-start | bytes 786440 | tf_op jit(solution)/shard_map/ppermute | solution.py:587
  75.8 0.1 collective-permute-start.2
  75.9 9.2 %all-to-all-start.1 = ((f32[128,24,128]{2,1,0:T(8,128)}), f32[128,24,128]{2,1,0:T(8,128)}, u32[]{:S(2)}, u32[]{:S(2)}) async-start(f32[128,24,128]{2,1,0:T(8,128)} %get-tuple-element.20), calls=%async_computation.1 | async-start | bytes 3145728 | tf_op jit(solution)/shard_map/all_to_all | solution.py:591
  85.1 0.0 collective-permute-done.3.refs_6_
  85.1 0.0 copy-start.4
  85.1 0.0 collective-permute-done.2.refs_5_
  85.1 0.0 copy-start.5
  85.1 0.7 copy-done.4
  85.8 0.1 copy-done.5
  85.9 13.8 %near_all.1.refs_9_ = f32[16,4096]{1,0:T(8,128)} custom-call(s32[112]{0:T(128)} %concatenate.3.refs_0_, bf16[8,512,256]{2,1,0:T(8,128)(2,1)} %get-tuple-element.23.refs_1_, bf16[16,512,256]{2,1,0:T(8,128)(2,1)} %get-tuple-element.24.refs_2_, bf16[8,256,512]{2,1,0:T(8,128)(2,1)} %get-tuple-element.16.refs_1_.refs_3_, ...), custom_call_target="tpu_custom_call" | custom-call | flops 40000000000 | bytes 6291456 | tf_op jit(solution)/shard_map/near_all/pallas_call | solution.py:111
  99.6 10.0 %all-to-all-done.1.refs_1_ = f32[128,24,128]{2,1,0:T(8,128)} async-done(((f32[128,24,128]{2,1,0:T(8,128)}), f32[128,24,128]{2,1,0:T(8,128)}, u32[]{:S(2)}, u32[]{:S(2)}) %all-to-all-start.1) | async-done | bytes 1572896 | tf_op jit(solution)/shard_map/all_to_all | solution.py:591
  109.7 8.5 %down_second.1 = (f32[16,4096]{1,0:T(8,128)}, f32[128,128]{1,0:T(8,128)}, f32[8,128]{1,0:T(8,128)}) custom-call(s32[112]{0:T(128)} %concatenate.3.refs_0_, f32[128,24,128]{2,1,0:T(8,128)} %all-to-all-done.1.refs_1_, f32[10,128,128]{2,1,0:T(8,128)} %get-tuple-element.21.refs_2_, f32[96,256,128]{2,1,0:T(8,128)} %refs_3_.5, f32[8,512,128]{2,1,0:T(8,128)} %refs_4_.5, ...), custom_call_target="tpu_custom_call" | custom-call | flops 1000000000 | bytes 6291456 | tf_op jit(solution)/shard_map/down_second/pallas_call | solution.py:111
  118.2 26.7 %all_to_all.21 = f32[128,1,128]{2,1,0:T(1,128)} all-to-all(f32[128,1,128]{2,1,0:T(1,128)} %bitcast.7), channel_id=1, replica_groups=mesh['leaf'=16,'sub'=8] {'leaf','sub'}, dimensions={0} | all-to-all | bytes 131072 | tf_op jit(solution)/shard_map/all_to_all | solution.py:591
  144.9 2.7 %finish.1 = (f32[16,4096]{1,0:T(8,128)}, f32[16,4096]{1,0:T(8,128)}) custom-call(f32[128,128]{1,0:T(8,128)} %bitcast.6, f32[8,128]{1,0:T(8,128)} %get-tuple-element.26.refs_1_, f32[16,4096]{1,0:T(8,128)} %refs_2_.7, f32[16,4096]{1,0:T(8,128)} %get-tuple-element.22.refs_4_.refs_8_.refs_3_, f32[16,4096]{1,0:T(8,128)} %get-tuple-element.27.refs_4_), custom_call_target="tpu_custom_call" | custom-call | flops 1000000 | bytes 6291456 | tf_op jit(solution)/shard_map/finish/pallas_call | solution.py:111
  (1 shorter events, 0.0 us)
Async XLA Ops:
  5.8 26.4 %collective-permute-start.1 = (f32[48,4096]{1,0:T(8,128)}, f32[48,4096]{1,0:T(8,128)S(1)}, u32[]{:S(2)}, u32[]{:S(2)}) collective-permute-start(f32[48,4096]{1,0:T(8,128)} %get-tuple-element.18), channel_id=1, source_target_pairs={{1,2},{3,4},{5,6},{7,8},{9,10},{11,12},{13,14},{15,16},{17,18},{19... | collective-permute-start | bytes 2359304 | tf_op jit(solution)/shard_map/ppermute | solution.py:587
  10.7 21.4 %collective-permute-start = (f32[48,4096]{1,0:T(8,128)}, f32[48,4096]{1,0:T(8,128)}, u32[]{:S(2)}, u32[]{:S(2)}) collective-permute-start(f32[48,4096]{1,0:T(8,128)} %get-tuple-element.18), channel_id=1, source_target_pairs={{0,1},{1,0},{2,3},{3,2},{4,5},{5,4},{6,7},{7,6},{8,9},{9,8},{10,11... | collective-permute-start | bytes 2359304 | tf_op jit(solution)/shard_map/ppermute | solution.py:587
  10.8 10.5 %copy-start.1 = (s32[8,12]{1,0:T(8,128)S(1)}, s32[8,12]{1,0:T(8,128)}, u32[]{:S(2)}) copy-start(s32[8,12]{1,0:T(8,128)} %param.27) | copy-start | bytes 1156
  10.8 10.6 %copy-start = (s32[96,4]{0,1:T(4,128)S(1)}, s32[96,4]{0,1:T(4,128)}, u32[]{:S(2)}) copy-start(s32[96,4]{0,1:T(4,128)} %param.29) | copy-start | bytes 4612
  10.8 10.8 %copy-start.2 = (s32[1,2]{1,0:T(1,128)S(1)}, s32[1,2]{1,0:T(1,128)}, u32[]{:S(2)}) copy-start(s32[1,2]{1,0:T(1,128)} %param.28) | copy-start | bytes 28
  10.8 52.0 %all-to-all-start = ((f32[128,48,128]{2,1,0:T(8,128)}), f32[128,48,128]{2,1,0:T(8,128)}, u32[]{:S(2)}, u32[]{:S(2)}) async-start(f32[128,48,128]{2,1,0:T(8,128)} %get-tuple-element.15), calls=%async_computation | async-start | bytes 6291456 | tf_op jit(solution)/shard_map/all_to_all | solution.py:591
  32.1 0.9 copy-start.3
  72.8 12.3 %collective-permute-start.3 = (f32[16,4096]{1,0:T(8,128)}, f32[16,4096]{1,0:T(8,128)S(1)}, u32[]{:S(2)}, u32[]{:S(2)}) collective-permute-start(f32[16,4096]{1,0:T(8,128)} %get-tuple-element.22.refs_4_.refs_8_.refs_3_), channel_id=1, source_target_pairs={{1,2},{3,4},{5,6},{7,8},{9,10},{11,12},{13,14},{15,16},{17,18},{19... | collective-permute-start | bytes 786440 | tf_op jit(solution)/shard_map/ppermute | solution.py:587
  75.8 9.3 %collective-permute-start.2 = (f32[16,4096]{1,0:T(8,128)}, f32[16,4096]{1,0:T(8,128)S(1)}, u32[]{:S(2)}, u32[]{:S(2)}) collective-permute-start(f32[16,4096]{1,0:T(8,128)} %get-tuple-element.22.refs_4_.refs_8_.refs_3_), channel_id=1, source_target_pairs={{0,1},{1,0},{2,3},{3,2},{4,5},{5,4},{6,7},{7,6},{8,9},{9,8},{10,11... | collective-permute-start | bytes 786440 | tf_op jit(solution)/shard_map/ppermute | solution.py:587
  75.9 33.8 %all-to-all-start.1 = ((f32[128,24,128]{2,1,0:T(8,128)}), f32[128,24,128]{2,1,0:T(8,128)}, u32[]{:S(2)}, u32[]{:S(2)}) async-start(f32[128,24,128]{2,1,0:T(8,128)} %get-tuple-element.20), calls=%async_computation.1 | async-start | bytes 3145728 | tf_op jit(solution)/shard_map/all_to_all | solution.py:591
  85.1 0.7 copy-start.4
  85.1 0.8 copy-start.5
